TPU v7x, 256 devices: a whole 4x4x8 slice. The times are simulated.
256 devices in a mesh: ha: 16 (over y, z_lo), wa: 8 (over x, z_hi), ta: 2 (over core).
Axes of the slice: x: 4, y: 4, z: 8 (z_hi: 2, z_lo: 4; z = z_hi * 4 + z_lo), core: 2. Of those that a mesh axis runs over, the one named last changes fastest.
Arguments:
- queries: bfloat16 [32, 16, 64, 1536], P('ha', None, 'wa', 'ta'), may hold values from -16 to 16
- key_video: bfloat16 [32, 16, 64, 1536], P('ha', None, 'wa', 'ta'), may hold values from -16 to 16
- value_video: bfloat16 [32, 16, 64, 1536], P('ha', None, 'wa', 'ta'), may hold values from -6 to 6
- grad_output: bfloat16 [32, 16, 64, 1536], P('ha', None, 'wa', 'ta'), may hold values from -6 to 6
- text_keys: bfloat16 [256, 1536], P(None, 'ta'), may hold values from -6 to 6
- text_values: bfloat16 [256, 1536], P(None, 'ta'), may hold values from -6 to 6
- window_reach: int32 [12, 6], P('ta'), may hold values from 0 to 1, as said below
- text_valid: int32 [256], replicated, may hold values from 0 to 1, as said below
Outputs:
- query_grad: bfloat16 [32, 16, 64, 1536], P('ha', None, 'wa', 'ta')
- key_grad: bfloat16 [32, 16, 64, 1536], P('ha', None, 'wa', 'ta')
- value_grad: bfloat16 [32, 16, 64, 1536], P('ha', None, 'wa', 'ta')
- text_key_grad: bfloat16 [256, 1536], P(None, 'ta')
- text_value_grad: bfloat16 [256, 1536], P(None, 'ta')
Inputs may be any that keep to these rules, and one draw needn't show every extreme that they name: `window_reach`: heads 0 and 11 reach one tile in all six directions. `text_valid`: the first 64 entries are 1 and the last 64 entries are 0.
All inputs are finite; a program needn't handle non-finite values.
Results may differ from a plain program's by a relative error of at most 0.023.
Values may be sent and summed in bfloat16 or wider, within the bound.
No kernel may reach another device: no remote copies, remote signals or barrier semaphores. Data moves between devices by JAX's collectives and lax.ppermute only.
A program may use at most 192 MiB of HBM per device.

v0:
```python
import jax
import jax.numpy as jnp
from jax import lax
from jax.sharding import PartitionSpec as P

HD = 128
TILE = 8
TILE_T = 2


def from_behind(block, axis, distance):
    devices = range(lax.axis_size(axis))
    route = [(i - distance, i) for i in devices if i - distance in devices]
    return lax.ppermute(block, axis, route)


def with_halo(block, sides, width):
    for axis, dim in sides:
        count = lax.axis_size(axis)
        forward = [(i, i + 1) for i in range(count - 1)]
        backward = [(target, source) for source, target in forward]
        low = lax.ppermute(
            lax.slice_in_dim(block, block.shape[dim] - width, None, axis=dim), axis, forward
        )
        high = lax.ppermute(lax.slice_in_dim(block, 0, width, axis=dim), axis, backward)
        block = jnp.concatenate([low, block, high], axis=dim)
    return block


def to_tiles(grid):
    frame_count, height, width, feature_count = grid.shape
    split_grid = grid.reshape(
        frame_count // TILE_T, TILE_T, height // TILE, TILE, width // TILE, TILE, feature_count
    )
    moved = split_grid.transpose(0, 2, 4, 1, 3, 5, 6)
    return moved.reshape(
        frame_count // TILE_T, height // TILE, width // TILE, TILE_T * TILE * TILE, feature_count
    )


def from_tiles(tiled):
    time_tiles, row_tiles, col_tiles, tile_size, feature_count = tiled.shape
    split_tiles = tiled.reshape(time_tiles, row_tiles, col_tiles, TILE_T, TILE, TILE, feature_count)
    moved = split_tiles.transpose(0, 3, 1, 4, 2, 5, 6)
    return moved.reshape(time_tiles * TILE_T, row_tiles * TILE, col_tiles * TILE, feature_count)


def windows(padded, window_counts):
    time_tiles, row_tiles, col_tiles = window_counts
    pieces = [
        padded[
            time_step : time_step + time_tiles,
            row_step : row_step + row_tiles,
            col_step : col_step + col_tiles,
        ]
        for time_step in range(3)
        for row_step in range(3)
        for col_step in range(3)
    ]
    stacked = jnp.stack(pieces, axis=3)
    return stacked.reshape(
        (time_tiles * row_tiles * col_tiles, 27 * padded.shape[3]) + padded.shape[4:]
    )


def window_extent(window_part, window_counts):
    time_tiles, row_tiles, col_tiles = window_counts
    shaped = window_part.reshape(time_tiles, row_tiles, col_tiles, 27, -1, window_part.shape[-1])
    totals = jnp.zeros(
        (time_tiles + 2, row_tiles + 2, col_tiles + 2) + shaped.shape[4:], jnp.float32
    )
    for time_step in range(3):
        for row_step in range(3):
            for col_step in range(3):
                position = time_step * 9 + row_step * 3 + col_step
                totals = totals.at[
                    time_step : time_step + time_tiles,
                    row_step : row_step + row_tiles,
                    col_step : col_step + col_tiles,
                ].add(shaped[:, :, :, position])
    return totals


def window_mask(spans, firsts, window_counts, grid_counts, direction, tile_size):
    offsets = jnp.arange(3, dtype=jnp.int32) - 1
    valids = []
    for axis_index in range(3):
        near = (
            firsts[axis_index]
            + jnp.arange(window_counts[axis_index], dtype=jnp.int32)[:, None]
            + offsets[None, :]
        )
        reach = (direction * offsets >= -spans[2 * axis_index]) & (
            direction * offsets <= spans[2 * axis_index + 1]
        )
        valids.append((near >= 0) & (near < grid_counts[axis_index]) & reach[None, :])
    joined = (
        valids[0][:, None, None, :, None, None]
        & valids[1][None, :, None, None, :, None]
        & valids[2][None, None, :, None, None, :]
    )
    joined = jnp.broadcast_to(joined[..., None], tuple(window_counts) + (3, 3, 3, tile_size))
    return joined.reshape(window_counts[0] * window_counts[1] * window_counts[2], 27 * tile_size)


def output_delta_product(form, left, right):
    return jnp.einsum(form, left, right, preferred_element_type=jnp.float32)


def pad_rows(grid):
    return jnp.pad(grid, ((0, 0), (TILE, TILE), (0, 0), (0, 0)))


def query_side(
    query_piece,
    key_piece,
    value_piece,
    gradient_piece,
    text_key_piece,
    text_value_piece,
    key_mask,
    text_mask,
    logit_scale_factor,
):
    score_matrix = output_delta_product("vns,vys->vny", query_piece, key_piece) * logit_scale_factor
    text_scores = (
        output_delta_product("bqe,te->bqt", query_piece, text_key_piece) * logit_scale_factor
    )
    score_matrix = jnp.where(key_mask[:, None, :], score_matrix, -jnp.inf)
    text_scores = jnp.where(text_mask[None, None, :], text_scores, -jnp.inf)
    highest = jnp.maximum(jnp.max(score_matrix, axis=2), jnp.max(text_scores, axis=2))
    totals = jnp.sum(jnp.exp(score_matrix - highest[..., None]), axis=2) + jnp.sum(
        jnp.exp(text_scores - highest[..., None]), axis=2
    )
    log_totals = highest + jnp.log(totals)
    probs = jnp.exp(score_matrix - log_totals[..., None])
    text_probs = jnp.exp(text_scores - log_totals[..., None])
    probabilities_reduced = probs.astype(jnp.bfloat16)
    text_probabilities_reduced = text_probs.astype(jnp.bfloat16)
    attended_output = output_delta_product(
        "djt,dth->djh", probabilities_reduced, value_piece
    ) + output_delta_product("ikd,dx->ikx", text_probabilities_reduced, text_value_piece)
    deltas = jnp.sum(gradient_piece.astype(jnp.float32) * attended_output, axis=2)
    probability_gradients = output_delta_product("vns,vys->vny", gradient_piece, value_piece)
    text_prob_grads = output_delta_product("bqe,te->bqt", gradient_piece, text_value_piece)
    score_gradients = (
        probs * (probability_gradients - deltas[..., None]) * logit_scale_factor
    ).astype(jnp.bfloat16)
    text_score_gradients = (
        text_probs * (text_prob_grads - deltas[..., None]) * logit_scale_factor
    ).astype(jnp.bfloat16)
    query_gradients = output_delta_product(
        "djt,dth->djh", score_gradients, key_piece
    ) + output_delta_product("ikd,dx->ikx", text_score_gradients, text_key_piece)
    text_key_grads = output_delta_product("bqt,bqe->te", text_score_gradients, query_piece)
    text_value_grads = output_delta_product(
        "bqt,bqe->te", text_probabilities_reduced, gradient_piece
    )
    return (
        query_gradients,
        log_totals,
        deltas,
        score_gradients,
        probabilities_reduced,
        text_key_grads,
        text_value_grads,
    )


def fold_cols(first_grid, second_grid):

    def pass_cols(first_part, second_part, offset):
        return from_behind((first_part, second_part), "wa", offset)

    from_right = pass_cols(first_grid[:, :, :TILE], second_grid[:, :, :TILE], -1)
    from_left = pass_cols(first_grid[:, :, -TILE:], second_grid[:, :, -TILE:], 1)
    results = []
    for position, whole_grid in enumerate((first_grid, second_grid)):
        inner_part = whole_grid[:, :, TILE:-TILE]
        inner_part = inner_part.at[:, :, -TILE:].add(from_right[position])
        inner_part = inner_part.at[:, :, :TILE].add(from_left[position])
        results.append(inner_part)
    return (results[0], results[1])


def fold_frames(first_grid, second_grid):

    def pass_frames(first_part, second_part, offset):
        return (
            from_behind(first_part.astype(jnp.bfloat16), "ha", offset).astype(first_part.dtype),
            from_behind(second_part.astype(jnp.bfloat16), "ha", offset).astype(second_part.dtype),
        )

    from_later = pass_frames(first_grid[:TILE_T], second_grid[:TILE_T], -1)
    from_earlier = pass_frames(first_grid[-TILE_T:], second_grid[-TILE_T:], 1)
    results = []
    for position, whole_grid in enumerate((first_grid, second_grid)):
        inner_part = whole_grid[TILE_T:-TILE_T]
        inner_part = inner_part.at[-TILE_T:].add(from_later[position])
        inner_part = inner_part.at[:TILE_T].add(from_earlier[position])
        results.append(inner_part)
    return (results[0], results[1])


def body(
    queries, key_video, value_video, grad_output, text_keys, text_values, window_reach, text_valid
):
    frame_count, height, width, feature_count = queries.shape
    head_count = feature_count // HD
    window_counts = (frame_count // TILE_T, height // TILE, width // TILE)
    tile_size = TILE_T * TILE * TILE
    batch_size = window_counts[0] * window_counts[1] * window_counts[2]
    logit_scale_factor = HD ** (-0.5)
    firsts = (lax.axis_index("ha") * window_counts[0], 0, lax.axis_index("wa") * window_counts[2])
    grid_counts = (
        lax.axis_size("ha") * window_counts[0],
        window_counts[1],
        lax.axis_size("wa") * window_counts[2],
    )
    text_mask = text_valid > 0
    col_keys, col_values = (
        with_halo(key_video, (("wa", 2),), TILE),
        with_halo(value_video, (("wa", 2),), TILE),
    )
    halo_keys, halo_values = (
        with_halo(col_keys, (("ha", 0),), TILE_T),
        with_halo(col_values, (("ha", 0),), TILE_T),
    )
    key_windows = windows(to_tiles(pad_rows(halo_keys)), window_counts)
    value_windows = windows(to_tiles(pad_rows(halo_values)), window_counts)
    query_tile_rows = to_tiles(queries).reshape(batch_size, tile_size, feature_count)
    gradient_tiles = to_tiles(grad_output).reshape(batch_size, tile_size, feature_count)
    tile_shape = window_counts + (tile_size,)
    query_parts, log_parts, delta_parts, text_key_parts, text_value_parts = ([], [], [], [], [])
    key_spread, value_spread = ([], [])
    for head_index in range(head_count):
        first_column, last_column = (head_index * HD, (head_index + 1) * HD)
        key_mask = window_mask(
            window_reach[head_index], firsts, window_counts, grid_counts, 1, tile_size
        )
        (
            query_gradients,
            log_totals,
            deltas,
            score_gradients,
            probabilities_reduced,
            text_key_grads,
            text_value_grads,
        ) = query_side(
            query_tile_rows[:, :, first_column:last_column],
            key_windows[:, :, first_column:last_column],
            value_windows[:, :, first_column:last_column],
            gradient_tiles[:, :, first_column:last_column],
            text_keys[:, first_column:last_column],
            text_values[:, first_column:last_column],
            key_mask,
            text_mask,
            logit_scale_factor,
        )
        query_parts.append(query_gradients.astype(jnp.bfloat16).reshape(tile_shape + (HD,)))
        log_parts.append(log_totals.reshape(tile_shape + (1,)))
        delta_parts.append(deltas.reshape(tile_shape + (1,)))
        text_key_parts.append(text_key_grads)
        text_value_parts.append(text_value_grads)
        key_spread.append(
            window_extent(
                output_delta_product(
                    "csy,csx->cyx", score_gradients, query_tile_rows[:, :, first_column:last_column]
                ),
                window_counts,
            )
        )
        value_spread.append(
            window_extent(
                output_delta_product(
                    "csy,csx->cyx",
                    probabilities_reduced,
                    gradient_tiles[:, :, first_column:last_column],
                ),
                window_counts,
            )
        )
    query_grad = from_tiles(jnp.concatenate(query_parts, axis=4))
    text_key_sum, text_value_sum = lax.psum(
        (jnp.concatenate(text_key_parts, axis=1), jnp.concatenate(text_value_parts, axis=1)),
        ("ha", "wa"),
    )
    key_total = from_tiles(jnp.concatenate(key_spread, axis=4))[:, TILE:-TILE]
    value_total = from_tiles(jnp.concatenate(value_spread, axis=4))[:, TILE:-TILE]
    key_total, value_total = fold_cols(key_total, value_total)
    key_total, value_total = fold_frames(key_total, value_total)
    return (
        query_grad,
        key_total.astype(jnp.bfloat16),
        value_total.astype(jnp.bfloat16),
        text_key_sum.astype(jnp.bfloat16),
        text_value_sum.astype(jnp.bfloat16),
    )


def solution(mesh):
    return jax.shard_map(
        body,
        mesh=mesh,
        in_specs=(
            P("ha", None, "wa", "ta"),
            P("ha", None, "wa", "ta"),
            P("ha", None, "wa", "ta"),
            P("ha", None, "wa", "ta"),
            P(None, "ta"),
            P(None, "ta"),
            P("ta", None),
            P(),
        ),
        out_specs=(
            P("ha", None, "wa", "ta"),
            P("ha", None, "wa", "ta"),
            P("ha", None, "wa", "ta"),
            P(None, "ta"),
            P(None, "ta"),
        ),
        check_vma=False,
    )
```

profile of v0, /device:TPU:10, one launch (start us, length us, event | category | flops | bytes accessed | tf_op | source)
XLA Modules:
  0.0 1459.4 jit_solution(9444105325278863351)
XLA Ops:
  0.6 9.2 collective-permute-start
  11.8 7.8 collective-permute-start.4
  61.1 6.0 collective-permute-start.3
  80.7 6.6 collective-permute-start.7
  89.5 41.2 %collective-permute-done.3 = bf16[2,16,24,768]{3,2,1,0:T(8,128)(2,1)S(1)} collective-permute-done((bf16[2,16,24,768]{3,2,1,0:T(8,128)(2,1)S(1)}, bf16[2,16,24,768]{3,2,1,0:T(8,128)(2,1)S(1)}, u32[]{:S(2)}, u32[]{:S(2)}) %collective-permute-start.3) | collective-permute-done | bytes 1179680 | tf_op jit(solution)/shard_map/ppermute | solution.py:25
  131.8 2.9 select_maximum_fusion.2
  136.6 18.4 %collective-permute-done.7 = bf16[2,16,24,768]{3,2,1,0:T(8,128)(2,1)} collective-permute-done((bf16[2,16,24,768]{3,2,1,0:T(8,128)(2,1)}, bf16[2,16,24,768]{3,2,1,0:T(8,128)(2,1)}, u32[]{:S(2)}, u32[]{:S(2)}) %collective-permute-start.7) | collective-permute-done | bytes 1179680 | tf_op jit(solution)/shard_map/ppermute | solution.py:25
  155.0 25.5 %collective-permute-done.6 = bf16[2,16,24,768]{3,2,1,0:T(8,128)(2,1)} collective-permute-done((bf16[2,16,24,768]{3,2,1,0:T(8,128)(2,1)}, bf16[2,16,24,768]{3,2,1,0:T(8,128)(2,1)}, u32[]{:S(2)}, u32[]{:S(2)}) %collective-permute-start.6) | collective-permute-done | bytes 1179680 | tf_op jit(solution)/shard_map/ppermute | solution.py:22
  180.5 2.9 select_maximum_fusion
  186.1 4.9 fusion.955
  195.3 4.3 fusion.957
  205.1 4.5 fusion.959
  215.1 4.3 fusion.961
  224.9 5.1 fusion.963
  234.0 4.7 fusion.965
  300.4 5.1 copy-done.1
  305.6 11.5 copy.273
  317.1 5.0 fusion.949
  322.1 5.5 collective-permute-start.9
  327.6 5.4 collective-permute-start.8
  359.4 5.0 copy-done
  364.4 11.6 copy.435
  376.0 5.0 fusion.948
  381.1 4.7 collective-permute-start.13
  385.8 6.1 collective-permute-start.12
  401.3 1019.9 %all-reduce.16 = (bf16[256,768]{0,1:T(8,128)(2,1)S(1)}, bf16[256,768]{0,1:T(8,128)(2,1)S(1)}) all-reduce(f32[256,768]{0,1:T(8,128)S(1)} %fusion.112, f32[256,768]{0,1:T(8,128)S(1)} %fusion.106), channel_id=1, replica_groups=mesh['ha'=16,'wa'=8,'ta'=2] {'ha','wa'}, use_global_device_ids=true, to_apply=%region_30.31 | all-reduce | flops 393216 | bytes 2359296 | tf_op jit(solution)/shard_map/psum | solution.py:284
  1421.3 3.6 fusion.946
  1425.9 4.8 collective-permute-start.11
  1430.7 3.8 collective-permute-start.10
  1434.6 5.0 fusion.944
  1442.7 6.4 collective-permute-start.14
  1453.8 3.1 collective-permute-done.14
  (692 shorter events, 182.6 us)
Async XLA Ops:
  0.6 60.4 %copy-start.45 = (bf16[2,16,8,768]{3,2,1,0:T(8,128)(2,1)S(1)}, bf16[2,16,8,768]{3,2,1,0:T(8,128)(2,1)}, u32[]{:S(2)}) copy-start(bf16[2,16,8,768]{3,2,1,0:T(8,128)(2,1)} %param.689) | copy-start | bytes 1179652
  0.6 60.3 %collective-permute-start = (bf16[2,16,8,768]{3,2,1,0:T(8,128)(2,1)}, bf16[2,16,8,768]{3,2,1,0:T(8,128)(2,1)S(1)}, u32[]{:S(2)}, u32[]{:S(2)}) collective-permute-start(bf16[2,16,8,768]{3,2,1,0:T(8,128)(2,1)} %param.689), channel_id=1, source_target_pairs={{0,2},{2,4},{4,6},{6,8},{8,10},{10,12},{12,14},{1,3},{3,5},{5,7},{... | collective-permute-start | bytes 1179656 | tf_op jit(solution)/shard_map/ppermute | solution.py:22
  9.9 51.2 %collective-permute-start.1 = (bf16[2,16,8,768]{3,2,1,0:T(8,128)(2,1)}, bf16[2,16,8,768]{3,2,1,0:T(8,128)(2,1)S(1)}, u32[]{:S(2)}, u32[]{:S(2)}) collective-permute-start(bf16[2,16,8,768]{3,2,1,0:T(8,128)(2,1)} %param.689), channel_id=1, source_target_pairs={{2,0},{4,2},{6,4},{8,6},{10,8},{12,10},{14,12},{3,1},{5,3},{7,5},{... | collective-permute-start | bytes 1179656 | tf_op jit(solution)/shard_map/ppermute | solution.py:25
  11.8 63.5 %collective-permute-start.4 = (bf16[2,16,8,768]{3,2,1,0:T(8,128)(2,1)}, bf16[2,16,8,768]{3,2,1,0:T(8,128)(2,1)}, u32[]{:S(2)}, u32[]{:S(2)}) collective-permute-start(bf16[2,16,8,768]{3,2,1,0:T(8,128)(2,1)} %param.690), channel_id=1, source_target_pairs={{0,2},{2,4},{4,6},{6,8},{8,10},{10,12},{12,14},{1,3},{3,5},{5,7},{... | collective-permute-start | bytes 1179656 | tf_op jit(solution)/shard_map/ppermute | solution.py:22
  19.6 59.3 %collective-permute-start.5 = (bf16[2,16,8,768]{3,2,1,0:T(8,128)(2,1)}, bf16[2,16,8,768]{3,2,1,0:T(8,128)(2,1)}, u32[]{:S(2)}, u32[]{:S(2)}) collective-permute-start(bf16[2,16,8,768]{3,2,1,0:T(8,128)(2,1)} %param.690), channel_id=1, source_target_pairs={{2,0},{4,2},{6,4},{8,6},{10,8},{12,10},{14,12},{3,1},{5,3},{7,5},{... | collective-permute-start | bytes 1179656 | tf_op jit(solution)/shard_map/ppermute | solution.py:25
  27.7 45.0 %copy-start.22 = (bf16[1,2,2,8,1,8,768]{6,5,3,1,2,4,0:T(8,128)(2,1)}, bf16[1,2,2,8,1,8,768]{6,5,3,1,2,4,0:T(8,128)(2,1)S(1)}, u32[]{:S(2)}) copy-start(bf16[1,2,2,8,1,8,768]{6,5,3,1,2,4,0:T(8,128)(2,1)S(1)} %copy.40) | copy-start | bytes 1179652
  61.1 69.6 %copy-start.25 = (bf16[2,16,24,768]{3,2,1,0:T(8,128)(2,1)}, bf16[2,16,24,768]{3,2,1,0:T(8,128)(2,1)S(1)}, u32[]{:S(2)}) copy-start(bf16[2,16,24,768]{3,2,1,0:T(8,128)(2,1)S(1)} %constant_dynamic-update-slice_fusion) | copy-start | bytes 3538948
  61.1 69.6 %collective-permute-start.3 = (bf16[2,16,24,768]{3,2,1,0:T(8,128)(2,1)S(1)}, bf16[2,16,24,768]{3,2,1,0:T(8,128)(2,1)S(1)}, u32[]{:S(2)}, u32[]{:S(2)}) collective-permute-start(bf16[2,16,24,768]{3,2,1,0:T(8,128)(2,1)S(1)} %constant_dynamic-update-slice_fusion), channel_id=1, source_target_pairs={{16,0},{32,16},{48,32},{64,48},{80,64},{96,80},{112,96},{128,112},... | collective-permute-start | bytes 3538952 | tf_op jit(solution)/shard_map/ppermute | solution.py:25
  67.1 64.6 %collective-permute-start.2 = (bf16[2,16,24,768]{3,2,1,0:T(8,128)(2,1)S(1)}, bf16[2,16,24,768]{3,2,1,0:T(8,128)(2,1)}, u32[]{:S(2)}, u32[]{:S(2)}) collective-permute-start(bf16[2,16,24,768]{3,2,1,0:T(8,128)(2,1)S(1)} %constant_dynamic-update-slice_fusion), channel_id=1, source_target_pairs={{0,16},{16,32},{32,48},{48,64},{64,80},{80,96},{96,112},{112,128},... | collective-permute-start | bytes 3538952 | tf_op jit(solution)/shard_map/ppermute | solution.py:22
  74.0 195.9 %copy-start.9 = (bf16[1,2,2,8,1,8,768]{6,5,3,1,2,4,0:T(8,128)(2,1)}, bf16[1,2,2,8,1,8,768]{6,5,3,1,2,4,0:T(8,128)(2,1)S(1)}, u32[]{:S(2)}) copy-start(bf16[1,2,2,8,1,8,768]{6,5,3,1,2,4,0:T(8,128)(2,1)S(1)} %copy.68) | copy-start | bytes 1179652
  80.7 74.3 %collective-permute-start.7 = (bf16[2,16,24,768]{3,2,1,0:T(8,128)(2,1)}, bf16[2,16,24,768]{3,2,1,0:T(8,128)(2,1)}, u32[]{:S(2)}, u32[]{:S(2)}) collective-permute-start(bf16[2,16,24,768]{3,2,1,0:T(8,128)(2,1)} %constant_dynamic-update-slice_fusion.3), channel_id=1, source_target_pairs={{16,0},{32,16},{48,32},{64,48},{80,64},{96,80},{112,96},{128,112},... | collective-permute-start | bytes 3538952 | tf_op jit(solution)/shard_map/ppermute | solution.py:25
  87.4 93.1 %collective-permute-start.6 = (bf16[2,16,24,768]{3,2,1,0:T(8,128)(2,1)}, bf16[2,16,24,768]{3,2,1,0:T(8,128)(2,1)}, u32[]{:S(2)}, u32[]{:S(2)}) collective-permute-start(bf16[2,16,24,768]{3,2,1,0:T(8,128)(2,1)} %constant_dynamic-update-slice_fusion.3), channel_id=1, source_target_pairs={{0,16},{16,32},{32,48},{48,64},{64,80},{80,96},{96,112},{112,128},... | collective-permute-start | bytes 3538952 | tf_op jit(solution)/shard_map/ppermute | solution.py:22
  136.6 18.4 %copy-start.56 = (bf16[1,2,1,27,128,768]{5,4,3,1,2,0:T(8,128)(2,1)}, bf16[1,2,1,27,128,768]{5,4,3,1,2,0:T(8,128)(2,1)S(1)}, u32[]{:S(2)}) copy-start(bf16[1,2,1,27,128,768]{5,4,3,1,2,0:T(8,128)(2,1)S(1)} %fusion.185) | copy-start | bytes 31850500
  185.3 36.5 %copy-start.7 = (bf16[1,2,1,27,128,768]{5,4,3,1,2,0:T(8,128)(2,1)}, bf16[1,2,1,27,128,768]{5,4,3,1,2,0:T(8,128)(2,1)S(1)}, u32[]{:S(2)}) copy-start(bf16[1,2,1,27,128,768]{5,4,3,1,2,0:T(8,128)(2,1)S(1)} %fusion.158) | copy-start | bytes 31850500
  192.2 67.9 %copy-start.54 = (f32[2,128]{1,0:T(2,128)}, f32[2,128]{1,0:T(2,128)S(1)}, u32[]{:S(2)}) copy-start(f32[2,128]{1,0:T(2,128)S(1)} %log_add_fusion.5) | copy-start | bytes 3076
  233.0 57.9 %copy-start.26 = (bf16[2,128,3456]{1,2,0:T(8,128)(2,1)}, bf16[2,128,3456]{1,2,0:T(8,128)(2,1)S(1)}, u32[]{:S(2)}) copy-start(bf16[2,128,3456]{1,2,0:T(8,128)(2,1)S(1)} %fusion.33) | copy-start | bytes 5308420
  322.1 1099.2 %collective-permute-start.9 = (f32[6,16,8,768]{3,2,1,0:T(8,128)}, f32[6,16,8,768]{3,2,1,0:T(8,128)}, u32[]{:S(2)}, u32[]{:S(2)}) collective-permute-start(f32[6,16,8,768]{3,2,1,0:T(8,128)} %get-tuple-element.4067), channel_id=1, source_target_pairs={{0,2},{2,4},{4,6},{6,8},{8,10},{10,12},{12,14},{1,3},{3,5},{5,7},{... | collective-permute-start | bytes 7077896 | tf_op jit(solution)/shard_map/ppermute | solution.py:14
  327.6 1093.7 %collective-permute-start.8 = (f32[6,16,8,768]{3,2,1,0:T(8,128)}, f32[6,16,8,768]{3,2,1,0:T(8,128)}, u32[]{:S(2)}, u32[]{:S(2)}) collective-permute-start(f32[6,16,8,768]{3,2,1,0:T(8,128)} %get-tuple-element.4066), channel_id=1, source_target_pairs={{2,0},{4,2},{6,4},{8,6},{10,8},{12,10},{14,12},{3,1},{5,3},{7,5},{... | collective-permute-start | bytes 7077896 | tf_op jit(solution)/shard_map/ppermute | solution.py:14
  376.0 16.4 %copy-start.37 = (bf16[2,128,256]{2,1,0:T(8,128)(2,1)S(1)}, bf16[2,128,256]{2,1,0:T(8,128)(2,1)}, u32[]{:S(2)}) copy-start(bf16[2,128,256]{2,1,0:T(8,128)(2,1)} %fusion.102) | copy-start | bytes 393220
  376.0 16.8 %copy-start.39 = (bf16[2,128,256]{2,1,0:T(8,128)(2,1)S(1)}, bf16[2,128,256]{2,1,0:T(8,128)(2,1)}, u32[]{:S(2)}) copy-start(bf16[2,128,256]{2,1,0:T(8,128)(2,1)} %fusion.103) | copy-start | bytes 393220
  376.0 16.8 %copy-start.48 = (f32[2,128,128]{2,1,0:T(8,128)S(1)}, f32[2,128,128]{2,1,0:T(8,128)}, u32[]{:S(2)}) copy-start(f32[2,128,128]{2,1,0:T(8,128)} %fusion.61) | copy-start | bytes 393220
  376.0 17.2 %copy-start.10 = (bf16[1,2,2,8,1,8,768]{6,5,3,1,2,4,0:T(8,128)(2,1)S(1)}, bf16[1,2,2,8,1,8,768]{6,5,3,1,2,4,0:T(8,128)(2,1)}, u32[]{:S(2)}) copy-start(bf16[1,2,2,8,1,8,768]{6,5,3,1,2,4,0:T(8,128)(2,1)} %copy-done.9) | copy-start | bytes 1179652
  376.0 17.2 %copy-start.18 = (f32[2,128,256]{2,1,0:T(8,128)S(1)}, f32[2,128,256]{2,1,0:T(8,128)}, u32[]{:S(2)}) copy-start(f32[2,128,256]{2,1,0:T(8,128)} %get-tuple-element.4124) | copy-start | bytes 786436
  376.0 17.2 %copy-start.42 = (f32[256,768]{0,1:T(8,128)S(1)}, f32[256,768]{0,1:T(8,128)}, u32[]{:S(2)}) copy-start(f32[256,768]{0,1:T(8,128)} %fusion.111) | copy-start | bytes 2359300
  381.1 1053.5 %collective-permute-start.13 = (f32[6,16,8,768]{3,2,1,0:T(8,128)}, f32[6,16,8,768]{3,2,1,0:T(8,128)}, u32[]{:S(2)}, u32[]{:S(2)}) collective-permute-start(f32[6,16,8,768]{3,2,1,0:T(8,128)} %get-tuple-element.4065), channel_id=1, source_target_pairs={{0,2},{2,4},{4,6},{6,8},{8,10},{10,12},{12,14},{1,3},{3,5},{5,7},{... | collective-permute-start | bytes 7077896 | tf_op jit(solution)/shard_map/ppermute | solution.py:14
  385.8 1048.8 %collective-permute-start.12 = (f32[6,16,8,768]{3,2,1,0:T(8,128)}, f32[6,16,8,768]{3,2,1,0:T(8,128)}, u32[]{:S(2)}, u32[]{:S(2)}) collective-permute-start(f32[6,16,8,768]{3,2,1,0:T(8,128)} %get-tuple-element.4064), channel_id=1, source_target_pairs={{2,0},{4,2},{6,4},{8,6},{10,8},{12,10},{14,12},{3,1},{5,3},{7,5},{... | collective-permute-start | bytes 7077896 | tf_op jit(solution)/shard_map/ppermute | solution.py:14
  1425.9 25.9 %collective-permute-start.11 = (bf16[2,16,8,768]{3,2,1,0:T(8,128)(2,1)}, bf16[2,16,8,768]{3,2,1,0:T(8,128)(2,1)}, u32[]{:S(2)}, u32[]{:S(2)}) collective-permute-start(bf16[2,16,8,768]{3,2,1,0:T(8,128)(2,1)} %get-tuple-element.4071), channel_id=1, source_target_pairs={{0,16},{16,32},{32,48},{48,64},{64,80},{80,96},{96,112},{112,128},... | collective-permute-start | bytes 1179656 | tf_op jit(solution)/shard_map/ppermute | solution.py:14
  1430.7 18.4 %copy-start.46 = (bf16[2,128,128]{2,1,0:T(8,128)(2,1)S(1)}, bf16[2,128,128]{2,1,0:T(8,128)(2,1)}, u32[]{:S(2)}) copy-start(bf16[2,128,128]{2,1,0:T(8,128)(2,1)} %fusion.128) | copy-start | bytes 196612
  1430.7 18.4 %copy-start.47 = (bf16[2,128,128]{2,1,0:T(8,128)(2,1)S(1)}, bf16[2,128,128]{2,1,0:T(8,128)(2,1)}, u32[]{:S(2)}) copy-start(bf16[2,128,128]{2,1,0:T(8,128)(2,1)} %fusion.129) | copy-start | bytes 196612
  1430.7 21.1 %collective-permute-start.10 = (bf16[2,16,8,768]{3,2,1,0:T(8,128)(2,1)}, bf16[2,16,8,768]{3,2,1,0:T(8,128)(2,1)}, u32[]{:S(2)}, u32[]{:S(2)}) collective-permute-start(bf16[2,16,8,768]{3,2,1,0:T(8,128)(2,1)} %get-tuple-element.4070), channel_id=1, source_target_pairs={{16,0},{32,16},{48,32},{64,48},{80,64},{96,80},{112,96},{128,112},... | collective-permute-start | bytes 1179656 | tf_op jit(solution)/shard_map/ppermute | solution.py:14
  1440.6 13.2 collective-permute-start.15
  1442.7 14.2 collective-permute-start.14
  (45 other events, 278.9 us)
where the time goes:
time: 1470 us; the launch traced here: 1460 us
  blocking collectives  1020 us (69%)
  matrix products  105 us (7%)
  waiting for transfers between devices  88.3 us (6%)
  local copies, waits for them, and re-layouts  85.3 us (6%)
  starting transfers between devices  77.3 us (5%)
  other arithmetic  67.2 us (5%)
  between operations  16.8 us (1%)
    psum x1, blocking collectives, body(): lax.psum((jnp.concatenate(text_key_parts, axis=1), jnp.concatenate(text_v...  1020 us
    dot_general x72, matrix products, output_delta_product(): return jnp.einsum(form, left, right, preferred_element_type=jnp.float32)  105 us
    ppermute x4, waiting for transfers between devices, with_halo(): lax.ppermute(lax.slice_in_dim(block, 0, width, axis=dim), axis, backward)  59.6 us
    ppermute x8, starting transfers between devices, from_behind(): return lax.ppermute(block, axis, route)  38.8 us
    unnamed x195, local copies, waits for them, and re-layouts  34.2 us
    scatter-add x300, other arithmetic, window_extent(): totals = totals.at[time_step:time_step + time_tiles, row_step:row_step +...  31.4 us
  transfers between devices with their start and end apart: 16, of which 4 were waited for; matrix products, arithmetic and copies ran while one was open for 7% of the time, Pallas kernels for 0%

commit v1 on v0

v1 whole, which is shorter than its diff:
```python
import functools

import jax
import jax.numpy as jnp
import numpy as np
from jax import lax
from jax.experimental import pallas as pl
from jax.experimental.pallas import tpu as pltpu
from jax.sharding import PartitionSpec as P

HD = 128
TILE = 8
TILE_T = 2
AXES = ("ha", "wa")
FRAME_PARTS = 16
COL_PARTS = 8
RUN = 4
HEADS = 3
HALF = HEADS * HD
PAIR = 2 * HD
BLOCK = 256
SCALE = HD**-0.5
EXP_SCALE = SCALE * float(np.log2(np.e))
COLS = ((0, 256), (0, 512), (0, 512), (256, 512))


def move(block, step):
    route = []
    for ha in range(FRAME_PARTS):
        for wa in range(COL_PARTS):
            there_ha, there_wa = step(ha, wa)
            if 0 <= there_ha < FRAME_PARTS and 0 <= there_wa < COL_PARTS:
                route.append((ha * COL_PARTS + wa, there_ha * COL_PARTS + there_wa))
    return lax.ppermute(block, AXES, route)


def across(ha, wa):
    return ha, wa ^ 1


def frames_by(distance):
    def step(ha, wa):
        there = ha + distance
        return there, wa ^ ((ha // RUN ^ there // RUN) & 1)

    return step


def cols_by(distance):
    return lambda ha, wa: (ha, wa + 2 * distance)


def flip(ha_bits, wa_bits):
    return lambda ha, wa: (ha ^ ha_bits, wa ^ wa_bits)


def lanes(start, count=HD):
    return pl.ds(pl.multiple_of(start, HD), count)


def split_kernel(group_ref, first_ref, second_ref, send_ref, keep_ref):
    group = group_ref[0]
    for out_ref, start in ((send_ref, (1 - group) * HALF), (keep_ref, group * HALF)):
        for head in range(HEADS):
            at = head * PAIR
            out_ref[:, at : at + HD] = first_ref[0, 0, :, lanes(start + head * HD)]
            out_ref[:, at + HD : at + PAIR] = second_ref[0, 0, :, lanes(start + head * HD)]


def split_heads(group, first, second):
    shape = (TILE_T, 2, TILE * TILE, 2 * HALF)
    rows = TILE * TILE
    source = pl.BlockSpec((1, 1, rows, 2 * HALF), lambda i, g: (i % 2, i // 2, 0, 0))
    target = pl.BlockSpec((rows, 2 * HALF), lambda i, g: (i, 0))
    out = jax.ShapeDtypeStruct((BLOCK, 2 * HALF), jnp.bfloat16)
    return pl.pallas_call(
        split_kernel,
        out_shape=(out, out),
        grid_spec=pltpu.PrefetchScalarGridSpec(
            num_scalar_prefetch=1, grid=(4,), in_specs=[source, source], out_specs=(target, target)
        ),
        cost_estimate=pl.CostEstimate(flops=0, bytes_accessed=1600000, transcendentals=0),
        name="split_heads",
    )(group, first.reshape(shape), second.reshape(shape))


def join_pair_kernel(group_ref, keep_ref, got_ref, first_ref, second_ref):
    group = group_ref[0]
    for in_ref, start in ((keep_ref, group * HALF), (got_ref, (1 - group) * HALF)):
        for head in range(HEADS):
            at = head * PAIR
            first_ref[0, 0, :, lanes(start + head * HD)] = in_ref[:, at : at + HD]
            second_ref[0, 0, :, lanes(start + head * HD)] = in_ref[:, at + HD : at + PAIR]


def join_one_kernel(group_ref, keep_ref, got_ref, out_ref):
    group = group_ref[0]
    for in_ref, start in ((keep_ref, group * HALF), (got_ref, (1 - group) * HALF)):
        out_ref[0, 0, :, lanes(start, HALF)] = in_ref[...]


def join_heads(group, keep, got, kernel, count):
    rows = TILE * TILE
    source = pl.BlockSpec((rows, keep.shape[1]), lambda i, g: (i, 0))
    target = pl.BlockSpec((1, 1, rows, 2 * HALF), lambda i, g: (i % 2, i // 2, 0, 0))
    out = jax.ShapeDtypeStruct((TILE_T, 2, rows, 2 * HALF), jnp.bfloat16)
    parts = pl.pallas_call(
        kernel,
        out_shape=(out,) * count,
        grid_spec=pltpu.PrefetchScalarGridSpec(
            num_scalar_prefetch=1,
            grid=(4,),
            in_specs=[source, source],
            out_specs=(target,) * count,
        ),
        cost_estimate=pl.CostEstimate(flops=0, bytes_accessed=800000 * count, transcendentals=0),
        name="join_heads",
    )(group, keep, got)
    return [part.reshape(TILE_T, 2 * TILE, TILE, 2 * HALF) for part in parts]


def dot_t(left, right):
    return lax.dot_general(
        left, right, (((1,), (1,)), ((), ())), preferred_element_type=jnp.float32
    )


def dot(left, right):
    return lax.dot_general(
        left, right, (((1,), (0,)), ((), ())), preferred_element_type=jnp.float32
    )


def t_dot(left, right):
    return lax.dot_general(
        left, right, (((0,), (0,)), ((), ())), preferred_element_type=jnp.float32
    )


def fold(values, op):
    return op(values.reshape(values.shape[0] // 8, 8, values.shape[1]), axis=0)


def attend_kernel(flag_ref, bias_ref, text_bias_ref, qg_ref, text_ref, *refs):
    kv_refs, (grad_refs, dq_ref, dtext_ref) = refs[:12], (refs[12:24], refs[24], refs[25])
    p_ref, dp_ref, high_ref, total_ref, delta_ref, dq_sum_ref = refs[26:]
    head = pl.program_id(0)

    def visible(block):
        return flag_ref[head * 12 + block] != 0

    def q(low, high):
        return qg_ref[low:high, :HD]

    def g(low, high):
        return qg_ref[low:high, HD:]

    def rows(block):
        return slice(block * BLOCK, (block + 1) * BLOCK)

    scores = dot_t(text_ref[:, :HD], q(0, 512)) + text_bias_ref[:, :1]
    p_ref[rows(12), :] = scores
    high_ref[...] = fold(scores, jnp.max)
    for block in range(12):
        low, high = COLS[block % 4]

        @pl.when(visible(block))
        def _(block=block, low=low, high=high):
            scores = dot_t(kv_refs[block][:, :HD], q(low, high))
            for half in range(2):
                part = scores[half * 128 : half * 128 + 128]
                part = part + bias_ref[0, 2 * block + half, low:high][None, :]
                at = block * BLOCK + half * 128
                p_ref[at : at + 128, low:high] = part
                high_ref[:, low:high] = jnp.maximum(high_ref[:, low:high], fold(part, jnp.max))

    highest = jnp.max(high_ref[...], axis=0, keepdims=True)
    total_ref[...] = jnp.zeros_like(total_ref)
    delta_ref[...] = jnp.zeros_like(delta_ref)

    def weigh(block, value, low, high):
        p = jnp.exp2((p_ref[rows(block), low:high] - highest[:, low:high]) * EXP_SCALE)
        dp = dot_t(value, g(low, high))
        p_ref[rows(block), low:high] = p
        dp_ref[rows(block), low:high] = dp
        total_ref[:, low:high] += fold(p, jnp.sum)
        delta_ref[:, low:high] += fold(p * dp, jnp.sum)

    weigh(12, text_ref[:, HD:], 0, 512)
    for block in range(12):
        low, high = COLS[block % 4]

        @pl.when(visible(block))
        def _(block=block, low=low, high=high):
            weigh(block, kv_refs[block][:, HD:], low, high)

    inverse = 1.0 / jnp.sum(total_ref[...], axis=0, keepdims=True)
    delta = jnp.sum(delta_ref[...], axis=0, keepdims=True) * inverse
    scaled = inverse * SCALE

    def spread(block, key, out_ref, low, high):
        p = p_ref[rows(block), low:high]
        prob = (p * inverse[:, low:high]).astype(jnp.bfloat16)
        ds = p * scaled[:, low:high] * (dp_ref[rows(block), low:high] - delta[:, low:high])
        ds = ds.astype(jnp.bfloat16)
        out_ref[:, :HD] = dot(ds, q(low, high)).astype(jnp.bfloat16)
        out_ref[:, HD:] = dot(prob, g(low, high)).astype(jnp.bfloat16)
        return t_dot(ds, key)

    dq_sum_ref[...] = spread(12, text_ref[:, :HD], dtext_ref, 0, 512)
    for block in range(12):
        low, high = COLS[block % 4]

        @pl.when(visible(block))
        def _(block=block, low=low, high=high):
            dq_sum_ref[low:high, :] += spread(
                block, kv_refs[block][:, :HD], grad_refs[block], low, high
            )

        @pl.when(jnp.logical_not(visible(block)))
        def _(block=block):
            grad_refs[block][...] = jnp.zeros_like(grad_refs[block])

    dq_ref[...] = dq_sum_ref[...].astype(jnp.bfloat16)


def attend(flags, bias, text_bias, qg, text, blocks):
    pair = pl.BlockSpec((BLOCK, PAIR), lambda h, f: (0, h))
    out = jax.ShapeDtypeStruct((BLOCK, 2 * HALF), jnp.bfloat16)
    results = pl.pallas_call(
        attend_kernel,
        out_shape=(out,) * 12 + (jax.ShapeDtypeStruct((2 * BLOCK, HALF), jnp.bfloat16), out),
        grid_spec=pltpu.PrefetchScalarGridSpec(
            num_scalar_prefetch=1,
            grid=(HEADS,),
            in_specs=[
                pl.BlockSpec((1, 24, 2 * BLOCK), lambda h, f: (h, 0, 0)),
                pl.BlockSpec((BLOCK, HD), lambda h, f: (0, 0)),
                pl.BlockSpec((2 * BLOCK, PAIR), lambda h, f: (0, h)),
                pair,
            ]
            + [pair] * 12,
            out_specs=(pair,) * 12 + (pl.BlockSpec((2 * BLOCK, HD), lambda h, f: (0, h)), pair),
            scratch_shapes=[
                pltpu.VMEM((13 * BLOCK, 2 * BLOCK), jnp.float32),
                pltpu.VMEM((13 * BLOCK, 2 * BLOCK), jnp.float32),
                pltpu.VMEM((8, 2 * BLOCK), jnp.float32),
                pltpu.VMEM((8, 2 * BLOCK), jnp.float32),
                pltpu.VMEM((8, 2 * BLOCK), jnp.float32),
                pltpu.VMEM((2 * BLOCK, HD), jnp.float32),
            ],
        ),
        compiler_params=pltpu.CompilerParams(vmem_limit_bytes=40 * 1024 * 1024),
        cost_estimate=pl.CostEstimate(
            flops=10 * 512 * 2560 * HD * HEADS,
            bytes_accessed=12000000,
            transcendentals=512 * 2560 * HEADS,
        ),
        name="attend",
    )(flags, bias, text_bias, qg, text, *blocks)
    return results[:12], results[12], results[13]


def visibility(reach, ha, wa):
    between = lambda d, low, high: (d >= -low) & (d <= high)
    column = wa // 2 * 2
    s = jnp.arange(3, dtype=jnp.int32) - 1
    frames = between(s[None, :], reach[:, 0:1], reach[:, 1:2])
    frames = frames & (ha + s >= 0)[None, :] & (ha + s < FRAME_PARTS)[None, :]
    two = jnp.arange(2, dtype=jnp.int32)
    r = two[:, None] - two[None, :]
    rows = between(r[None], reach[:, 2, None, None], reach[:, 3, None, None])
    c = jnp.arange(4, dtype=jnp.int32) - 1
    d = c[:, None] - two[None, :]
    cols = between(d[None], reach[:, 4, None, None], reach[:, 5, None, None])
    cols = cols & ((column + c >= 0) & (column + c < COL_PARTS))[None, :, None]
    seen = (
        frames[:, :, None, None, None, None]
        & cols[:, None, :, None, :, None]
        & rows[:, None, None, :, None, :]
    )
    flags = jnp.any(seen, axis=(3, 4, 5)).astype(jnp.int32).reshape(HEADS * 12)
    bias = jnp.where(seen, 0.0, -jnp.inf).astype(jnp.float32).reshape(HEADS, 24, 4, 1)
    bias = jnp.broadcast_to(bias, (HEADS, 24, 4, 128)).reshape(HEADS, 24, 512)
    return flags, bias


def added(*parts):
    total = parts[0].astype(jnp.float32)
    for part in parts[1:]:
        total = total + part.astype(jnp.float32)
    return total.astype(jnp.bfloat16)


def sum_text(part, group, ha, wa):
    y, x = ha // RUN, wa // 2
    upper = y // 2
    other = lax.dynamic_slice_in_dim(part, (1 - upper) * 128, 128, 0)
    part = added(
        lax.dynamic_slice_in_dim(part, upper * 128, 128, 0), move(other, flip(2 * RUN, 0))
    )
    pieces = [
        move(lax.dynamic_slice_in_dim(part, (x ^ d) * 32, 32, 0), flip(0, 2 * d))
        for d in (1, 2, 3)
    ]
    part = added(lax.dynamic_slice_in_dim(part, x * 32, 32, 0), *pieces)
    near = [move(part, flip(d, 0)).astype(jnp.float32) for d in (1, 2, 3)]
    part = ((part.astype(jnp.float32) + near[0]) + (near[1] + near[2])).astype(jnp.bfloat16)
    mine = added(part, move(part, flip(RUN, 1)))
    theirs = added(move(part, flip(RUN, 0)), move(part, flip(0, 1)))
    both = jnp.stack(
        [jnp.where(group == 0, mine, theirs), jnp.where(group == 0, theirs, mine)], axis=0
    )
    quarter = jnp.zeros((4,) + both.shape, both.dtype)
    quarter = lax.dynamic_update_index_in_dim(quarter, both, x, 0)
    for d in (1, 2, 3):
        quarter = lax.dynamic_update_index_in_dim(quarter, move(both, flip(0, 2 * d)), x ^ d, 0)
    distant = move(quarter, flip(2 * RUN, 0))
    whole = jnp.stack(
        [jnp.where(upper == 0, quarter, distant), jnp.where(upper == 0, distant, quarter)], axis=0
    )
    whole = whole.reshape(2, 4, 2, 32, HEADS, 2, HD)
    whole = whole.transpose(5, 0, 1, 3, 2, 4, 6).reshape(2, 256, 2 * HALF)
    return whole[0], whole[1]


def body(
    queries, key_video, value_video, grad_output, text_keys, text_values, window_reach, text_valid
):
    ha, wa = lax.axis_index("ha"), lax.axis_index("wa")
    side = wa % 2
    group = (side + ha // RUN) % 2
    group_at = group.reshape(1).astype(jnp.int32)

    def placed(keep, got):
        return jnp.where(side == 0, keep, got), jnp.where(side == 0, got, keep)

    send_kv, keep_kv = split_heads(group_at, key_video, value_video)
    own = placed(keep_kv, move(send_kv, across))
    send_qg, keep_qg = split_heads(group_at, queries, grad_output)
    earlier = [move(block, frames_by(1)) for block in own]
    later = [move(block, frames_by(-1)) for block in own]
    send_qg, earlier, later = lax.optimization_barrier((send_qg, earlier, later))
    qg = jnp.concatenate(placed(keep_qg, move(send_qg, across)), axis=0)

    blocks = []
    for left, right in (earlier, own, later):
        blocks += [move(right, cols_by(1)), left, right, move(left, cols_by(-1))]

    reach = lax.dynamic_slice_in_dim(window_reach, group * HEADS, HEADS, 0)
    flags, bias = visibility(reach, ha, wa)
    text_bias = jnp.where(text_valid > 0, 0.0, -jnp.inf).astype(jnp.float32)
    text_bias = jnp.broadcast_to(text_bias[:, None], (256, HD))
    text = jnp.stack(
        [
            lax.dynamic_slice_in_dim(t, group * HALF, HALF, 1).reshape(256, HEADS, HD)
            for t in (text_keys, text_values)
        ],
        axis=2,
    ).reshape(256, 2 * HALF)

    grads, dq, dtext = attend(flags, bias, text_bias, qg, text, blocks)

    def columns_in(step):
        beyond_left, left, right, beyond_right = grads[4 * step : 4 * step + 4]
        return (left, move(beyond_right, cols_by(1))), (right, move(beyond_left, cols_by(-1)))

    outer = []
    for step, distance in ((0, -1), (2, 1)):
        outer.append([move(added(*parts), frames_by(distance)) for parts in columns_in(step)])
    totals = [
        added(*parts, first, second) for parts, first, second in zip(columns_in(1), *outer)
    ]

    text_key_grad, text_value_grad = sum_text(dtext, group, ha, wa)

    dq_own = jnp.where(side == 0, dq[:BLOCK], dq[BLOCK:])
    dq_other = jnp.where(side == 0, dq[BLOCK:], dq[:BLOCK])
    (query_grad,) = join_heads(group_at, dq_own, move(dq_other, across), join_one_kernel, 1)
    keep = jnp.where(side == 0, totals[0], totals[1])
    send = jnp.where(side == 0, totals[1], totals[0])
    key_grad, value_grad = join_heads(group_at, keep, move(send, across), join_pair_kernel, 2)
    return query_grad, key_grad, value_grad, text_key_grad, text_value_grad


def solution(mesh):
    video = P("ha", None, "wa", "ta")
    text = P(None, "ta")
    return jax.shard_map(
        body,
        mesh=mesh,
        in_specs=(video, video, video, video, text, text, P("ta", None), P()),
        out_specs=(video, video, video, text, text),
        check_vma=False,
    )
```

time: 1470 us -> 242 us (0.16)
  blocking collectives: 1020 us -> 0 us
  matrix products: 105 us -> 0 us
  local copies, waits for them, and re-layouts: 85.3 us -> 13.5 us
  other arithmetic: 67.2 us -> 10.3 us
  starting transfers between devices: 77.3 us -> 125 us
  Pallas kernels: 0 us -> 34.8 us
  waiting for transfers between devices: 88.3 us -> 55.9 us
  between operations: 16.8 us -> 1.6 us
    psum x1 -> x0, blocking collectives: 1020 us -> none  [body(): lax.psum((jnp.concatenate(text_key_parts, axis=1), jnp.concatenate(text_v...]
    dot_general x72 -> x0, matrix products: 105 us -> none  [output_delta_product(): return jnp.einsum(form, left, right, preferred_element_type=jnp.float32)]
    ppermute x16 -> x38, starting transfers between devices: 77.3 us -> 125 us  [move(): return lax.ppermute(block, AXES, route)]
    pallas_call x0 -> x5, Pallas kernels: none -> 34.8 us  [the longest x1 21.6 us: attend(): pl.pallas_call(attend_kernel, out_shape=(out,) * 12 + (jax.ShapeDtypeStru...]
    ppermute x16 -> x38, waiting for transfers between devices: 88.3 us -> 55.9 us  [move(): return lax.ppermute(block, AXES, route)]
    scatter-add x300 -> x0, other arithmetic: 31.4 us -> none  [window_extent(): totals = totals.at[time_step:time_step + time_tiles, row_step:row_step +...]
    unnamed x195 -> x64, local copies, waits for them, and re-layouts: 34.2 us -> 6.78 us
    reshape x4 -> x2, local copies, waits for them, and re-layouts: 25.1 us -> 0.9 us  [the longest x1 0.72 us: visibility(): bias = jnp.broadcast_to(bias, (HEADS, 24, 4, 128)).reshape(HEADS, 24, 512)]
  transfers between devices with their start and end apart: 16 -> 38, of which waited for: 4 -> 14; matrix products, arithmetic and copies ran while one was open for 7% -> 7% of each run, Pallas kernels for 0% -> 3%
where the time goes in v1:
time: 242 us; the launch traced here: 241 us
  starting transfers between devices  125 us (52%)
  waiting for transfers between devices  55.9 us (23%)
  Pallas kernels  34.8 us (14%)
  local copies, waits for them, and re-layouts  13.5 us (6%)
  other arithmetic  10.3 us (4%)
    ppermute x38, starting transfers between devices, move(): return lax.ppermute(block, AXES, route)  125 us
    ppermute x38, waiting for transfers between devices, move(): return lax.ppermute(block, AXES, route)  55.9 us
    pallas_call x1, Pallas kernels, attend(): pl.pallas_call(attend_kernel, out_shape=(out,) * 12 + (jax.ShapeDtypeStru...  21.6 us
    pallas_call x2, Pallas kernels, split_heads(): pl.pallas_call(split_kernel, out_shape=(out, out), grid_spec=pltpu.Prefet...  6.8 us
    unnamed x64, local copies, waits for them, and re-layouts  6.78 us
    pallas_call x2, Pallas kernels, join_heads(): pl.pallas_call(kernel, out_shape=(out,) * count, grid_spec=pltpu.Prefetch...  6.36 us
  transfers between devices with their start and end apart: 38, of which 14 were waited for; matrix products, arithmetic and copies ran while one was open for 7% of the time, Pallas kernels for 3%

profile of v1, /device:TPU:10, one launch (start us, length us, event | category | flops | bytes accessed | tf_op | source)
XLA Modules:
  0.0 240.7 jit_solution(4784091999506153745)
XLA Ops:
  0.7 3.5 %split_heads.3 = (bf16[256,768]{1,0:T(8,128)(2,1)}, bf16[256,768]{1,0:T(8,128)(2,1)}) custom-call(s32[1]{0:T(128)} %bitcast.group_ref, bf16[2,2,64,768]{3,2,1,0:T(8,128)(2,1)} %bitcast.32, bf16[2,2,64,768]{3,2,1,0:T(8,128)(2,1)} %bitcast.33), custom_call_target="tpu_custom_call" | custom-call | bytes 1600000 | tf_op jit(solution)/shard_map/split_heads/pallas_call | solution.py:76
  4.2 7.2 %collective-permute-start = (bf16[256,768]{1,0:T(8,128)(2,1)}, bf16[256,768]{1,0:T(8,128)(2,1)S(1)}, u32[]{:S(2)}, u32[]{:S(2)}) collective-permute-start(bf16[256,768]{1,0:T(8,128)(2,1)} %get-tuple-element.33), channel_id=1, source_target_pairs={{0,2},{2,0},{4,6},{6,4},{8,10},{10,8},{12,14},{14,12},{16,18},{18,... | collective-permute-start | bytes 1179656 | tf_op jit(solution)/shard_map/ppermute | solution.py:34
  12.1 3.4 %split_heads.2 = (bf16[256,768]{1,0:T(8,128)(2,1)}, bf16[256,768]{1,0:T(8,128)(2,1)}) custom-call(s32[1]{0:T(128)} %bitcast.group_ref, bf16[2,2,64,768]{3,2,1,0:T(8,128)(2,1)} %bitcast.34, bf16[2,2,64,768]{3,2,1,0:T(8,128)(2,1)} %bitcast.35), custom_call_target="tpu_custom_call" | custom-call | bytes 1600000 | tf_op jit(solution)/shard_map/split_heads/pallas_call | solution.py:76
  15.7 6.1 %collective-permute-done = bf16[256,768]{1,0:T(8,128)(2,1)S(1)} collective-permute-done((bf16[256,768]{1,0:T(8,128)(2,1)}, bf16[256,768]{1,0:T(8,128)(2,1)S(1)}, u32[]{:S(2)}, u32[]{:S(2)}) %collective-permute-start) | collective-permute-done | bytes 393248 | tf_op jit(solution)/shard_map/ppermute | solution.py:34
  21.9 10.3 %collective-permute-start.1 = (bf16[256,768]{1,0:T(8,128)(2,1)S(1)}, bf16[256,768]{1,0:T(8,128)(2,1)S(1)}, u32[]{:S(2)}, u32[]{:S(2)}) collective-permute-start(bf16[256,768]{1,0:T(8,128)(2,1)S(1)} %get-tuple-element.71.refs_5_), channel_id=1, source_target_pairs={{0,16},{2,18},{4,20},{6,22},{8,24},{10,26},{12,28},{14,30},{16,32}... | collective-permute-start | bytes 1179656 | tf_op jit(solution)/shard_map/ppermute | solution.py:34
  34.1 3.9 %collective-permute-start.2 = (bf16[256,768]{1,0:T(8,128)(2,1)S(1)}, bf16[256,768]{1,0:T(8,128)(2,1)S(1)}, u32[]{:S(2)}, u32[]{:S(2)}) collective-permute-start(bf16[256,768]{1,0:T(8,128)(2,1)S(1)} %get-tuple-element.70.refs_6_), channel_id=1, source_target_pairs={{0,16},{2,18},{4,20},{6,22},{8,24},{10,26},{12,28},{14,30},{16,32}... | collective-permute-start | bytes 1179656 | tf_op jit(solution)/shard_map/ppermute | solution.py:34
  38.1 4.0 %collective-permute-start.4 = (bf16[256,768]{1,0:T(8,128)(2,1)S(1)}, bf16[256,768]{1,0:T(8,128)(2,1)S(1)}, u32[]{:S(2)}, u32[]{:S(2)}) collective-permute-start(bf16[256,768]{1,0:T(8,128)(2,1)S(1)} %get-tuple-element.70.refs_6_), channel_id=1, source_target_pairs={{16,0},{18,2},{20,4},{22,6},{24,8},{26,10},{28,12},{30,14},{32,16}... | collective-permute-start | bytes 1179656 | tf_op jit(solution)/shard_map/ppermute | solution.py:34
  42.9 3.4 %collective-permute-start.8 = (bf16[256,768]{1,0:T(8,128)(2,1)S(1)}, bf16[256,768]{1,0:T(8,128)(2,1)S(1)}, u32[]{:S(2)}, u32[]{:S(2)}) collective-permute-start(bf16[256,768]{1,0:T(8,128)(2,1)S(1)} %get-tuple-element.70.refs_6_), channel_id=1, source_target_pairs={{0,4},{2,6},{4,8},{6,10},{8,12},{10,14},{16,20},{18,22},{20,24},{2... | collective-permute-start | bytes 1179656 | tf_op jit(solution)/shard_map/ppermute | solution.py:34
  46.3 3.2 %collective-permute-done.2.refs_2_ = bf16[256,768]{1,0:T(8,128)(2,1)S(1)} collective-permute-done((bf16[256,768]{1,0:T(8,128)(2,1)S(1)}, bf16[256,768]{1,0:T(8,128)(2,1)S(1)}, u32[]{:S(2)}, u32[]{:S(2)}) %collective-permute-start.2) | collective-permute-done | bytes 393248 | tf_op jit(solution)/shard_map/ppermute | solution.py:34
  52.5 5.3 %collective-permute-start.5 = (bf16[256,768]{1,0:T(8,128)(2,1)}, bf16[256,768]{1,0:T(8,128)(2,1)}, u32[]{:S(2)}, u32[]{:S(2)}) collective-permute-start(bf16[256,768]{1,0:T(8,128)(2,1)} %get-tuple-element.34), channel_id=1, source_target_pairs={{0,2},{2,0},{4,6},{6,4},{8,10},{10,8},{12,14},{14,12},{16,18},{18,... | collective-permute-start | bytes 1179656 | tf_op jit(solution)/shard_map/ppermute | solution.py:34
  63.4 3.4 %collective-permute-start.10 = (bf16[256,768]{1,0:T(8,128)(2,1)S(1)}, bf16[256,768]{1,0:T(8,128)(2,1)S(1)}, u32[]{:S(2)}, u32[]{:S(2)}) collective-permute-start(bf16[256,768]{1,0:T(8,128)(2,1)S(1)} %collective-permute-done.4.refs_10_), channel_id=1, source_target_pairs={{0,4},{2,6},{4,8},{6,10},{8,12},{10,14},{16,20},{18,22},{20,24},{2... | collective-permute-start | bytes 1179656 | tf_op jit(solution)/shard_map/ppermute | solution.py:34
  69.3 3.4 %collective-permute-start.6 = (bf16[256,768]{1,0:T(8,128)(2,1)S(1)}, bf16[256,768]{1,0:T(8,128)(2,1)S(1)}, u32[]{:S(2)}, u32[]{:S(2)}) collective-permute-start(bf16[256,768]{1,0:T(8,128)(2,1)S(1)} %collective-permute-done.2.refs_2_), channel_id=1, source_target_pairs={{0,4},{2,6},{4,8},{6,10},{8,12},{10,14},{16,20},{18,22},{20,24},{2... | collective-permute-start | bytes 1179656 | tf_op jit(solution)/shard_map/ppermute | solution.py:34
  76.8 6.0 %collective-permute-done.11.refs_11_ = bf16[256,768]{1,0:T(8,128)(2,1)S(1)} collective-permute-done((bf16[256,768]{1,0:T(8,128)(2,1)S(1)}, bf16[256,768]{1,0:T(8,128)(2,1)S(1)}, u32[]{:S(2)}, u32[]{:S(2)}) %collective-permute-start.11) | collective-permute-done | bytes 393248 | tf_op jit(solution)/shard_map/ppermute | solution.py:34
  82.8 5.4 %collective-permute-done.7.refs_3_ = bf16[256,768]{1,0:T(8,128)(2,1)S(1)} collective-permute-done((bf16[256,768]{1,0:T(8,128)(2,1)S(1)}, bf16[256,768]{1,0:T(8,128)(2,1)S(1)}, u32[]{:S(2)}, u32[]{:S(2)}) %collective-permute-start.7) | collective-permute-done | bytes 393248 | tf_op jit(solution)/shard_map/ppermute | solution.py:34
  89.3 21.6 %attend.1 = (bf16[256,768]{1,0:T(8,128)(2,1)S(1)}, bf16[256,768]{1,0:T(8,128)(2,1)S(1)}, bf16[256,768]{1,0:T(8,128)(2,1)S(1)}, bf16[256,768]{1,0:T(8,128)(2,1)S(...) custom-call(s32[36]{0:T(128)S(1)} %reshape.254.flag_ref, ...), custom_call_target="tpu_custom_call" | custom-call | flops 5033164800 | bytes 12000000 | tf_op jit(solution)/shard_map/attend/pallas_call | solution.py:230
  117.9 5.1 %collective-permute-done.24 = bf16[128,768]{1,0:T(8,128)(2,1)S(1)} collective-permute-done((bf16[128,768]{1,0:T(8,128)(2,1)S(1)}, bf16[128,768]{1,0:T(8,128)(2,1)S(1)}, u32[]{:S(2)}, u32[]{:S(2)}) %collective-permute-start.24) | collective-permute-done | bytes 196640 | tf_op jit(solution)/shard_map/ppermute | solution.py:34
  130.2 3.3 %collective-permute-start.28 = (bf16[32,768]{1,0:T(8,128)(2,1)S(1)}, bf16[32,768]{1,0:T(8,128)(2,1)S(1)}, u32[]{:S(2)}, u32[]{:S(2)}) collective-permute-start(bf16[32,768]{1,0:T(8,128)(2,1)S(1)} %add_convert_fusion.10), channel_id=1, source_target_pairs={{0,16},{2,18},{4,20},{6,22},{8,24},{10,26},{12,28},{14,30},{16,0},... | collective-permute-start | bytes 147464 | tf_op jit(solution)/shard_map/ppermute | solution.py:34
  140.8 5.7 %collective-permute-start.31 = (bf16[32,768]{1,0:T(8,128)(2,1)}, bf16[32,768]{1,0:T(8,128)(2,1)}, u32[]{:S(2)}, u32[]{:S(2)}) collective-permute-start(bf16[32,768]{1,0:T(8,128)(2,1)} %add_convert_fusion.9), channel_id=1, source_target_pairs={{0,66},{2,64},{4,70},{6,68},{8,74},{10,72},{12,78},{14,76},{16,82}... | collective-permute-start | bytes 147464 | tf_op jit(solution)/shard_map/ppermute | solution.py:34
  148.6 3.8 %collective-permute-start.14 = (bf16[256,768]{1,0:T(8,128)(2,1)}, bf16[256,768]{1,0:T(8,128)(2,1)}, u32[]{:S(2)}, u32[]{:S(2)}) collective-permute-start(bf16[256,768]{1,0:T(8,128)(2,1)} %copy-done.14), channel_id=1, source_target_pairs={{0,4},{2,6},{4,8},{6,10},{8,12},{10,14},{16,20},{18,22},{20,24},{2... | collective-permute-start | bytes 1179656 | tf_op jit(solution)/shard_map/ppermute | solution.py:34
  152.4 3.5 %collective-permute-start.16 = (bf16[256,768]{1,0:T(8,128)(2,1)}, bf16[256,768]{1,0:T(8,128)(2,1)}, u32[]{:S(2)}, u32[]{:S(2)}) collective-permute-start(bf16[256,768]{1,0:T(8,128)(2,1)} %copy-done.13), channel_id=1, source_target_pairs={{0,4},{2,6},{4,8},{6,10},{8,12},{10,14},{16,20},{18,22},{20,24},{2... | collective-permute-start | bytes 1179656 | tf_op jit(solution)/shard_map/ppermute | solution.py:34
  155.9 3.0 %join_heads.2 = bf16[2,2,64,768]{3,2,1,0:T(8,128)(2,1)} custom-call(s32[1]{0:T(128)} %bitcast.group_ref, bf16[256,384]{1,0:T(8,128)(2,1)} %get-tuple-element.73.keep_ref, bf16[256,384]{1,0:T(8,128)(2,1)} %copy-done.27), custom_call_target="tpu_custom_call" | custom-call | bytes 800000 | tf_op jit(solution)/shard_map/join_heads/pallas_call | solution.py:107
  159.0 3.0 %collective-permute-start.19 = (bf16[256,768]{1,0:T(8,128)(2,1)}, bf16[256,768]{1,0:T(8,128)(2,1)S(1)}, u32[]{:S(2)}, u32[]{:S(2)}) collective-permute-start(bf16[256,768]{1,0:T(8,128)(2,1)} %copy-done.12), channel_id=1, source_target_pairs={{4,0},{6,2},{8,4},{10,6},{12,8},{14,10},{20,16},{22,18},{24,20},{2... | collective-permute-start | bytes 1179656 | tf_op jit(solution)/shard_map/ppermute | solution.py:34
  164.0 3.9 %collective-permute-start.13 = (bf16[256,768]{1,0:T(8,128)(2,1)S(1)}, bf16[256,768]{1,0:T(8,128)(2,1)S(1)}, u32[]{:S(2)}, u32[]{:S(2)}) collective-permute-start(bf16[256,768]{1,0:T(8,128)(2,1)S(1)} %copy-done.9), channel_id=1, source_target_pairs={{0,4},{2,6},{4,8},{6,10},{8,12},{10,14},{16,20},{18,22},{20,24},{2... | collective-permute-start | bytes 1179656 | tf_op jit(solution)/shard_map/ppermute | solution.py:34
  173.2 3.5 %collective-permute-start.35 = (bf16[2,32,768]{2,1,0:T(8,128)(2,1)S(1)}, bf16[2,32,768]{2,1,0:T(8,128)(2,1)S(1)}, u32[]{:S(2)}, u32[]{:S(2)}) collective-permute-start(bf16[2,32,768]{2,1,0:T(8,128)(2,1)S(1)} %pad_maximum_fusion.2), channel_id=1, source_target_pairs={{0,8},{2,10},{4,12},{6,14},{8,0},{10,2},{12,4},{14,6},{16,24},{18,... | collective-permute-start | bytes 294920 | tf_op jit(solution)/shard_map/ppermute | solution.py:34
  176.8 3.3 %collective-permute-done.21 = bf16[256,768]{1,0:T(8,128)(2,1)S(1)} collective-permute-done((bf16[256,768]{1,0:T(8,128)(2,1)S(1)}, bf16[256,768]{1,0:T(8,128)(2,1)S(1)}, u32[]{:S(2)}, u32[]{:S(2)}) %collective-permute-start.21) | collective-permute-done | bytes 393248 | tf_op jit(solution)/shard_map/ppermute | solution.py:34
  180.6 3.6 %collective-permute-done.34 = bf16[2,32,768]{2,1,0:T(8,128)(2,1)S(1)} collective-permute-done((bf16[2,32,768]{2,1,0:T(8,128)(2,1)S(1)}, bf16[2,32,768]{2,1,0:T(8,128)(2,1)S(1)}, u32[]{:S(2)}, u32[]{:S(2)}) %collective-permute-start.34) | collective-permute-done | bytes 98336 | tf_op jit(solution)/shard_map/ppermute | solution.py:34
  184.2 4.6 %collective-permute-start.15 = (bf16[256,768]{1,0:T(8,128)(2,1)S(1)}, bf16[256,768]{1,0:T(8,128)(2,1)S(1)}, u32[]{:S(2)}, u32[]{:S(2)}) collective-permute-start(bf16[256,768]{1,0:T(8,128)(2,1)S(1)} %add_convert_fusion.5), channel_id=1, source_target_pairs={{16,0},{18,2},{20,4},{22,6},{24,8},{26,10},{28,12},{30,14},{32,16}... | collective-permute-start | bytes 1179656 | tf_op jit(solution)/shard_map/ppermute | solution.py:34
  190.8 6.0 %collective-permute-start.20 = (bf16[256,768]{1,0:T(8,128)(2,1)S(1)}, bf16[256,768]{1,0:T(8,128)(2,1)S(1)}, u32[]{:S(2)}, u32[]{:S(2)}) collective-permute-start(bf16[256,768]{1,0:T(8,128)(2,1)S(1)} %add_convert_fusion.2), channel_id=1, source_target_pairs={{16,0},{18,2},{20,4},{22,6},{24,8},{26,10},{28,12},{30,14},{32,16}... | collective-permute-start | bytes 1179656 | tf_op jit(solution)/shard_map/ppermute | solution.py:34
  201.6 5.7 %collective-permute-done.17 = bf16[256,768]{1,0:T(8,128)(2,1)S(1)} collective-permute-done((bf16[256,768]{1,0:T(8,128)(2,1)S(1)}, bf16[256,768]{1,0:T(8,128)(2,1)S(1)}, u32[]{:S(2)}, u32[]{:S(2)}) %collective-permute-start.17) | collective-permute-done | bytes 393248 | tf_op jit(solution)/shard_map/ppermute | solution.py:34
  207.3 10.3 %collective-permute-done.22 = bf16[256,768]{1,0:T(8,128)(2,1)S(1)} collective-permute-done((bf16[256,768]{1,0:T(8,128)(2,1)S(1)}, bf16[256,768]{1,0:T(8,128)(2,1)S(1)}, u32[]{:S(2)}, u32[]{:S(2)}) %collective-permute-start.22) | collective-permute-done | bytes 393248 | tf_op jit(solution)/shard_map/ppermute | solution.py:34
  218.0 12.8 %collective-permute-start.23 = (bf16[256,768]{1,0:T(8,128)(2,1)S(1)}, bf16[256,768]{1,0:T(8,128)(2,1)S(1)}, u32[]{:S(2)}, u32[]{:S(2)}) collective-permute-start(bf16[256,768]{1,0:T(8,128)(2,1)S(1)} %get-tuple-element.61), channel_id=1, source_target_pairs={{0,2},{2,0},{4,6},{6,4},{8,10},{10,8},{12,14},{14,12},{16,18},{18,... | collective-permute-start | bytes 1179656 | tf_op jit(solution)/shard_map/ppermute | solution.py:34
  237.4 3.3 %join_heads.3 = (bf16[2,2,64,768]{3,2,1,0:T(8,128)(2,1)}, bf16[2,2,64,768]{3,2,1,0:T(8,128)(2,1)}) custom-call(s32[1]{0:T(128)} %bitcast.group_ref, bf16[256,768]{1,0:T(8,128)(2,1)} %broadcast_select_fusion.3.keep_ref, bf16[256,768]{1,0:T(8,128)(2,1)} %copy-done.26), custom_call_target="tpu_custom_call" | custom-call | bytes 1600000 | tf_op jit(solution)/shard_map/join_heads/pallas_call | solution.py:107
  (170 shorter events, 64.5 us)
Async XLA Ops:
  4.2 17.6 %collective-permute-start = (bf16[256,768]{1,0:T(8,128)(2,1)}, bf16[256,768]{1,0:T(8,128)(2,1)S(1)}, u32[]{:S(2)}, u32[]{:S(2)}) collective-permute-start(bf16[256,768]{1,0:T(8,128)(2,1)} %get-tuple-element.33), channel_id=1, source_target_pairs={{0,2},{2,0},{4,6},{6,4},{8,10},{10,8},{12,14},{14,12},{16,18},{18,... | collective-permute-start | bytes 1179656 | tf_op jit(solution)/shard_map/ppermute | solution.py:34
  21.9 24.4 %collective-permute-start.1 = (bf16[256,768]{1,0:T(8,128)(2,1)S(1)}, bf16[256,768]{1,0:T(8,128)(2,1)S(1)}, u32[]{:S(2)}, u32[]{:S(2)}) collective-permute-start(bf16[256,768]{1,0:T(8,128)(2,1)S(1)} %get-tuple-element.71.refs_5_), channel_id=1, source_target_pairs={{0,16},{2,18},{4,20},{6,22},{8,24},{10,26},{12,28},{14,30},{16,32}... | collective-permute-start | bytes 1179656 | tf_op jit(solution)/shard_map/ppermute | solution.py:34
  32.2 17.3 %collective-permute-start.3 = (bf16[256,768]{1,0:T(8,128)(2,1)S(1)}, bf16[256,768]{1,0:T(8,128)(2,1)S(1)}, u32[]{:S(2)}, u32[]{:S(2)}) collective-permute-start(bf16[256,768]{1,0:T(8,128)(2,1)S(1)} %get-tuple-element.71.refs_5_), channel_id=1, source_target_pairs={{16,0},{18,2},{20,4},{22,6},{24,8},{26,10},{28,12},{30,14},{32,16}... | collective-permute-start | bytes 1179656 | tf_op jit(solution)/shard_map/ppermute | solution.py:34
  34.1 15.4 %collective-permute-start.2 = (bf16[256,768]{1,0:T(8,128)(2,1)S(1)}, bf16[256,768]{1,0:T(8,128)(2,1)S(1)}, u32[]{:S(2)}, u32[]{:S(2)}) collective-permute-start(bf16[256,768]{1,0:T(8,128)(2,1)S(1)} %get-tuple-element.70.refs_6_), channel_id=1, source_target_pairs={{0,16},{2,18},{4,20},{6,22},{8,24},{10,26},{12,28},{14,30},{16,32}... | collective-permute-start | bytes 1179656 | tf_op jit(solution)/shard_map/ppermute | solution.py:34
  38.1 14.4 %collective-permute-start.4 = (bf16[256,768]{1,0:T(8,128)(2,1)S(1)}, bf16[256,768]{1,0:T(8,128)(2,1)S(1)}, u32[]{:S(2)}, u32[]{:S(2)}) collective-permute-start(bf16[256,768]{1,0:T(8,128)(2,1)S(1)} %get-tuple-element.70.refs_6_), channel_id=1, source_target_pairs={{16,0},{18,2},{20,4},{22,6},{24,8},{26,10},{28,12},{30,14},{32,16}... | collective-permute-start | bytes 1179656 | tf_op jit(solution)/shard_map/ppermute | solution.py:34
  42.9 26.4 %collective-permute-start.8 = (bf16[256,768]{1,0:T(8,128)(2,1)S(1)}, bf16[256,768]{1,0:T(8,128)(2,1)S(1)}, u32[]{:S(2)}, u32[]{:S(2)}) collective-permute-start(bf16[256,768]{1,0:T(8,128)(2,1)S(1)} %get-tuple-element.70.refs_6_), channel_id=1, source_target_pairs={{0,4},{2,6},{4,8},{6,10},{8,12},{10,14},{16,20},{18,22},{20,24},{2... | collective-permute-start | bytes 1179656 | tf_op jit(solution)/shard_map/ppermute | solution.py:34
  52.5 20.2 %collective-permute-start.5 = (bf16[256,768]{1,0:T(8,128)(2,1)}, bf16[256,768]{1,0:T(8,128)(2,1)}, u32[]{:S(2)}, u32[]{:S(2)}) collective-permute-start(bf16[256,768]{1,0:T(8,128)(2,1)} %get-tuple-element.34), channel_id=1, source_target_pairs={{0,2},{2,0},{4,6},{6,4},{8,10},{10,8},{12,14},{14,12},{16,18},{18,... | collective-permute-start | bytes 1179656 | tf_op jit(solution)/shard_map/ppermute | solution.py:34
  60.9 15.8 %collective-permute-start.9 = (bf16[256,768]{1,0:T(8,128)(2,1)S(1)}, bf16[256,768]{1,0:T(8,128)(2,1)S(1)}, u32[]{:S(2)}, u32[]{:S(2)}) collective-permute-start(bf16[256,768]{1,0:T(8,128)(2,1)S(1)} %get-tuple-element.71.refs_5_), channel_id=1, source_target_pairs={{4,0},{6,2},{8,4},{10,6},{12,8},{14,10},{20,16},{22,18},{24,20},{2... | collective-permute-start | bytes 1179656 | tf_op jit(solution)/shard_map/ppermute | solution.py:34
  63.4 13.4 %collective-permute-start.10 = (bf16[256,768]{1,0:T(8,128)(2,1)S(1)}, bf16[256,768]{1,0:T(8,128)(2,1)S(1)}, u32[]{:S(2)}, u32[]{:S(2)}) collective-permute-start(bf16[256,768]{1,0:T(8,128)(2,1)S(1)} %collective-permute-done.4.refs_10_), channel_id=1, source_target_pairs={{0,4},{2,6},{4,8},{6,10},{8,12},{10,14},{16,20},{18,22},{20,24},{2... | collective-permute-start | bytes 1179656 | tf_op jit(solution)/shard_map/ppermute | solution.py:34
  66.8 16.0 %collective-permute-start.11 = (bf16[256,768]{1,0:T(8,128)(2,1)S(1)}, bf16[256,768]{1,0:T(8,128)(2,1)S(1)}, u32[]{:S(2)}, u32[]{:S(2)}) collective-permute-start(bf16[256,768]{1,0:T(8,128)(2,1)S(1)} %collective-permute-done.3.refs_9_), channel_id=1, source_target_pairs={{4,0},{6,2},{8,4},{10,6},{12,8},{14,10},{20,16},{22,18},{24,20},{2... | collective-permute-start | bytes 1179656 | tf_op jit(solution)/shard_map/ppermute | solution.py:34
  69.3 13.5 %collective-permute-start.6 = (bf16[256,768]{1,0:T(8,128)(2,1)S(1)}, bf16[256,768]{1,0:T(8,128)(2,1)S(1)}, u32[]{:S(2)}, u32[]{:S(2)}) collective-permute-start(bf16[256,768]{1,0:T(8,128)(2,1)S(1)} %collective-permute-done.2.refs_2_), channel_id=1, source_target_pairs={{0,4},{2,6},{4,8},{6,10},{8,12},{10,14},{16,20},{18,22},{20,24},{2... | collective-permute-start | bytes 1179656 | tf_op jit(solution)/shard_map/ppermute | solution.py:34
  72.7 15.5 %collective-permute-start.7 = (bf16[256,768]{1,0:T(8,128)(2,1)S(1)}, bf16[256,768]{1,0:T(8,128)(2,1)S(1)}, u32[]{:S(2)}, u32[]{:S(2)}) collective-permute-start(bf16[256,768]{1,0:T(8,128)(2,1)S(1)} %collective-permute-done.1.refs_1_), channel_id=1, source_target_pairs={{4,0},{6,2},{8,4},{10,6},{12,8},{14,10},{20,16},{22,18},{24,20},{2... | collective-permute-start | bytes 1179656 | tf_op jit(solution)/shard_map/ppermute | solution.py:34
  130.2 9.2 %collective-permute-start.28 = (bf16[32,768]{1,0:T(8,128)(2,1)S(1)}, bf16[32,768]{1,0:T(8,128)(2,1)S(1)}, u32[]{:S(2)}, u32[]{:S(2)}) collective-permute-start(bf16[32,768]{1,0:T(8,128)(2,1)S(1)} %add_convert_fusion.10), channel_id=1, source_target_pairs={{0,16},{2,18},{4,20},{6,22},{8,24},{10,26},{12,28},{14,30},{16,0},... | collective-permute-start | bytes 147464 | tf_op jit(solution)/shard_map/ppermute | solution.py:34
  136.8 15.6 %collective-permute-start.12 = (bf16[256,384]{1,0:T(8,128)(2,1)}, bf16[256,384]{1,0:T(8,128)(2,1)S(1)}, u32[]{:S(2)}, u32[]{:S(2)}) collective-permute-start(bf16[256,384]{1,0:T(8,128)(2,1)} %get-tuple-element.72), channel_id=1, source_target_pairs={{0,2},{2,0},{4,6},{6,4},{8,10},{10,8},{12,14},{14,12},{16,18},{18,... | collective-permute-start | bytes 589832 | tf_op jit(solution)/shard_map/ppermute | solution.py:34
  140.8 18.2 %collective-permute-start.31 = (bf16[32,768]{1,0:T(8,128)(2,1)}, bf16[32,768]{1,0:T(8,128)(2,1)}, u32[]{:S(2)}, u32[]{:S(2)}) collective-permute-start(bf16[32,768]{1,0:T(8,128)(2,1)} %add_convert_fusion.9), channel_id=1, source_target_pairs={{0,66},{2,64},{4,70},{6,68},{8,74},{10,72},{12,78},{14,76},{16,82}... | collective-permute-start | bytes 147464 | tf_op jit(solution)/shard_map/ppermute | solution.py:34
  146.5 15.5 %collective-permute-start.32 = (bf16[32,768]{1,0:T(8,128)(2,1)}, bf16[32,768]{1,0:T(8,128)(2,1)}, u32[]{:S(2)}, u32[]{:S(2)}) collective-permute-start(bf16[32,768]{1,0:T(8,128)(2,1)} %add_convert_fusion.9), channel_id=1, source_target_pairs={{0,64},{2,66},{4,68},{6,70},{8,72},{10,74},{12,76},{14,78},{16,80}... | collective-permute-start | bytes 147464 | tf_op jit(solution)/shard_map/ppermute | solution.py:34
  148.6 15.4 %collective-permute-start.33 = (bf16[32,768]{1,0:T(8,128)(2,1)}, bf16[32,768]{1,0:T(8,128)(2,1)}, u32[]{:S(2)}, u32[]{:S(2)}) collective-permute-start(bf16[32,768]{1,0:T(8,128)(2,1)} %add_convert_fusion.9), channel_id=1, source_target_pairs={{0,2},{2,0},{4,6},{6,4},{8,10},{10,8},{12,14},{14,12},{16,18},{18,... | collective-permute-start | bytes 147464 | tf_op jit(solution)/shard_map/ppermute | solution.py:34
  148.6 20.3 %collective-permute-start.14 = (bf16[256,768]{1,0:T(8,128)(2,1)}, bf16[256,768]{1,0:T(8,128)(2,1)}, u32[]{:S(2)}, u32[]{:S(2)}) collective-permute-start(bf16[256,768]{1,0:T(8,128)(2,1)} %copy-done.14), channel_id=1, source_target_pairs={{0,4},{2,6},{4,8},{6,10},{8,12},{10,14},{16,20},{18,22},{20,24},{2... | collective-permute-start | bytes 1179656 | tf_op jit(solution)/shard_map/ppermute | solution.py:34
  152.4 19.6 %collective-permute-start.16 = (bf16[256,768]{1,0:T(8,128)(2,1)}, bf16[256,768]{1,0:T(8,128)(2,1)}, u32[]{:S(2)}, u32[]{:S(2)}) collective-permute-start(bf16[256,768]{1,0:T(8,128)(2,1)} %copy-done.13), channel_id=1, source_target_pairs={{0,4},{2,6},{4,8},{6,10},{8,12},{10,14},{16,20},{18,22},{20,24},{2... | collective-permute-start | bytes 1179656 | tf_op jit(solution)/shard_map/ppermute | solution.py:34
  159.0 14.2 %collective-permute-start.19 = (bf16[256,768]{1,0:T(8,128)(2,1)}, bf16[256,768]{1,0:T(8,128)(2,1)S(1)}, u32[]{:S(2)}, u32[]{:S(2)}) collective-permute-start(bf16[256,768]{1,0:T(8,128)(2,1)} %copy-done.12), channel_id=1, source_target_pairs={{4,0},{6,2},{8,4},{10,6},{12,8},{14,10},{20,16},{22,18},{24,20},{2... | collective-permute-start | bytes 1179656 | tf_op jit(solution)/shard_map/ppermute | solution.py:34
  162.0 18.2 %collective-permute-start.21 = (bf16[256,768]{1,0:T(8,128)(2,1)S(1)}, bf16[256,768]{1,0:T(8,128)(2,1)S(1)}, u32[]{:S(2)}, u32[]{:S(2)}) collective-permute-start(bf16[256,768]{1,0:T(8,128)(2,1)S(1)} %copy-done.11), channel_id=1, source_target_pairs={{4,0},{6,2},{8,4},{10,6},{12,8},{14,10},{20,16},{22,18},{24,20},{2... | collective-permute-start | bytes 1179656 | tf_op jit(solution)/shard_map/ppermute | solution.py:34
  164.0 24.9 %collective-permute-start.13 = (bf16[256,768]{1,0:T(8,128)(2,1)S(1)}, bf16[256,768]{1,0:T(8,128)(2,1)S(1)}, u32[]{:S(2)}, u32[]{:S(2)}) collective-permute-start(bf16[256,768]{1,0:T(8,128)(2,1)S(1)} %copy-done.9), channel_id=1, source_target_pairs={{0,4},{2,6},{4,8},{6,10},{8,12},{10,14},{16,20},{18,22},{20,24},{2... | collective-permute-start | bytes 1179656 | tf_op jit(solution)/shard_map/ppermute | solution.py:34
  168.9 29.9 %collective-permute-start.18 = (bf16[256,768]{1,0:T(8,128)(2,1)S(1)}, bf16[256,768]{1,0:T(8,128)(2,1)S(1)}, u32[]{:S(2)}, u32[]{:S(2)}) collective-permute-start(bf16[256,768]{1,0:T(8,128)(2,1)S(1)} %copy-done.7), channel_id=1, source_target_pairs={{4,0},{6,2},{8,4},{10,6},{12,8},{14,10},{20,16},{22,18},{24,20},{2... | collective-permute-start | bytes 1179656 | tf_op jit(solution)/shard_map/ppermute | solution.py:34
  172.0 12.2 %collective-permute-start.34 = (bf16[2,32,768]{2,1,0:T(8,128)(2,1)S(1)}, bf16[2,32,768]{2,1,0:T(8,128)(2,1)S(1)}, u32[]{:S(2)}, u32[]{:S(2)}) collective-permute-start(bf16[2,32,768]{2,1,0:T(8,128)(2,1)S(1)} %pad_maximum_fusion.2), channel_id=1, source_target_pairs={{0,4},{2,6},{4,0},{6,2},{8,12},{10,14},{12,8},{14,10},{16,20},{18,... | collective-permute-start | bytes 294920 | tf_op jit(solution)/shard_map/ppermute | solution.py:34
  173.2 17.6 %collective-permute-start.35 = (bf16[2,32,768]{2,1,0:T(8,128)(2,1)S(1)}, bf16[2,32,768]{2,1,0:T(8,128)(2,1)S(1)}, u32[]{:S(2)}, u32[]{:S(2)}) collective-permute-start(bf16[2,32,768]{2,1,0:T(8,128)(2,1)S(1)} %pad_maximum_fusion.2), channel_id=1, source_target_pairs={{0,8},{2,10},{4,12},{6,14},{8,0},{10,2},{12,4},{14,6},{16,24},{18,... | collective-permute-start | bytes 294920 | tf_op jit(solution)/shard_map/ppermute | solution.py:34
  180.2 16.6 %collective-permute-start.36 = (bf16[2,32,768]{2,1,0:T(8,128)(2,1)S(1)}, bf16[2,32,768]{2,1,0:T(8,128)(2,1)S(1)}, u32[]{:S(2)}, u32[]{:S(2)}) collective-permute-start(bf16[2,32,768]{2,1,0:T(8,128)(2,1)S(1)} %pad_maximum_fusion.2), channel_id=1, source_target_pairs={{0,12},{2,14},{4,8},{6,10},{8,4},{10,6},{12,0},{14,2},{16,28},{18,... | collective-permute-start | bytes 294920 | tf_op jit(solution)/shard_map/ppermute | solution.py:34
  184.2 17.4 %collective-permute-start.15 = (bf16[256,768]{1,0:T(8,128)(2,1)S(1)}, bf16[256,768]{1,0:T(8,128)(2,1)S(1)}, u32[]{:S(2)}, u32[]{:S(2)}) collective-permute-start(bf16[256,768]{1,0:T(8,128)(2,1)S(1)} %add_convert_fusion.5), channel_id=1, source_target_pairs={{16,0},{18,2},{20,4},{22,6},{24,8},{26,10},{28,12},{30,14},{32,16}... | collective-permute-start | bytes 1179656 | tf_op jit(solution)/shard_map/ppermute | solution.py:34
  188.8 18.4 %collective-permute-start.17 = (bf16[256,768]{1,0:T(8,128)(2,1)S(1)}, bf16[256,768]{1,0:T(8,128)(2,1)S(1)}, u32[]{:S(2)}, u32[]{:S(2)}) collective-permute-start(bf16[256,768]{1,0:T(8,128)(2,1)S(1)} %add_convert_fusion.4), channel_id=1, source_target_pairs={{0,16},{2,18},{4,20},{6,22},{8,24},{10,26},{12,28},{14,30},{16,32}... | collective-permute-start | bytes 1179656 | tf_op jit(solution)/shard_map/ppermute | solution.py:34
  190.8 16.5 %collective-permute-start.20 = (bf16[256,768]{1,0:T(8,128)(2,1)S(1)}, bf16[256,768]{1,0:T(8,128)(2,1)S(1)}, u32[]{:S(2)}, u32[]{:S(2)}) collective-permute-start(bf16[256,768]{1,0:T(8,128)(2,1)S(1)} %add_convert_fusion.2), channel_id=1, source_target_pairs={{16,0},{18,2},{20,4},{22,6},{24,8},{26,10},{28,12},{30,14},{32,16}... | collective-permute-start | bytes 1179656 | tf_op jit(solution)/shard_map/ppermute | solution.py:34
  196.8 20.7 %collective-permute-start.22 = (bf16[256,768]{1,0:T(8,128)(2,1)S(1)}, bf16[256,768]{1,0:T(8,128)(2,1)S(1)}, u32[]{:S(2)}, u32[]{:S(2)}) collective-permute-start(bf16[256,768]{1,0:T(8,128)(2,1)S(1)} %add_convert_fusion.1), channel_id=1, source_target_pairs={{0,16},{2,18},{4,20},{6,22},{8,24},{10,26},{12,28},{14,30},{16,32}... | collective-permute-start | bytes 1179656 | tf_op jit(solution)/shard_map/ppermute | solution.py:34
  198.8 32.8 %collective-permute-start.37 = (bf16[4,2,32,768]{3,2,1,0:T(8,128)(2,1)S(1)}, bf16[4,2,32,768]{3,2,1,0:T(8,128)(2,1)S(1)}, u32[]{:S(2)}, u32[]{:S(2)}) collective-permute-start(bf16[4,2,32,768]{3,2,1,0:T(8,128)(2,1)S(1)} %bitcast_dynamic-update-slice_fusion), channel_id=1, source_target_pairs={{0,128},{2,130},{4,132},{6,134},{8,136},{10,138},{12,140},{14,142}... | collective-permute-start | bytes 1179656 | tf_op jit(solution)/shard_map/ppermute | solution.py:34
  218.0 18.6 %collective-permute-start.23 = (bf16[256,768]{1,0:T(8,128)(2,1)S(1)}, bf16[256,768]{1,0:T(8,128)(2,1)S(1)}, u32[]{:S(2)}, u32[]{:S(2)}) collective-permute-start(bf16[256,768]{1,0:T(8,128)(2,1)S(1)} %get-tuple-element.61), channel_id=1, source_target_pairs={{0,2},{2,0},{4,6},{6,4},{8,10},{10,8},{12,14},{14,12},{16,18},{18,... | collective-permute-start | bytes 1179656 | tf_op jit(solution)/shard_map/ppermute | solution.py:34
  (37 other events, 370.9 us)

commit v2 on v1

v2 whole, which is shorter than its diff:
```python
import functools

import jax
import jax.numpy as jnp
import numpy as np
from jax import lax
from jax.experimental import pallas as pl
from jax.experimental.pallas import tpu as pltpu
from jax.sharding import PartitionSpec as P

HD = 128
TILE = 8
TILE_T = 2
AXES = ("ha", "wa")
FRAME_PARTS = 16
COL_PARTS = 8
RUN = 4
HEADS = 3
HALF = HEADS * HD
PAIR = 2 * HD
BLOCK = 256
TEXT = 192
SCALE = HD**-0.5
EXP_SCALE = SCALE * float(np.log2(np.e))
GROUPS = ((4,), (7,), (1, 2), (0,), (3,), (9, 10), (8,), (11,))
TILE_PARTS = ((0, 0, 0), (64, 1, 0), (128, 0, 1), (192, 1, 1))
COLS = ((0, 256), (0, 512), (0, 512), (256, 512))


def move(block, step):
    route = []
    for ha in range(FRAME_PARTS):
        for wa in range(COL_PARTS):
            there_ha, there_wa = step(ha, wa)
            if 0 <= there_ha < FRAME_PARTS and 0 <= there_wa < COL_PARTS:
                route.append((ha * COL_PARTS + wa, there_ha * COL_PARTS + there_wa))
    return lax.ppermute(block, AXES, route)


def across(ha, wa):
    return ha, wa ^ 1


def frames_by(distance):
    def step(ha, wa):
        there = ha + distance
        return there, wa ^ ((ha // RUN ^ there // RUN) & 1)

    return step


def cols_by(distance):
    return lambda ha, wa: (ha, wa + 2 * distance)


def flip(ha_bits, wa_bits):
    return lambda ha, wa: (ha ^ ha_bits, wa ^ wa_bits)


def lanes(start, count=HD):
    return pl.ds(pl.multiple_of(start, HD), count)


def split_kernel(group_ref, first_ref, second_ref, send_ref, keep_ref):
    group = group_ref[0]
    for out_ref, start in ((send_ref, (1 - group) * HALF), (keep_ref, group * HALF)):
        for at, frame, row in TILE_PARTS:
            for head in range(HEADS):
                for ref, low in ((first_ref, head * PAIR), (second_ref, head * PAIR + HD)):
                    part = ref[frame, row, :, lanes(start + head * HD)]
                    out_ref[at : at + 64, low : low + HD] = part


def split_heads(group, first, second):
    shape = (TILE_T, 2, TILE * TILE, 2 * HALF)
    source = pl.BlockSpec(shape, lambda i, g: (0, 0, 0, 0))
    target = pl.BlockSpec((BLOCK, 2 * HALF), lambda i, g: (0, 0))
    out = jax.ShapeDtypeStruct((BLOCK, 2 * HALF), jnp.bfloat16)
    return pl.pallas_call(
        split_kernel,
        out_shape=(out, out),
        grid_spec=pltpu.PrefetchScalarGridSpec(
            num_scalar_prefetch=1, grid=(1,), in_specs=[source, source], out_specs=(target, target)
        ),
        cost_estimate=pl.CostEstimate(flops=0, bytes_accessed=1600000, transcendentals=0),
        name="split_heads",
    )(group, first.reshape(shape), second.reshape(shape))


def join_pair_kernel(group_ref, keep_ref, got_ref, first_ref, second_ref):
    group = group_ref[0]
    for in_ref, start in ((keep_ref, group * HALF), (got_ref, (1 - group) * HALF)):
        for at, frame, row in TILE_PARTS:
            for head in range(HEADS):
                for ref, low in ((first_ref, head * PAIR), (second_ref, head * PAIR + HD)):
                    part = in_ref[at : at + 64, low : low + HD]
                    ref[frame, row, :, lanes(start + head * HD)] = part


def join_one_kernel(group_ref, keep_ref, got_ref, out_ref):
    group = group_ref[0]
    for in_ref, start in ((keep_ref, group * HALF), (got_ref, (1 - group) * HALF)):
        for at, frame, row in TILE_PARTS:
            out_ref[frame, row, :, lanes(start, HALF)] = in_ref[at : at + 64, :]


def join_heads(group, keep, got, kernel, count):
    shape = (TILE_T, 2, TILE * TILE, 2 * HALF)
    source = pl.BlockSpec(keep.shape, lambda i, g: (0, 0))
    target = pl.BlockSpec(shape, lambda i, g: (0, 0, 0, 0))
    out = jax.ShapeDtypeStruct(shape, jnp.bfloat16)
    parts = pl.pallas_call(
        kernel,
        out_shape=(out,) * count,
        grid_spec=pltpu.PrefetchScalarGridSpec(
            num_scalar_prefetch=1,
            grid=(1,),
            in_specs=[source, source],
            out_specs=(target,) * count,
        ),
        cost_estimate=pl.CostEstimate(flops=0, bytes_accessed=800000 * count, transcendentals=0),
        name="join_heads",
    )(group, keep, got)
    return [part.reshape(TILE_T, 2 * TILE, TILE, 2 * HALF) for part in parts]


def dot_t(left, right):
    return lax.dot_general(
        left, right, (((1,), (1,)), ((), ())), preferred_element_type=jnp.float32
    )


def dot(left, right):
    return lax.dot_general(
        left, right, (((1,), (0,)), ((), ())), preferred_element_type=jnp.float32
    )


def t_dot(left, right):
    return lax.dot_general(
        left, right, (((0,), (0,)), ((), ())), preferred_element_type=jnp.float32
    )


def fold(values, op):
    return op(values.reshape(values.shape[0] // 8, 8, values.shape[1]), axis=0)


def attend_kernel(flag_ref, bias_ref, text_bias_ref, qg_ref, text_ref, *refs):
    kv_refs, far_refs, mid_refs = refs[:12], refs[12:14], refs[14:17]
    dq_refs, dtext_ref, side_refs = refs[17:19], refs[19], refs[20:22]
    p_ref, dp_ref, high_ref, total_ref, delta_ref, dq_sum_ref = refs[22:]
    head = pl.program_id(0)

    def visible(block):
        return flag_ref[head * 12 + block] != 0

    def q(low, high):
        return qg_ref[low:high, :HD]

    def g(low, high):
        return qg_ref[low:high, HD:]

    def rows(block):
        return slice(block * BLOCK, block * BLOCK + (TEXT if block == 12 else BLOCK))

    def grad(block):
        step, column = divmod(block, 4)
        if column in (1, 2):
            return mid_refs[step].at[rows(column - 1), :]
        if step == 1:
            return side_refs[column // 3]
        return far_refs[column // 3].at[rows(step // 2), :]

    def spare(block):
        return slice(block * 8, block * 8 + 8)

    def weigh(block, pair_ref, bias, low, high, start=False):
        width = high - low
        scores = dot_t(pair_ref[:, :HD], q(low, high))
        dp = dot_t(pair_ref[:, HD:], g(low, high))
        dp_ref[rows(block), low:high] = dp
        if start:
            scores = scores + bias
        else:
            scores = (scores.reshape(2, 128, width) + bias[:, None, :]).reshape(BLOCK, width)
        highest = fold(scores, jnp.max)
        if not start:
            old = high_ref[spare(12), low:high]
            highest = jnp.maximum(old, highest)
            shrink = jnp.exp2((old - highest) * EXP_SCALE)
        p = jnp.exp2((scores.reshape(-1, 8, width) - highest[None]) * EXP_SCALE)
        total, delta = jnp.sum(p, axis=0), jnp.sum(p * dp.reshape(-1, 8, width), axis=0)
        p_ref[rows(block), low:high] = p.reshape(-1, width)
        if not start:
            total = total + total_ref[:, low:high] * shrink
            delta = delta + delta_ref[:, low:high] * shrink
            high_ref[spare(block), low:high] = highest
        else:
            high_ref[spare(13), low:high] = highest
        high_ref[spare(12), low:high] = highest
        total_ref[:, low:high] = total
        delta_ref[:, low:high] = delta

    weigh(12, text_ref, text_bias_ref[:, :1], 0, 512, start=True)
    def weigh_all(group):
        for block in group:
            low, high = COLS[block % 4]
            bias = bias_ref[0, 2 * block : 2 * block + 2, low:high]
            weigh(block, kv_refs[block], bias, low, high)

    weigh_all((5, 6))
    for group in GROUPS:
        pl.when(visible(group[0]))(functools.partial(weigh_all, group))

    last = high_ref[spare(12), :]
    highest = jnp.max(last, axis=0, keepdims=True)
    shrink = jnp.exp2((last - highest) * EXP_SCALE)
    inverse = 1.0 / jnp.sum(total_ref[...] * shrink, axis=0, keepdims=True)
    delta = jnp.sum(delta_ref[...] * shrink, axis=0, keepdims=True) * inverse

    def spread(block, key, out_ref, low, high):
        width = high - low
        at = spare(block + (block == 12))
        shrink = jnp.exp2((high_ref[at, low:high] - highest[:, low:high]) * EXP_SCALE)
        shrink = shrink * inverse[:, low:high]
        prob = p_ref[rows(block), low:high].reshape(-1, 8, width) * shrink[None]
        prob = prob.reshape(-1, width)
        ds = prob * ((dp_ref[rows(block), low:high] - delta[:, low:high]) * SCALE)
        ds = ds.astype(jnp.bfloat16)
        prob = prob.astype(jnp.bfloat16)
        out_ref[:, :HD] = dot(ds, q(low, high)).astype(jnp.bfloat16)
        out_ref[:, HD:] = dot(prob, g(low, high)).astype(jnp.bfloat16)
        return t_dot(key, ds)

    dq_sum_ref[...] = spread(12, text_ref[:, :HD], dtext_ref, 0, 512)
    def spread_all(group):
        for block in group:
            low, high = COLS[block % 4]
            dq_sum_ref[:, low:high] += spread(
                block, kv_refs[block][:, :HD], grad(block), low, high
            )

    def clear_all(group):
        for block in group:
            grad(block)[...] = jnp.zeros((BLOCK, PAIR), jnp.bfloat16)

    spread_all((5, 6))
    for group in GROUPS:
        pl.when(visible(group[0]))(functools.partial(spread_all, group))
        pl.when(jnp.logical_not(visible(group[0])))(functools.partial(clear_all, group))

    mirrored = flag_ref[36] != 0
    for ref, low, high in zip(dq_refs, (0, BLOCK), (BLOCK, 0)):
        sums = jnp.where(
            mirrored, dq_sum_ref[:, high : high + BLOCK], dq_sum_ref[:, low : low + BLOCK]
        )
        ref[...] = sums.T.astype(jnp.bfloat16)


def attend(flags, bias, text_bias, qg, text, blocks):
    pair = pl.BlockSpec((BLOCK, PAIR), lambda h, f: (0, h))
    text_pair = pl.BlockSpec((TEXT, PAIR), lambda h, f: (0, h))
    text_out = jax.ShapeDtypeStruct((TEXT, 2 * HALF), jnp.bfloat16)
    wide = pl.BlockSpec((2 * BLOCK, PAIR), lambda h, f: (0, h))
    out = jax.ShapeDtypeStruct((BLOCK, 2 * HALF), jnp.bfloat16)
    wide_out = jax.ShapeDtypeStruct((2 * BLOCK, 2 * HALF), jnp.bfloat16)
    results = pl.pallas_call(
        attend_kernel,
        out_shape=(wide_out,) * 2
        + (wide_out,) * 3
        + (jax.ShapeDtypeStruct((BLOCK, HALF), jnp.bfloat16),) * 2
        + (text_out,)
        + (out,) * 2,
        grid_spec=pltpu.PrefetchScalarGridSpec(
            num_scalar_prefetch=1,
            grid=(HEADS,),
            in_specs=[
                pl.BlockSpec((1, 24, 2 * BLOCK), lambda h, f: (h, 0, 0)),
                pl.BlockSpec((TEXT, HD), lambda h, f: (0, 0)),
                pl.BlockSpec((2 * BLOCK, PAIR), lambda h, f: (0, h)),
                text_pair,
            ]
            + [pair] * 12,
            out_specs=(wide,) * 2
            + (wide,) * 3
            + (pl.BlockSpec((BLOCK, HD), lambda h, f: (0, h)),) * 2
            + (text_pair,)
            + (pair,) * 2,
            scratch_shapes=[
                pltpu.VMEM((13 * BLOCK, 2 * BLOCK), jnp.float32),
                pltpu.VMEM((13 * BLOCK, 2 * BLOCK), jnp.float32),
                pltpu.VMEM((8 * 14, 2 * BLOCK), jnp.float32),
                pltpu.VMEM((8, 2 * BLOCK), jnp.float32),
                pltpu.VMEM((8, 2 * BLOCK), jnp.float32),
                pltpu.VMEM((HD, 2 * BLOCK), jnp.float32),
            ],
        ),
        compiler_params=pltpu.CompilerParams(vmem_limit_bytes=60 * 1024 * 1024),
        cost_estimate=pl.CostEstimate(
            flops=10 * 512 * 2560 * HD * HEADS,
            bytes_accessed=12000000,
            transcendentals=512 * 2560 * HEADS,
        ),
        name="attend",
    )(flags, bias, text_bias, qg, text, *blocks)
    return results[:2], results[2:5], results[5:7], results[7], results[8:]


def visibility(reach, ha, wa):
    between = lambda d, low, high: (d >= -low) & (d <= high)
    column = wa // 2 * 2
    s = jnp.arange(3, dtype=jnp.int32) - 1
    frames = between(s[None, :], reach[:, 0:1], reach[:, 1:2])
    frames = frames & (ha + s >= 0)[None, :] & (ha + s < FRAME_PARTS)[None, :]
    two = jnp.arange(2, dtype=jnp.int32)
    r = two[:, None] - two[None, :]
    rows = between(r[None], reach[:, 2, None, None], reach[:, 3, None, None])
    c = jnp.arange(4, dtype=jnp.int32) - 1
    d = c[:, None] - two[None, :]
    cols = between(d[None], reach[:, 4, None, None], reach[:, 5, None, None])
    cols = cols & ((column + c >= 0) & (column + c < COL_PARTS))[None, :, None]
    seen = (
        frames[:, :, None, None, None, None]
        & cols[:, None, :, None, :, None]
        & rows[:, None, None, :, None, :]
    )
    flags = jnp.any(seen, axis=(3, 4, 5)).astype(jnp.int32).reshape(HEADS * 12)
    bias = jnp.where(seen, 0.0, -jnp.inf).astype(jnp.float32).reshape(HEADS, 24, 4, 1)
    bias = jnp.broadcast_to(bias, (HEADS, 24, 4, 128)).reshape(HEADS, 24, 512)
    return flags, bias


def added(*parts):
    total = parts[0].astype(jnp.float32)
    for part in parts[1:]:
        total = total + part.astype(jnp.float32)
    return total.astype(jnp.bfloat16)


def halve_text(part, ha):
    upper = ha // RUN // 2
    other = lax.dynamic_slice_in_dim(part, (1 - upper) * (TEXT // 2), TEXT // 2, 0)
    return lax.dynamic_slice_in_dim(part, upper * (TEXT // 2), TEXT // 2, 0), move(other, flip(2 * RUN, 0))


def sum_text(part, group, ha, wa, beyond):
    upper, x = ha // RUN // 2, wa // 2
    pieces = [
        move(lax.dynamic_slice_in_dim(part, (x ^ d) * (TEXT // 8), TEXT // 8, 0), flip(0, 2 * d))
        for d in (1, 2, 3)
    ]
    part = added(lax.dynamic_slice_in_dim(part, x * (TEXT // 8), TEXT // 8, 0), *pieces)
    part, beyond[0], beyond[1] = lax.optimization_barrier((part, beyond[0], beyond[1]))
    near = [move(part, flip(d, 0)).astype(jnp.float32) for d in (1, 2, 3)]
    part = ((part.astype(jnp.float32) + near[0]) + (near[1] + near[2])).astype(jnp.bfloat16)
    mine = added(part, move(part, flip(RUN, 1)))
    theirs = added(move(part, flip(RUN, 0)), move(part, flip(0, 1)))
    both = jnp.stack(
        [jnp.where(group == 0, mine, theirs), jnp.where(group == 0, theirs, mine)], axis=0
    )
    quarter = jnp.zeros((4,) + both.shape, both.dtype)
    quarter = lax.dynamic_update_index_in_dim(quarter, both, x, 0)
    for d in (1, 2, 3):
        quarter = lax.dynamic_update_index_in_dim(quarter, move(both, flip(0, 2 * d)), x ^ d, 0)
    distant = move(quarter, flip(2 * RUN, 0))
    whole = jnp.stack(
        [jnp.where(upper == 0, quarter, distant), jnp.where(upper == 0, distant, quarter)], axis=0
    )
    whole = whole.reshape(2, 4, 2, TEXT // 8, HEADS, 2, HD)
    whole = whole.transpose(5, 0, 1, 3, 2, 4, 6).reshape(2, TEXT, 2 * HALF)
    whole = jnp.pad(whole, ((0, 0), (0, 256 - TEXT), (0, 0)))
    return whole[0], whole[1]


def body(
    queries, key_video, value_video, grad_output, text_keys, text_values, window_reach, text_valid
):
    ha, wa = lax.axis_index("ha"), lax.axis_index("wa")
    side = wa % 2
    group = (side + ha // RUN) % 2
    group_at = group.reshape(1).astype(jnp.int32)

    def placed(keep, got):
        return jnp.where(side == 0, keep, got), jnp.where(side == 0, got, keep)

    send_kv, keep_kv = split_heads(group_at, key_video, value_video)
    own = placed(keep_kv, move(send_kv, across))
    send_qg, keep_qg = split_heads(group_at, queries, grad_output)
    earlier = [move(block, frames_by(1)) for block in own]
    later = [move(block, frames_by(-1)) for block in own]
    beside = [move(own[1], cols_by(1)), move(own[0], cols_by(-1))]
    reach = lax.dynamic_slice_in_dim(window_reach, group * HEADS, HEADS, 0)
    flags, bias = visibility(reach, ha, wa)
    flags = jnp.concatenate([flags, side.reshape(1).astype(jnp.int32)])
    text_bias = jnp.where(text_valid[:TEXT] > 0, 0.0, -jnp.inf).astype(jnp.float32)
    text_bias = jnp.broadcast_to(text_bias[:, None], (TEXT, HD))
    text = jnp.stack(
        [
            lax.dynamic_slice_in_dim(t[:TEXT], group * HALF, HALF, 1).reshape(TEXT, HEADS, HD)
            for t in (text_keys, text_values)
        ],
        axis=2,
    ).reshape(TEXT, 2 * HALF)
    send_qg, keep_qg, flags, bias, text_bias, text, _, _, _ = lax.optimization_barrier(
        (send_qg, keep_qg, flags, bias, text_bias, text, earlier, later, beside)
    )
    qg = jnp.concatenate(placed(keep_qg, move(send_qg, across)), axis=0)

    blocks = []
    for left, right in (earlier, later):
        blocks += [move(right, cols_by(1)), left, right, move(left, cols_by(-1))]
    blocks[4:4] = [beside[0], *own, beside[1]]

    far, mids, (dq_own, dq_other), dtext, sides = attend(
        flags, bias, text_bias, qg, text, blocks
    )

    to_left = move(far[1], cols_by(1))
    to_right = move(far[0], cols_by(-1))
    dq_got = move(dq_other, across)
    dtext = halve_text(dtext, ha)
    to_left, to_right, dtext, sides = lax.optimization_barrier((to_left, to_right, dtext, sides))

    def frames(step):
        at = slice(step // 2 * BLOCK, (step // 2 + 1) * BLOCK)
        return added(mids[step], jnp.concatenate([to_left[at], to_right[at]], axis=0))

    outer = [move(frames(0), frames_by(-1)), move(frames(2), frames_by(1))]
    beyond = [move(sides[1], cols_by(1)), move(sides[0], cols_by(-1))]
    text_key_grad, text_value_grad = sum_text(added(*dtext), group, ha, wa, beyond)
    totals = added(mids[1], outer[0], outer[1], jnp.concatenate(beyond, axis=0))
    (query_grad,) = join_heads(group_at, dq_own, dq_got, join_one_kernel, 1)
    keep = jnp.where(side == 0, totals[:BLOCK], totals[BLOCK:])
    send = jnp.where(side == 0, totals[BLOCK:], totals[:BLOCK])
    key_grad, value_grad = join_heads(group_at, keep, move(send, across), join_pair_kernel, 2)
    return query_grad, key_grad, value_grad, text_key_grad, text_value_grad


def solution(mesh):
    video = P("ha", None, "wa", "ta")
    text = P(None, "ta")
    return jax.shard_map(
        body,
        mesh=mesh,
        in_specs=(video, video, video, video, text, text, P("ta", None), P()),
        out_specs=(video, video, video, text, text),
        check_vma=False,
    )
```

time: 242 us -> 207 us (0.86); the launches traced: 241 us -> 209 us
  starting transfers between devices: 125 us -> 94.8 us
  waiting for transfers between devices: 55.9 us -> 74.4 us
  Pallas kernels: 34.8 us -> 22.9 us
  local copies, waits for them, and re-layouts: 13.5 us -> 8.69 us
  other arithmetic: 10.3 us -> 6.56 us
    ppermute x38 -> x34, starting transfers between devices: 125 us -> 94.8 us  [move(): return lax.ppermute(block, AXES, route)]
    ppermute x38 -> x34, waiting for transfers between devices: 55.9 us -> 74.4 us  [move(): return lax.ppermute(block, AXES, route)]
    pallas_call x1, Pallas kernels: 21.6 us -> 14.7 us  [attend(): pl.pallas_call(attend_kernel, out_shape=(wide_out,) * 2 + (wide_out,) * 3...]
    unnamed x64 -> x42, local copies, waits for them, and re-layouts: 6.78 us -> 2.26 us
    pallas_call x2, Pallas kernels: 6.8 us -> 4.26 us  [split_heads(): pl.pallas_call(split_kernel, out_shape=(out, out), grid_spec=pltpu.Prefet...]
    pallas_call x2, Pallas kernels: 6.36 us -> 3.93 us  [join_heads(): pl.pallas_call(kernel, out_shape=(out,) * count, grid_spec=pltpu.Prefetch...]
  transfers between devices with their start and end apart: 38 -> 34, of which waited for: 14 -> 16; matrix products, arithmetic and copies ran while one was open for 7% -> 6% of each run, Pallas kernels for 3% -> 2%
where the time goes in v2:
time: 207 us; the launch traced here: 209 us
  starting transfers between devices  94.8 us (46%)
  waiting for transfers between devices  74.4 us (36%)
  Pallas kernels  22.9 us (11%)
  local copies, waits for them, and re-layouts  8.69 us (4%)
  other arithmetic  6.56 us (3%)
    ppermute x34, starting transfers between devices, move(): return lax.ppermute(block, AXES, route)  94.8 us
    ppermute x34, waiting for transfers between devices, move(): return lax.ppermute(block, AXES, route)  74.4 us
    pallas_call x1, Pallas kernels, attend(): pl.pallas_call(attend_kernel, out_shape=(wide_out,) * 2 + (wide_out,) * 3...  14.7 us
    pallas_call x2, Pallas kernels, split_heads(): pl.pallas_call(split_kernel, out_shape=(out, out), grid_spec=pltpu.Prefet...  4.26 us
  transfers between devices with their start and end apart: 34, of which 16 were waited for; matrix products, arithmetic and copies ran while one was open for 6% of the time, Pallas kernels for 2%

profile of v2, /device:TPU:10, one launch (start us, length us, event | category | flops | bytes accessed | tf_op | source)
XLA Modules:
  0.0 208.8 jit_solution(3539656190472338818)
XLA Ops:
  2.8 7.2 %collective-permute-start = (bf16[256,768]{1,0:T(8,128)(2,1)}, bf16[256,768]{1,0:T(8,128)(2,1)S(1)}, u32[]{:S(2)}, u32[]{:S(2)}) collective-permute-start(bf16[256,768]{1,0:T(8,128)(2,1)} %get-tuple-element.39), channel_id=1, source_target_pairs={{0,2},{2,0},{4,6},{6,4},{8,10},{10,8},{12,14},{14,12},{16,18},{18,... | collective-permute-start | bytes 1179656 | tf_op jit(solution)/shard_map/ppermute | solution.py:37
  10.7 9.8 %collective-permute-done = bf16[256,768]{1,0:T(8,128)(2,1)S(1)} collective-permute-done((bf16[256,768]{1,0:T(8,128)(2,1)}, bf16[256,768]{1,0:T(8,128)(2,1)S(1)}, u32[]{:S(2)}, u32[]{:S(2)}) %collective-permute-start) | collective-permute-done | bytes 393248 | tf_op jit(solution)/shard_map/ppermute | solution.py:37
  20.6 10.4 %collective-permute-start.1 = (bf16[256,768]{1,0:T(8,128)(2,1)S(1)}, bf16[256,768]{1,0:T(8,128)(2,1)S(1)}, u32[]{:S(2)}, u32[]{:S(2)}) collective-permute-start(bf16[256,768]{1,0:T(8,128)(2,1)S(1)} %get-tuple-element.82.refs_5_), channel_id=1, source_target_pairs={{0,16},{2,18},{4,20},{6,22},{8,24},{10,26},{12,28},{14,30},{16,32}... | collective-permute-start | bytes 1179656 | tf_op jit(solution)/shard_map/ppermute | solution.py:37
  33.5 3.9 %collective-permute-start.2 = (bf16[256,768]{1,0:T(8,128)(2,1)S(1)}, bf16[256,768]{1,0:T(8,128)(2,1)S(1)}, u32[]{:S(2)}, u32[]{:S(2)}) collective-permute-start(bf16[256,768]{1,0:T(8,128)(2,1)S(1)} %get-tuple-element.81.refs_6_), channel_id=1, source_target_pairs={{0,16},{2,18},{4,20},{6,22},{8,24},{10,26},{12,28},{14,30},{16,32}... | collective-permute-start | bytes 1179656 | tf_op jit(solution)/shard_map/ppermute | solution.py:37
  37.4 4.0 %collective-permute-start.4 = (bf16[256,768]{1,0:T(8,128)(2,1)S(1)}, bf16[256,768]{1,0:T(8,128)(2,1)S(1)}, u32[]{:S(2)}, u32[]{:S(2)}) collective-permute-start(bf16[256,768]{1,0:T(8,128)(2,1)S(1)} %get-tuple-element.81.refs_6_), channel_id=1, source_target_pairs={{16,0},{18,2},{20,4},{22,6},{24,8},{26,10},{28,12},{30,14},{32,16}... | collective-permute-start | bytes 1179656 | tf_op jit(solution)/shard_map/ppermute | solution.py:37
  41.5 3.4 %collective-permute-start.5 = (bf16[256,768]{1,0:T(8,128)(2,1)S(1)}, bf16[256,768]{1,0:T(8,128)(2,1)S(1)}, u32[]{:S(2)}, u32[]{:S(2)}) collective-permute-start(bf16[256,768]{1,0:T(8,128)(2,1)S(1)} %get-tuple-element.81.refs_6_), channel_id=1, source_target_pairs={{0,4},{2,6},{4,8},{6,10},{8,12},{10,14},{16,20},{18,22},{20,24},{2... | collective-permute-start | bytes 1179656 | tf_op jit(solution)/shard_map/ppermute | solution.py:37
  44.9 2.5 %collective-permute-start.6 = (bf16[256,768]{1,0:T(8,128)(2,1)S(1)}, bf16[256,768]{1,0:T(8,128)(2,1)}, u32[]{:S(2)}, u32[]{:S(2)}) collective-permute-start(bf16[256,768]{1,0:T(8,128)(2,1)S(1)} %get-tuple-element.82.refs_5_), channel_id=1, source_target_pairs={{4,0},{6,2},{8,4},{10,6},{12,8},{14,10},{20,16},{22,18},{24,20},{2... | collective-permute-start | bytes 1179656 | tf_op jit(solution)/shard_map/ppermute | solution.py:37
  53.2 3.3 %collective-permute-done.6.refs_7_ = bf16[256,768]{1,0:T(8,128)(2,1)} collective-permute-done((bf16[256,768]{1,0:T(8,128)(2,1)S(1)}, bf16[256,768]{1,0:T(8,128)(2,1)}, u32[]{:S(2)}, u32[]{:S(2)}) %collective-permute-start.6) | collective-permute-done | bytes 393248 | tf_op jit(solution)/shard_map/ppermute | solution.py:37
  57.2 6.3 %collective-permute-start.7 = (bf16[256,768]{1,0:T(8,128)(2,1)}, bf16[256,768]{1,0:T(8,128)(2,1)S(1)}, u32[]{:S(2)}, u32[]{:S(2)}) collective-permute-start(bf16[256,768]{1,0:T(8,128)(2,1)} %get-tuple-element.44), channel_id=1, source_target_pairs={{0,2},{2,0},{4,6},{6,4},{8,10},{10,8},{12,14},{14,12},{16,18},{18,... | collective-permute-start | bytes 1179656 | tf_op jit(solution)/shard_map/ppermute | solution.py:37
  63.4 3.1 %collective-permute-start.10 = (bf16[256,768]{1,0:T(8,128)(2,1)S(1)}, bf16[256,768]{1,0:T(8,128)(2,1)S(1)}, u32[]{:S(2)}, u32[]{:S(2)}) collective-permute-start(bf16[256,768]{1,0:T(8,128)(2,1)S(1)} %collective-permute-done.4.refs_10_), channel_id=1, source_target_pairs={{0,4},{2,6},{4,8},{6,10},{8,12},{10,14},{16,20},{18,22},{20,24},{2... | collective-permute-start | bytes 1179656 | tf_op jit(solution)/shard_map/ppermute | solution.py:37
  66.5 2.8 %collective-permute-start.11 = (bf16[256,768]{1,0:T(8,128)(2,1)S(1)}, bf16[256,768]{1,0:T(8,128)(2,1)S(1)}, u32[]{:S(2)}, u32[]{:S(2)}) collective-permute-start(bf16[256,768]{1,0:T(8,128)(2,1)S(1)} %collective-permute-done.3.refs_9_), channel_id=1, source_target_pairs={{4,0},{6,2},{8,4},{10,6},{12,8},{14,10},{20,16},{22,18},{24,20},{2... | collective-permute-start | bytes 1179656 | tf_op jit(solution)/shard_map/ppermute | solution.py:37
  69.3 3.1 %collective-permute-start.8 = (bf16[256,768]{1,0:T(8,128)(2,1)S(1)}, bf16[256,768]{1,0:T(8,128)(2,1)S(1)}, u32[]{:S(2)}, u32[]{:S(2)}) collective-permute-start(bf16[256,768]{1,0:T(8,128)(2,1)S(1)} %collective-permute-done.2.refs_2_), channel_id=1, source_target_pairs={{0,4},{2,6},{4,8},{6,10},{8,12},{10,14},{16,20},{18,22},{20,24},{2... | collective-permute-start | bytes 1179656 | tf_op jit(solution)/shard_map/ppermute | solution.py:37
  72.4 2.8 %collective-permute-start.9 = (bf16[256,768]{1,0:T(8,128)(2,1)S(1)}, bf16[256,768]{1,0:T(8,128)(2,1)S(1)}, u32[]{:S(2)}, u32[]{:S(2)}) collective-permute-start(bf16[256,768]{1,0:T(8,128)(2,1)S(1)} %collective-permute-done.1.refs_1_), channel_id=1, source_target_pairs={{4,0},{6,2},{8,4},{10,6},{12,8},{14,10},{20,16},{22,18},{24,20},{2... | collective-permute-start | bytes 1179656 | tf_op jit(solution)/shard_map/ppermute | solution.py:37
  75.2 3.1 %collective-permute-done.7 = bf16[256,768]{1,0:T(8,128)(2,1)S(1)} collective-permute-done((bf16[256,768]{1,0:T(8,128)(2,1)}, bf16[256,768]{1,0:T(8,128)(2,1)S(1)}, u32[]{:S(2)}, u32[]{:S(2)}) %collective-permute-start.7) | collective-permute-done | bytes 393248 | tf_op jit(solution)/shard_map/ppermute | solution.py:37
  80.4 2.5 %collective-permute-done.9.refs_3_ = bf16[256,768]{1,0:T(8,128)(2,1)S(1)} collective-permute-done((bf16[256,768]{1,0:T(8,128)(2,1)S(1)}, bf16[256,768]{1,0:T(8,128)(2,1)S(1)}, u32[]{:S(2)}, u32[]{:S(2)}) %collective-permute-start.9) | collective-permute-done | bytes 393248 | tf_op jit(solution)/shard_map/ppermute | solution.py:37
  83.6 14.7 %attend.1 = (bf16[512,768]{1,0:T(8,128)(2,1)}, bf16[512,768]{1,0:T(8,128)(2,1)}, bf16[512,768]{1,0:T(8,128)(2,1)}, bf16[512,768]{1,0:T(8,128)(2,1)}, bf16[512,76...) custom-call(s32[37]{0:T(128)} %pad_add_fusion.flag_ref, ...), custom_call_target="tpu_custom_call" | custom-call | flops 5033164800 | bytes 12000000 | tf_op jit(solution)/shard_map/attend/pallas_call | solution.py:268
  98.3 3.3 %collective-permute-start.13 = (bf16[512,768]{1,0:T(8,128)(2,1)}, bf16[512,768]{1,0:T(8,128)(2,1)S(1)}, u32[]{:S(2)}, u32[]{:S(2)}) collective-permute-start(bf16[512,768]{1,0:T(8,128)(2,1)} %get-tuple-element.50), channel_id=1, source_target_pairs={{0,4},{2,6},{4,8},{6,10},{8,12},{10,14},{16,20},{18,22},{20,24},{2... | collective-permute-start | bytes 2359304 | tf_op jit(solution)/shard_map/ppermute | solution.py:37
  101.6 2.6 %collective-permute-start.14 = (bf16[512,768]{1,0:T(8,128)(2,1)}, bf16[512,768]{1,0:T(8,128)(2,1)S(1)}, u32[]{:S(2)}, u32[]{:S(2)}) collective-permute-start(bf16[512,768]{1,0:T(8,128)(2,1)} %get-tuple-element.51), channel_id=1, source_target_pairs={{4,0},{6,2},{8,4},{10,6},{12,8},{14,10},{20,16},{22,18},{24,20},{2... | collective-permute-start | bytes 2359304 | tf_op jit(solution)/shard_map/ppermute | solution.py:37
  106.8 2.9 %collective-permute-start.15 = (bf16[96,768]{1,0:T(8,128)(2,1)S(1)}, bf16[96,768]{1,0:T(8,128)(2,1)S(1)}, u32[]{:S(2)}, u32[]{:S(2)}) collective-permute-start(bf16[96,768]{1,0:T(8,128)(2,1)S(1)} %get-tuple-element.87), channel_id=1, source_target_pairs={{0,128},{2,130},{4,132},{6,134},{8,136},{10,138},{12,140},{14,142}... | collective-permute-start | bytes 442376 | tf_op jit(solution)/shard_map/ppermute | solution.py:37
  109.6 6.8 %collective-permute-done.12.got_ref = bf16[256,384]{1,0:T(8,128)(2,1)S(1)} collective-permute-done((bf16[256,384]{1,0:T(8,128)(2,1)}, bf16[256,384]{1,0:T(8,128)(2,1)S(1)}, u32[]{:S(2)}, u32[]{:S(2)}) %collective-permute-start.12) | collective-permute-done | bytes 196640 | tf_op jit(solution)/shard_map/ppermute | solution.py:37
  119.5 2.8 %collective-permute-done.14 = bf16[512,768]{1,0:T(8,128)(2,1)S(1)} collective-permute-done((bf16[512,768]{1,0:T(8,128)(2,1)}, bf16[512,768]{1,0:T(8,128)(2,1)S(1)}, u32[]{:S(2)}, u32[]{:S(2)}) %collective-permute-start.14) | collective-permute-done | bytes 786464 | tf_op jit(solution)/shard_map/ppermute | solution.py:37
  128.2 3.7 %collective-permute-start.22 = (bf16[256,768]{1,0:T(8,128)(2,1)S(1)}, bf16[256,768]{1,0:T(8,128)(2,1)S(1)}, u32[]{:S(2)}, u32[]{:S(2)}) collective-permute-start(bf16[256,768]{1,0:T(8,128)(2,1)S(1)} %copy-done.10), channel_id=1, source_target_pairs={{4,0},{6,2},{8,4},{10,6},{12,8},{14,10},{20,16},{22,18},{24,20},{2... | collective-permute-start | bytes 1179656 | tf_op jit(solution)/shard_map/ppermute | solution.py:37
  132.1 4.3 %collective-permute-done.21 = bf16[256,768]{1,0:T(8,128)(2,1)S(1)} collective-permute-done((bf16[256,768]{1,0:T(8,128)(2,1)S(1)}, bf16[256,768]{1,0:T(8,128)(2,1)S(1)}, u32[]{:S(2)}, u32[]{:S(2)}) %collective-permute-start.21) | collective-permute-done | bytes 393248 | tf_op jit(solution)/shard_map/ppermute | solution.py:37
  139.3 3.6 %collective-permute-start.26 = (bf16[24,768]{1,0:T(8,128)(2,1)S(1)}, bf16[24,768]{1,0:T(8,128)(2,1)S(1)}, u32[]{:S(2)}, u32[]{:S(2)}) collective-permute-start(bf16[24,768]{1,0:T(8,128)(2,1)S(1)} %add_convert_fusion.7), channel_id=1, source_target_pairs={{0,48},{2,50},{4,52},{6,54},{8,56},{10,58},{12,60},{14,62},{16,32}... | collective-permute-start | bytes 110600 | tf_op jit(solution)/shard_map/ppermute | solution.py:37
  143.2 3.6 %collective-permute-start.16 = (bf16[512,768]{1,0:T(8,128)(2,1)S(1)}, bf16[512,768]{1,0:T(8,128)(2,1)S(1)}, u32[]{:S(2)}, u32[]{:S(2)}) collective-permute-start(bf16[512,768]{1,0:T(8,128)(2,1)S(1)} %add_convert_fusion.2), channel_id=1, source_target_pairs={{16,0},{18,2},{20,4},{22,6},{24,8},{26,10},{28,12},{30,14},{32,16}... | collective-permute-start | bytes 2359304 | tf_op jit(solution)/shard_map/ppermute | solution.py:37
  146.8 3.1 %collective-permute-start.27 = (bf16[24,768]{1,0:T(8,128)(2,1)S(1)}, bf16[24,768]{1,0:T(8,128)(2,1)S(1)}, u32[]{:S(2)}, u32[]{:S(2)}) collective-permute-start(bf16[24,768]{1,0:T(8,128)(2,1)S(1)} %add_convert_fusion.6), channel_id=1, source_target_pairs={{0,66},{2,64},{4,70},{6,68},{8,74},{10,72},{12,78},{14,76},{16,82}... | collective-permute-start | bytes 110600 | tf_op jit(solution)/shard_map/ppermute | solution.py:37
  149.9 3.3 %collective-permute-start.28 = (bf16[24,768]{1,0:T(8,128)(2,1)S(1)}, bf16[24,768]{1,0:T(8,128)(2,1)S(1)}, u32[]{:S(2)}, u32[]{:S(2)}) collective-permute-start(bf16[24,768]{1,0:T(8,128)(2,1)S(1)} %add_convert_fusion.6), channel_id=1, source_target_pairs={{0,64},{2,66},{4,68},{6,70},{8,72},{10,74},{12,76},{14,78},{16,80}... | collective-permute-start | bytes 110600 | tf_op jit(solution)/shard_map/ppermute | solution.py:37
  154.5 2.5 %collective-permute-start.17 = (bf16[512,768]{1,0:T(8,128)(2,1)S(1)}, bf16[512,768]{1,0:T(8,128)(2,1)S(1)}, u32[]{:S(2)}, u32[]{:S(2)}) collective-permute-start(bf16[512,768]{1,0:T(8,128)(2,1)S(1)} %add_convert_fusion.1), channel_id=1, source_target_pairs={{0,16},{2,18},{4,20},{6,22},{8,24},{10,26},{12,28},{14,30},{16,32}... | collective-permute-start | bytes 2359304 | tf_op jit(solution)/shard_map/ppermute | solution.py:37
  157.1 4.5 %collective-permute-done.29 = bf16[24,768]{1,0:T(8,128)(2,1)S(1)} collective-permute-done((bf16[24,768]{1,0:T(8,128)(2,1)S(1)}, bf16[24,768]{1,0:T(8,128)(2,1)S(1)}, u32[]{:S(2)}, u32[]{:S(2)}) %collective-permute-start.29) | collective-permute-done | bytes 36896 | tf_op jit(solution)/shard_map/ppermute | solution.py:37
  162.0 2.7 %collective-permute-start.31 = (bf16[2,24,768]{2,1,0:T(8,128)(2,1)S(1)}, bf16[2,24,768]{2,1,0:T(8,128)(2,1)S(1)}, u32[]{:S(2)}, u32[]{:S(2)}) collective-permute-start(bf16[2,24,768]{2,1,0:T(8,128)(2,1)S(1)} %pad_maximum_fusion.2), channel_id=1, source_target_pairs={{0,8},{2,10},{4,12},{6,14},{8,0},{10,2},{12,4},{14,6},{16,24},{18,... | collective-permute-start | bytes 221192 | tf_op jit(solution)/shard_map/ppermute | solution.py:37
  171.3 21.7 %collective-permute-done.17 = bf16[512,768]{1,0:T(8,128)(2,1)S(1)} collective-permute-done((bf16[512,768]{1,0:T(8,128)(2,1)S(1)}, bf16[512,768]{1,0:T(8,128)(2,1)S(1)}, u32[]{:S(2)}, u32[]{:S(2)}) %collective-permute-start.17) | collective-permute-done | bytes 786464 | tf_op jit(solution)/shard_map/ppermute | solution.py:37
  197.1 8.8 %collective-permute-done.23.got_ref = bf16[256,768]{1,0:T(8,128)(2,1)S(1)} collective-permute-done((bf16[256,768]{1,0:T(8,128)(2,1)S(1)}, bf16[256,768]{1,0:T(8,128)(2,1)S(1)}, u32[]{:S(2)}, u32[]{:S(2)}) %collective-permute-start.23) | collective-permute-done | bytes 393248 | tf_op jit(solution)/shard_map/ppermute | solution.py:37
  (144 shorter events, 44.6 us)
Async XLA Ops:
  2.8 17.6 %collective-permute-start = (bf16[256,768]{1,0:T(8,128)(2,1)}, bf16[256,768]{1,0:T(8,128)(2,1)S(1)}, u32[]{:S(2)}, u32[]{:S(2)}) collective-permute-start(bf16[256,768]{1,0:T(8,128)(2,1)} %get-tuple-element.39), channel_id=1, source_target_pairs={{0,2},{2,0},{4,6},{6,4},{8,10},{10,8},{12,14},{14,12},{16,18},{18,... | collective-permute-start | bytes 1179656 | tf_op jit(solution)/shard_map/ppermute | solution.py:37
  20.6 24.3 %collective-permute-start.1 = (bf16[256,768]{1,0:T(8,128)(2,1)S(1)}, bf16[256,768]{1,0:T(8,128)(2,1)S(1)}, u32[]{:S(2)}, u32[]{:S(2)}) collective-permute-start(bf16[256,768]{1,0:T(8,128)(2,1)S(1)} %get-tuple-element.82.refs_5_), channel_id=1, source_target_pairs={{0,16},{2,18},{4,20},{6,22},{8,24},{10,26},{12,28},{14,30},{16,32}... | collective-permute-start | bytes 1179656 | tf_op jit(solution)/shard_map/ppermute | solution.py:37
  31.5 21.4 %collective-permute-start.3 = (bf16[256,768]{1,0:T(8,128)(2,1)S(1)}, bf16[256,768]{1,0:T(8,128)(2,1)S(1)}, u32[]{:S(2)}, u32[]{:S(2)}) collective-permute-start(bf16[256,768]{1,0:T(8,128)(2,1)S(1)} %get-tuple-element.82.refs_5_), channel_id=1, source_target_pairs={{16,0},{18,2},{20,4},{22,6},{24,8},{26,10},{28,12},{30,14},{32,16}... | collective-permute-start | bytes 1179656 | tf_op jit(solution)/shard_map/ppermute | solution.py:37
  33.5 19.4 %collective-permute-start.2 = (bf16[256,768]{1,0:T(8,128)(2,1)S(1)}, bf16[256,768]{1,0:T(8,128)(2,1)S(1)}, u32[]{:S(2)}, u32[]{:S(2)}) collective-permute-start(bf16[256,768]{1,0:T(8,128)(2,1)S(1)} %get-tuple-element.81.refs_6_), channel_id=1, source_target_pairs={{0,16},{2,18},{4,20},{6,22},{8,24},{10,26},{12,28},{14,30},{16,32}... | collective-permute-start | bytes 1179656 | tf_op jit(solution)/shard_map/ppermute | solution.py:37
  37.4 15.5 %collective-permute-start.4 = (bf16[256,768]{1,0:T(8,128)(2,1)S(1)}, bf16[256,768]{1,0:T(8,128)(2,1)S(1)}, u32[]{:S(2)}, u32[]{:S(2)}) collective-permute-start(bf16[256,768]{1,0:T(8,128)(2,1)S(1)} %get-tuple-element.81.refs_6_), channel_id=1, source_target_pairs={{16,0},{18,2},{20,4},{22,6},{24,8},{26,10},{28,12},{30,14},{32,16}... | collective-permute-start | bytes 1179656 | tf_op jit(solution)/shard_map/ppermute | solution.py:37
  41.5 11.7 %collective-permute-start.5 = (bf16[256,768]{1,0:T(8,128)(2,1)S(1)}, bf16[256,768]{1,0:T(8,128)(2,1)S(1)}, u32[]{:S(2)}, u32[]{:S(2)}) collective-permute-start(bf16[256,768]{1,0:T(8,128)(2,1)S(1)} %get-tuple-element.81.refs_6_), channel_id=1, source_target_pairs={{0,4},{2,6},{4,8},{6,10},{8,12},{10,14},{16,20},{18,22},{20,24},{2... | collective-permute-start | bytes 1179656 | tf_op jit(solution)/shard_map/ppermute | solution.py:37
  44.9 11.5 %collective-permute-start.6 = (bf16[256,768]{1,0:T(8,128)(2,1)S(1)}, bf16[256,768]{1,0:T(8,128)(2,1)}, u32[]{:S(2)}, u32[]{:S(2)}) collective-permute-start(bf16[256,768]{1,0:T(8,128)(2,1)S(1)} %get-tuple-element.82.refs_5_), channel_id=1, source_target_pairs={{4,0},{6,2},{8,4},{10,6},{12,8},{14,10},{20,16},{22,18},{24,20},{2... | collective-permute-start | bytes 1179656 | tf_op jit(solution)/shard_map/ppermute | solution.py:37
  57.2 21.1 %collective-permute-start.7 = (bf16[256,768]{1,0:T(8,128)(2,1)}, bf16[256,768]{1,0:T(8,128)(2,1)S(1)}, u32[]{:S(2)}, u32[]{:S(2)}) collective-permute-start(bf16[256,768]{1,0:T(8,128)(2,1)} %get-tuple-element.44), channel_id=1, source_target_pairs={{0,2},{2,0},{4,6},{6,4},{8,10},{10,8},{12,14},{14,12},{16,18},{18,... | collective-permute-start | bytes 1179656 | tf_op jit(solution)/shard_map/ppermute | solution.py:37
  63.4 16.9 %collective-permute-start.10 = (bf16[256,768]{1,0:T(8,128)(2,1)S(1)}, bf16[256,768]{1,0:T(8,128)(2,1)S(1)}, u32[]{:S(2)}, u32[]{:S(2)}) collective-permute-start(bf16[256,768]{1,0:T(8,128)(2,1)S(1)} %collective-permute-done.4.refs_10_), channel_id=1, source_target_pairs={{0,4},{2,6},{4,8},{6,10},{8,12},{10,14},{16,20},{18,22},{20,24},{2... | collective-permute-start | bytes 1179656 | tf_op jit(solution)/shard_map/ppermute | solution.py:37
  66.5 13.8 %collective-permute-start.11 = (bf16[256,768]{1,0:T(8,128)(2,1)S(1)}, bf16[256,768]{1,0:T(8,128)(2,1)S(1)}, u32[]{:S(2)}, u32[]{:S(2)}) collective-permute-start(bf16[256,768]{1,0:T(8,128)(2,1)S(1)} %collective-permute-done.3.refs_9_), channel_id=1, source_target_pairs={{4,0},{6,2},{8,4},{10,6},{12,8},{14,10},{20,16},{22,18},{24,20},{2... | collective-permute-start | bytes 1179656 | tf_op jit(solution)/shard_map/ppermute | solution.py:37
  69.3 11.1 %collective-permute-start.8 = (bf16[256,768]{1,0:T(8,128)(2,1)S(1)}, bf16[256,768]{1,0:T(8,128)(2,1)S(1)}, u32[]{:S(2)}, u32[]{:S(2)}) collective-permute-start(bf16[256,768]{1,0:T(8,128)(2,1)S(1)} %collective-permute-done.2.refs_2_), channel_id=1, source_target_pairs={{0,4},{2,6},{4,8},{6,10},{8,12},{10,14},{16,20},{18,22},{20,24},{2... | collective-permute-start | bytes 1179656 | tf_op jit(solution)/shard_map/ppermute | solution.py:37
  72.4 10.4 %collective-permute-start.9 = (bf16[256,768]{1,0:T(8,128)(2,1)S(1)}, bf16[256,768]{1,0:T(8,128)(2,1)S(1)}, u32[]{:S(2)}, u32[]{:S(2)}) collective-permute-start(bf16[256,768]{1,0:T(8,128)(2,1)S(1)} %collective-permute-done.1.refs_1_), channel_id=1, source_target_pairs={{4,0},{6,2},{8,4},{10,6},{12,8},{14,10},{20,16},{22,18},{24,20},{2... | collective-permute-start | bytes 1179656 | tf_op jit(solution)/shard_map/ppermute | solution.py:37
  98.3 21.2 %collective-permute-start.13 = (bf16[512,768]{1,0:T(8,128)(2,1)}, bf16[512,768]{1,0:T(8,128)(2,1)S(1)}, u32[]{:S(2)}, u32[]{:S(2)}) collective-permute-start(bf16[512,768]{1,0:T(8,128)(2,1)} %get-tuple-element.50), channel_id=1, source_target_pairs={{0,4},{2,6},{4,8},{6,10},{8,12},{10,14},{16,20},{18,22},{20,24},{2... | collective-permute-start | bytes 2359304 | tf_op jit(solution)/shard_map/ppermute | solution.py:37
  101.6 20.8 %collective-permute-start.14 = (bf16[512,768]{1,0:T(8,128)(2,1)}, bf16[512,768]{1,0:T(8,128)(2,1)S(1)}, u32[]{:S(2)}, u32[]{:S(2)}) collective-permute-start(bf16[512,768]{1,0:T(8,128)(2,1)} %get-tuple-element.51), channel_id=1, source_target_pairs={{4,0},{6,2},{8,4},{10,6},{12,8},{14,10},{20,16},{22,18},{24,20},{2... | collective-permute-start | bytes 2359304 | tf_op jit(solution)/shard_map/ppermute | solution.py:37
  104.2 12.2 %collective-permute-start.12 = (bf16[256,384]{1,0:T(8,128)(2,1)}, bf16[256,384]{1,0:T(8,128)(2,1)S(1)}, u32[]{:S(2)}, u32[]{:S(2)}) collective-permute-start(bf16[256,384]{1,0:T(8,128)(2,1)} %get-tuple-element.47), channel_id=1, source_target_pairs={{0,2},{2,0},{4,6},{6,4},{8,10},{10,8},{12,14},{14,12},{16,18},{18,... | collective-permute-start | bytes 589832 | tf_op jit(solution)/shard_map/ppermute | solution.py:37
  106.8 12.2 %collective-permute-start.15 = (bf16[96,768]{1,0:T(8,128)(2,1)S(1)}, bf16[96,768]{1,0:T(8,128)(2,1)S(1)}, u32[]{:S(2)}, u32[]{:S(2)}) collective-permute-start(bf16[96,768]{1,0:T(8,128)(2,1)S(1)} %get-tuple-element.87), channel_id=1, source_target_pairs={{0,128},{2,130},{4,132},{6,134},{8,136},{10,138},{12,140},{14,142}... | collective-permute-start | bytes 442376 | tf_op jit(solution)/shard_map/ppermute | solution.py:37
  122.4 9.6 %collective-permute-start.18 = (bf16[24,768]{1,0:T(8,128)(2,1)S(1)}, bf16[24,768]{1,0:T(8,128)(2,1)S(1)}, u32[]{:S(2)}, u32[]{:S(2)}) collective-permute-start(bf16[24,768]{1,0:T(8,128)(2,1)S(1)} %get-tuple-element.91), channel_id=1, source_target_pairs={{0,4},{2,6},{4,0},{6,2},{8,12},{10,14},{12,8},{14,10},{16,20},{18,... | collective-permute-start | bytes 110600 | tf_op jit(solution)/shard_map/ppermute | solution.py:37
  123.3 8.7 %collective-permute-start.19 = (bf16[24,768]{1,0:T(8,128)(2,1)S(1)}, bf16[24,768]{1,0:T(8,128)(2,1)S(1)}, u32[]{:S(2)}, u32[]{:S(2)}) collective-permute-start(bf16[24,768]{1,0:T(8,128)(2,1)S(1)} %get-tuple-element.93), channel_id=1, source_target_pairs={{0,8},{2,10},{4,12},{6,14},{8,0},{10,2},{12,4},{14,6},{16,24},{18,... | collective-permute-start | bytes 110600 | tf_op jit(solution)/shard_map/ppermute | solution.py:37
  124.2 7.8 %collective-permute-start.20 = (bf16[24,768]{1,0:T(8,128)(2,1)S(1)}, bf16[24,768]{1,0:T(8,128)(2,1)S(1)}, u32[]{:S(2)}, u32[]{:S(2)}) collective-permute-start(bf16[24,768]{1,0:T(8,128)(2,1)S(1)} %get-tuple-element.92), channel_id=1, source_target_pairs={{0,12},{2,14},{4,8},{6,10},{8,4},{10,6},{12,0},{14,2},{16,28},{18,... | collective-permute-start | bytes 110600 | tf_op jit(solution)/shard_map/ppermute | solution.py:37
  126.0 10.3 %collective-permute-start.21 = (bf16[256,768]{1,0:T(8,128)(2,1)S(1)}, bf16[256,768]{1,0:T(8,128)(2,1)S(1)}, u32[]{:S(2)}, u32[]{:S(2)}) collective-permute-start(bf16[256,768]{1,0:T(8,128)(2,1)S(1)} %copy-done.11), channel_id=1, source_target_pairs={{0,4},{2,6},{4,8},{6,10},{8,12},{10,14},{16,20},{18,22},{20,24},{2... | collective-permute-start | bytes 1179656 | tf_op jit(solution)/shard_map/ppermute | solution.py:37
  128.2 10.4 %collective-permute-start.22 = (bf16[256,768]{1,0:T(8,128)(2,1)S(1)}, bf16[256,768]{1,0:T(8,128)(2,1)S(1)}, u32[]{:S(2)}, u32[]{:S(2)}) collective-permute-start(bf16[256,768]{1,0:T(8,128)(2,1)S(1)} %copy-done.10), channel_id=1, source_target_pairs={{4,0},{6,2},{8,4},{10,6},{12,8},{14,10},{20,16},{22,18},{24,20},{2... | collective-permute-start | bytes 1179656 | tf_op jit(solution)/shard_map/ppermute | solution.py:37
  138.5 8.2 %collective-permute-start.24 = (bf16[24,768]{1,0:T(8,128)(2,1)S(1)}, bf16[24,768]{1,0:T(8,128)(2,1)S(1)}, u32[]{:S(2)}, u32[]{:S(2)}) collective-permute-start(bf16[24,768]{1,0:T(8,128)(2,1)S(1)} %add_convert_fusion.7), channel_id=1, source_target_pairs={{0,16},{2,18},{4,20},{6,22},{8,24},{10,26},{12,28},{14,30},{16,0},... | collective-permute-start | bytes 110600 | tf_op jit(solution)/shard_map/ppermute | solution.py:37
  138.5 8.2 %collective-permute-start.25 = (bf16[24,768]{1,0:T(8,128)(2,1)S(1)}, bf16[24,768]{1,0:T(8,128)(2,1)S(1)}, u32[]{:S(2)}, u32[]{:S(2)}) collective-permute-start(bf16[24,768]{1,0:T(8,128)(2,1)S(1)} %add_convert_fusion.7), channel_id=1, source_target_pairs={{0,32},{2,34},{4,36},{6,38},{8,40},{10,42},{12,44},{14,46},{16,48}... | collective-permute-start | bytes 110600 | tf_op jit(solution)/shard_map/ppermute | solution.py:37
  139.3 7.5 %collective-permute-start.26 = (bf16[24,768]{1,0:T(8,128)(2,1)S(1)}, bf16[24,768]{1,0:T(8,128)(2,1)S(1)}, u32[]{:S(2)}, u32[]{:S(2)}) collective-permute-start(bf16[24,768]{1,0:T(8,128)(2,1)S(1)} %add_convert_fusion.7), channel_id=1, source_target_pairs={{0,48},{2,50},{4,52},{6,54},{8,56},{10,58},{12,60},{14,62},{16,32}... | collective-permute-start | bytes 110600 | tf_op jit(solution)/shard_map/ppermute | solution.py:37
  143.2 28.2 %collective-permute-start.16 = (bf16[512,768]{1,0:T(8,128)(2,1)S(1)}, bf16[512,768]{1,0:T(8,128)(2,1)S(1)}, u32[]{:S(2)}, u32[]{:S(2)}) collective-permute-start(bf16[512,768]{1,0:T(8,128)(2,1)S(1)} %add_convert_fusion.2), channel_id=1, source_target_pairs={{16,0},{18,2},{20,4},{22,6},{24,8},{26,10},{28,12},{30,14},{32,16}... | collective-permute-start | bytes 2359304 | tf_op jit(solution)/shard_map/ppermute | solution.py:37
  146.8 10.2 %collective-permute-start.27 = (bf16[24,768]{1,0:T(8,128)(2,1)S(1)}, bf16[24,768]{1,0:T(8,128)(2,1)S(1)}, u32[]{:S(2)}, u32[]{:S(2)}) collective-permute-start(bf16[24,768]{1,0:T(8,128)(2,1)S(1)} %add_convert_fusion.6), channel_id=1, source_target_pairs={{0,66},{2,64},{4,70},{6,68},{8,74},{10,72},{12,78},{14,76},{16,82}... | collective-permute-start | bytes 110600 | tf_op jit(solution)/shard_map/ppermute | solution.py:37
  149.9 7.1 %collective-permute-start.28 = (bf16[24,768]{1,0:T(8,128)(2,1)S(1)}, bf16[24,768]{1,0:T(8,128)(2,1)S(1)}, u32[]{:S(2)}, u32[]{:S(2)}) collective-permute-start(bf16[24,768]{1,0:T(8,128)(2,1)S(1)} %add_convert_fusion.6), channel_id=1, source_target_pairs={{0,64},{2,66},{4,68},{6,70},{8,72},{10,74},{12,76},{14,78},{16,80}... | collective-permute-start | bytes 110600 | tf_op jit(solution)/shard_map/ppermute | solution.py:37
  153.2 8.3 %collective-permute-start.29 = (bf16[24,768]{1,0:T(8,128)(2,1)S(1)}, bf16[24,768]{1,0:T(8,128)(2,1)S(1)}, u32[]{:S(2)}, u32[]{:S(2)}) collective-permute-start(bf16[24,768]{1,0:T(8,128)(2,1)S(1)} %add_convert_fusion.6), channel_id=1, source_target_pairs={{0,2},{2,0},{4,6},{6,4},{8,10},{10,8},{12,14},{14,12},{16,18},{18,... | collective-permute-start | bytes 110600 | tf_op jit(solution)/shard_map/ppermute | solution.py:37
  154.5 38.5 %collective-permute-start.17 = (bf16[512,768]{1,0:T(8,128)(2,1)S(1)}, bf16[512,768]{1,0:T(8,128)(2,1)S(1)}, u32[]{:S(2)}, u32[]{:S(2)}) collective-permute-start(bf16[512,768]{1,0:T(8,128)(2,1)S(1)} %add_convert_fusion.1), channel_id=1, source_target_pairs={{0,16},{2,18},{4,20},{6,22},{8,24},{10,26},{12,28},{14,30},{16,32}... | collective-permute-start | bytes 2359304 | tf_op jit(solution)/shard_map/ppermute | solution.py:37
  162.0 5.9 %collective-permute-start.31 = (bf16[2,24,768]{2,1,0:T(8,128)(2,1)S(1)}, bf16[2,24,768]{2,1,0:T(8,128)(2,1)S(1)}, u32[]{:S(2)}, u32[]{:S(2)}) collective-permute-start(bf16[2,24,768]{2,1,0:T(8,128)(2,1)S(1)} %pad_maximum_fusion.2), channel_id=1, source_target_pairs={{0,8},{2,10},{4,12},{6,14},{8,0},{10,2},{12,4},{14,6},{16,24},{18,... | collective-permute-start | bytes 221192 | tf_op jit(solution)/shard_map/ppermute | solution.py:37
  169.0 25.2 %collective-permute-start.33 = (bf16[4,2,24,768]{3,2,1,0:T(8,128)(2,1)S(1)}, bf16[4,2,24,768]{3,2,1,0:T(8,128)(2,1)S(1)}, u32[]{:S(2)}, u32[]{:S(2)}) collective-permute-start(bf16[4,2,24,768]{3,2,1,0:T(8,128)(2,1)S(1)} %bitcast_dynamic-update-slice_fusion), channel_id=1, source_target_pairs={{0,128},{2,130},{4,132},{6,134},{8,136},{10,138},{12,140},{14,142}... | collective-permute-start | bytes 884744 | tf_op jit(solution)/shard_map/ppermute | solution.py:37
  194.3 11.7 %collective-permute-start.23 = (bf16[256,768]{1,0:T(8,128)(2,1)S(1)}, bf16[256,768]{1,0:T(8,128)(2,1)S(1)}, u32[]{:S(2)}, u32[]{:S(2)}) collective-permute-start(bf16[256,768]{1,0:T(8,128)(2,1)S(1)} %get-tuple-element.73), channel_id=1, source_target_pairs={{0,2},{2,0},{4,6},{6,4},{8,10},{10,8},{12,14},{14,12},{16,18},{18,... | collective-permute-start | bytes 1179656 | tf_op jit(solution)/shard_map/ppermute | solution.py:37
  (25 other events, 350.3 us)

commit v3 on v2

--- a/solution.py
+++ b/solution.py
@@ -146,11 +146,15 @@
     return op(values.reshape(values.shape[0] // 8, 8, values.shape[1]), axis=0)
 
 
-def attend_kernel(flag_ref, bias_ref, text_bias_ref, qg_ref, text_ref, *refs):
+def attend_kernel(flag_ref, bias_ref, text_bias_ref, keep_ref, got_ref, text_ref, *refs):
     kv_refs, far_refs, mid_refs = refs[:12], refs[12:14], refs[14:17]
     dq_refs, dtext_ref, side_refs = refs[17:19], refs[19], refs[20:22]
-    p_ref, dp_ref, high_ref, total_ref, delta_ref, dq_sum_ref = refs[22:]
+    qg_ref, p_ref, dp_ref, high_ref, total_ref, delta_ref, dq_sum_ref = refs[22:]
     head = pl.program_id(0)
+    mirrored = flag_ref[36] != 0
+    keep, got = keep_ref[...], got_ref[...]
+    qg_ref[:BLOCK, :] = jnp.where(mirrored, got, keep)
+    qg_ref[BLOCK:, :] = jnp.where(mirrored, keep, got)
 
     def visible(block):
         return flag_ref[head * 12 + block] != 0
@@ -250,7 +254,6 @@
         pl.when(visible(group[0]))(functools.partial(spread_all, group))
         pl.when(jnp.logical_not(visible(group[0])))(functools.partial(clear_all, group))
 
-    mirrored = flag_ref[36] != 0
     for ref, low, high in zip(dq_refs, (0, BLOCK), (BLOCK, 0)):
         sums = jnp.where(
             mirrored, dq_sum_ref[:, high : high + BLOCK], dq_sum_ref[:, low : low + BLOCK]
@@ -258,7 +261,7 @@
         ref[...] = sums.T.astype(jnp.bfloat16)
 
 
-def attend(flags, bias, text_bias, qg, text, blocks):
+def attend(flags, bias, text_bias, keep_qg, got_qg, text, blocks):
     pair = pl.BlockSpec((BLOCK, PAIR), lambda h, f: (0, h))
     text_pair = pl.BlockSpec((TEXT, PAIR), lambda h, f: (0, h))
     text_out = jax.ShapeDtypeStruct((TEXT, 2 * HALF), jnp.bfloat16)
@@ -278,7 +281,8 @@
             in_specs=[
                 pl.BlockSpec((1, 24, 2 * BLOCK), lambda h, f: (h, 0, 0)),
                 pl.BlockSpec((TEXT, HD), lambda h, f: (0, 0)),
-                pl.BlockSpec((2 * BLOCK, PAIR), lambda h, f: (0, h)),
+                pair,
+                pair,
                 text_pair,
             ]
             + [pair] * 12,
@@ -288,6 +292,7 @@
             + (text_pair,)
             + (pair,) * 2,
             scratch_shapes=[
+                pltpu.VMEM((2 * BLOCK, PAIR), jnp.bfloat16),
                 pltpu.VMEM((13 * BLOCK, 2 * BLOCK), jnp.float32),
                 pltpu.VMEM((13 * BLOCK, 2 * BLOCK), jnp.float32),
                 pltpu.VMEM((8 * 14, 2 * BLOCK), jnp.float32),
@@ -303,7 +308,7 @@
             transcendentals=512 * 2560 * HEADS,
         ),
         name="attend",
-    )(flags, bias, text_bias, qg, text, *blocks)
+    )(flags, bias, text_bias, keep_qg, got_qg, text, *blocks)
     return results[:2], results[2:5], results[5:7], results[7], results[8:]
 
 
@@ -341,7 +346,8 @@
 def halve_text(part, ha):
     upper = ha // RUN // 2
     other = lax.dynamic_slice_in_dim(part, (1 - upper) * (TEXT // 2), TEXT // 2, 0)
-    return lax.dynamic_slice_in_dim(part, upper * (TEXT // 2), TEXT // 2, 0), move(other, flip(2 * RUN, 0))
+    mine = lax.dynamic_slice_in_dim(part, upper * (TEXT // 2), TEXT // 2, 0)
+    return mine, move(other, flip(2 * RUN, 0))
 
 
 def sum_text(part, group, ha, wa, beyond):
@@ -351,7 +357,6 @@
         for d in (1, 2, 3)
     ]
     part = added(lax.dynamic_slice_in_dim(part, x * (TEXT // 8), TEXT // 8, 0), *pieces)
-    part, beyond[0], beyond[1] = lax.optimization_barrier((part, beyond[0], beyond[1]))
     near = [move(part, flip(d, 0)).astype(jnp.float32) for d in (1, 2, 3)]
     part = ((part.astype(jnp.float32) + near[0]) + (near[1] + near[2])).astype(jnp.bfloat16)
     mine = added(part, move(part, flip(RUN, 1)))
@@ -359,6 +364,7 @@
     both = jnp.stack(
         [jnp.where(group == 0, mine, theirs), jnp.where(group == 0, theirs, mine)], axis=0
     )
+    both, beyond[0], beyond[1] = lax.optimization_barrier((both, beyond[0], beyond[1]))
     quarter = jnp.zeros((4,) + both.shape, both.dtype)
     quarter = lax.dynamic_update_index_in_dim(quarter, both, x, 0)
     for d in (1, 2, 3):
@@ -402,10 +408,10 @@
         ],
         axis=2,
     ).reshape(TEXT, 2 * HALF)
-    send_qg, keep_qg, flags, bias, text_bias, text, _, _, _ = lax.optimization_barrier(
-        (send_qg, keep_qg, flags, bias, text_bias, text, earlier, later, beside)
-    )
-    qg = jnp.concatenate(placed(keep_qg, move(send_qg, across)), axis=0)
+    send_qg, keep_qg, flags, bias, text_bias, text, _, _ = lax.optimization_barrier(
+        (send_qg, keep_qg, flags, bias, text_bias, text, earlier[0], later[0])
+    )
+    got_qg = move(send_qg, across)
 
     blocks = []
     for left, right in (earlier, later):
@@ -413,7 +419,7 @@
     blocks[4:4] = [beside[0], *own, beside[1]]
 
     far, mids, (dq_own, dq_other), dtext, sides = attend(
-        flags, bias, text_bias, qg, text, blocks
+        flags, bias, text_bias, keep_qg, got_qg, text, blocks
     )
 
     to_left = move(far[1], cols_by(1))

time: 207 us -> 201 us (0.971); the launches traced: 209 us -> 199 us
  waiting for transfers between devices: 74.4 us -> 61 us
  starting transfers between devices: 94.8 us -> 101 us
    ppermute x34, waiting for transfers between devices: 74.4 us -> 61 us  [move(): return lax.ppermute(block, AXES, route)]
    ppermute x34, starting transfers between devices: 94.8 us -> 101 us  [move(): return lax.ppermute(block, AXES, route)]
where the time goes in v3:
time: 201 us; the launch traced here: 199 us
  starting transfers between devices  101 us (50%)
  waiting for transfers between devices  61 us (30%)
  Pallas kernels  21.9 us (11%)
  local copies, waits for them, and re-layouts  8.79 us (4%)
  other arithmetic  4.55 us (2%)
    ppermute x34, starting transfers between devices, move(): return lax.ppermute(block, AXES, route)  101 us
    ppermute x34, waiting for transfers between devices, move(): return lax.ppermute(block, AXES, route)  61 us
    pallas_call x1, Pallas kernels, attend(): pl.pallas_call(attend_kernel, out_shape=(wide_out,) * 2 + (wide_out,) * 3...  13.7 us
    pallas_call x2, Pallas kernels, split_heads(): pl.pallas_call(split_kernel, out_shape=(out, out), grid_spec=pltpu.Prefet...  4.26 us
  transfers between devices with their start and end apart: 34, of which 16 were waited for; matrix products, arithmetic and copies ran while one was open for 6% of the time, Pallas kernels for 2%

profile of v3, /device:TPU:10, one launch (start us, length us, event | category | flops | bytes accessed | tf_op | source)
XLA Modules:
  0.0 198.6 jit_solution(11134988698755821833)
XLA Ops:
  0.7 2.1 %split_heads.3 = (bf16[256,768]{1,0:T(8,128)(2,1)}, bf16[256,768]{1,0:T(8,128)(2,1)}) custom-call(s32[1]{0:T(128)} %bitcast.group_ref, bf16[2,2,64,768]{3,2,1,0:T(8,128)(2,1)} %bitcast.33, bf16[2,2,64,768]{3,2,1,0:T(8,128)(2,1)} %bitcast.34), custom_call_target="tpu_custom_call" | custom-call | bytes 1600000 | tf_op jit(solution)/shard_map/split_heads/pallas_call | solution.py:79
  2.8 7.2 %collective-permute-start = (bf16[256,768]{1,0:T(8,128)(2,1)}, bf16[256,768]{1,0:T(8,128)(2,1)S(1)}, u32[]{:S(2)}, u32[]{:S(2)}) collective-permute-start(bf16[256,768]{1,0:T(8,128)(2,1)} %get-tuple-element.39), channel_id=1, source_target_pairs={{0,2},{2,0},{4,6},{6,4},{8,10},{10,8},{12,14},{14,12},{16,18},{18,... | collective-permute-start | bytes 1179656 | tf_op jit(solution)/shard_map/ppermute | solution.py:37
  10.7 9.8 %collective-permute-done = bf16[256,768]{1,0:T(8,128)(2,1)S(1)} collective-permute-done((bf16[256,768]{1,0:T(8,128)(2,1)}, bf16[256,768]{1,0:T(8,128)(2,1)S(1)}, u32[]{:S(2)}, u32[]{:S(2)}) %collective-permute-start) | collective-permute-done | bytes 393248 | tf_op jit(solution)/shard_map/ppermute | solution.py:37
  20.6 10.4 %collective-permute-start.1 = (bf16[256,768]{1,0:T(8,128)(2,1)S(1)}, bf16[256,768]{1,0:T(8,128)(2,1)S(1)}, u32[]{:S(2)}, u32[]{:S(2)}) collective-permute-start(bf16[256,768]{1,0:T(8,128)(2,1)S(1)} %get-tuple-element.80.refs_5_), channel_id=1, source_target_pairs={{0,16},{2,18},{4,20},{6,22},{8,24},{10,26},{12,28},{14,30},{16,32}... | collective-permute-start | bytes 1179656 | tf_op jit(solution)/shard_map/ppermute | solution.py:37
  33.5 6.0 %collective-permute-start.9 = (bf16[256,768]{1,0:T(8,128)(2,1)S(1)}, bf16[256,768]{1,0:T(8,128)(2,1)S(1)}, u32[]{:S(2)}, u32[]{:S(2)}) collective-permute-start(bf16[256,768]{1,0:T(8,128)(2,1)S(1)} %get-tuple-element.79.refs_6_), channel_id=1, source_target_pairs={{16,0},{18,2},{20,4},{22,6},{24,8},{26,10},{28,12},{30,14},{32,16}... | collective-permute-start | bytes 1179656 | tf_op jit(solution)/shard_map/ppermute | solution.py:37
  41.4 3.4 %collective-permute-start.7 = (bf16[256,768]{1,0:T(8,128)(2,1)S(1)}, bf16[256,768]{1,0:T(8,128)(2,1)S(1)}, u32[]{:S(2)}, u32[]{:S(2)}) collective-permute-start(bf16[256,768]{1,0:T(8,128)(2,1)S(1)} %get-tuple-element.79.refs_6_), channel_id=1, source_target_pairs={{0,4},{2,6},{4,8},{6,10},{8,12},{10,14},{16,20},{18,22},{20,24},{2... | collective-permute-start | bytes 1179656 | tf_op jit(solution)/shard_map/ppermute | solution.py:37
  44.8 2.5 %collective-permute-start.8 = (bf16[256,768]{1,0:T(8,128)(2,1)S(1)}, bf16[256,768]{1,0:T(8,128)(2,1)}, u32[]{:S(2)}, u32[]{:S(2)}) collective-permute-start(bf16[256,768]{1,0:T(8,128)(2,1)S(1)} %get-tuple-element.80.refs_5_), channel_id=1, source_target_pairs={{4,0},{6,2},{8,4},{10,6},{12,8},{14,10},{20,16},{22,18},{24,20},{2... | collective-permute-start | bytes 1179656 | tf_op jit(solution)/shard_map/ppermute | solution.py:37
  50.1 2.1 %split_heads.2 = (bf16[256,768]{1,0:T(8,128)(2,1)}, bf16[256,768]{1,0:T(8,128)(2,1)}) custom-call(s32[1]{0:T(128)} %bitcast.group_ref, bf16[2,2,64,768]{3,2,1,0:T(8,128)(2,1)} %bitcast.35, bf16[2,2,64,768]{3,2,1,0:T(8,128)(2,1)} %bitcast.36), custom_call_target="tpu_custom_call" | custom-call | bytes 1600000 | tf_op jit(solution)/shard_map/split_heads/pallas_call | solution.py:79
  53.6 6.0 %collective-permute-start.3 = (bf16[256,768]{1,0:T(8,128)(2,1)}, bf16[256,768]{1,0:T(8,128)(2,1)S(1)}, u32[]{:S(2)}, u32[]{:S(2)}) collective-permute-start(bf16[256,768]{1,0:T(8,128)(2,1)} %get-tuple-element.44), channel_id=1, source_target_pairs={{0,2},{2,0},{4,6},{6,4},{8,10},{10,8},{12,14},{14,12},{16,18},{18,... | collective-permute-start | bytes 1179656 | tf_op jit(solution)/shard_map/ppermute | solution.py:37
  61.6 3.9 %collective-permute-start.10 = (bf16[256,768]{1,0:T(8,128)(2,1)S(1)}, bf16[256,768]{1,0:T(8,128)(2,1)S(1)}, u32[]{:S(2)}, u32[]{:S(2)}) collective-permute-start(bf16[256,768]{1,0:T(8,128)(2,1)S(1)} %collective-permute-done.9.refs_10_), channel_id=1, source_target_pairs={{0,4},{2,6},{4,8},{6,10},{8,12},{10,14},{16,20},{18,22},{20,24},{2... | collective-permute-start | bytes 1179656 | tf_op jit(solution)/shard_map/ppermute | solution.py:37
  65.5 3.4 %collective-permute-start.5 = (bf16[256,768]{1,0:T(8,128)(2,1)S(1)}, bf16[256,768]{1,0:T(8,128)(2,1)S(1)}, u32[]{:S(2)}, u32[]{:S(2)}) collective-permute-start(bf16[256,768]{1,0:T(8,128)(2,1)S(1)} %collective-permute-done.4.refs_2_), channel_id=1, source_target_pairs={{0,4},{2,6},{4,8},{6,10},{8,12},{10,14},{16,20},{18,22},{20,24},{2... | collective-permute-start | bytes 1179656 | tf_op jit(solution)/shard_map/ppermute | solution.py:37
  68.9 2.5 %collective-permute-start.6 = (bf16[256,768]{1,0:T(8,128)(2,1)S(1)}, bf16[256,768]{1,0:T(8,128)(2,1)S(1)}, u32[]{:S(2)}, u32[]{:S(2)}) collective-permute-start(bf16[256,768]{1,0:T(8,128)(2,1)S(1)} %collective-permute-done.1.refs_1_), channel_id=1, source_target_pairs={{4,0},{6,2},{8,4},{10,6},{12,8},{14,10},{20,16},{22,18},{24,20},{2... | collective-permute-start | bytes 1179656 | tf_op jit(solution)/shard_map/ppermute | solution.py:37
  71.4 2.2 %collective-permute-done.3.got_ref = bf16[256,768]{1,0:T(8,128)(2,1)S(1)} collective-permute-done((bf16[256,768]{1,0:T(8,128)(2,1)}, bf16[256,768]{1,0:T(8,128)(2,1)S(1)}, u32[]{:S(2)}, u32[]{:S(2)}) %collective-permute-start.3) | collective-permute-done | bytes 393248 | tf_op jit(solution)/shard_map/ppermute | solution.py:37
  73.6 4.1 %collective-permute-done.5.refs_0_ = bf16[256,768]{1,0:T(8,128)(2,1)S(1)} collective-permute-done((bf16[256,768]{1,0:T(8,128)(2,1)S(1)}, bf16[256,768]{1,0:T(8,128)(2,1)S(1)}, u32[]{:S(2)}, u32[]{:S(2)}) %collective-permute-start.5) | collective-permute-done | bytes 393248 | tf_op jit(solution)/shard_map/ppermute | solution.py:37
  79.4 13.7 %attend.1 = (bf16[512,768]{1,0:T(8,128)(2,1)}, bf16[512,768]{1,0:T(8,128)(2,1)}, bf16[512,768]{1,0:T(8,128)(2,1)}, bf16[512,768]{1,0:T(8,128)(2,1)}, bf16[512,76...) custom-call(s32[37]{0:T(128)} %pad_add_fusion.flag_ref, ...), custom_call_target="tpu_custom_call" | custom-call | flops 5033164800 | bytes 12000000 | tf_op jit(solution)/shard_map/attend/pallas_call | solution.py:271
  93.2 3.5 %collective-permute-start.13 = (bf16[512,768]{1,0:T(8,128)(2,1)}, bf16[512,768]{1,0:T(8,128)(2,1)S(1)}, u32[]{:S(2)}, u32[]{:S(2)}) collective-permute-start(bf16[512,768]{1,0:T(8,128)(2,1)} %get-tuple-element.50), channel_id=1, source_target_pairs={{0,4},{2,6},{4,8},{6,10},{8,12},{10,14},{16,20},{18,22},{20,24},{2... | collective-permute-start | bytes 2359304 | tf_op jit(solution)/shard_map/ppermute | solution.py:37
  96.6 2.4 %collective-permute-start.14 = (bf16[512,768]{1,0:T(8,128)(2,1)}, bf16[512,768]{1,0:T(8,128)(2,1)S(1)}, u32[]{:S(2)}, u32[]{:S(2)}) collective-permute-start(bf16[512,768]{1,0:T(8,128)(2,1)} %get-tuple-element.51), channel_id=1, source_target_pairs={{4,0},{6,2},{8,4},{10,6},{12,8},{14,10},{20,16},{22,18},{24,20},{2... | collective-permute-start | bytes 2359304 | tf_op jit(solution)/shard_map/ppermute | solution.py:37
  99.1 6.3 %collective-permute-start.12 = (bf16[256,384]{1,0:T(8,128)(2,1)}, bf16[256,384]{1,0:T(8,128)(2,1)S(1)}, u32[]{:S(2)}, u32[]{:S(2)}) collective-permute-start(bf16[256,384]{1,0:T(8,128)(2,1)} %get-tuple-element.47), channel_id=1, source_target_pairs={{0,2},{2,0},{4,6},{6,4},{8,10},{10,8},{12,14},{14,12},{16,18},{18,... | collective-permute-start | bytes 589832 | tf_op jit(solution)/shard_map/ppermute | solution.py:37
  106.4 2.7 %collective-permute-start.15 = (bf16[96,768]{1,0:T(8,128)(2,1)S(1)}, bf16[96,768]{1,0:T(8,128)(2,1)S(1)}, u32[]{:S(2)}, u32[]{:S(2)}) collective-permute-start(bf16[96,768]{1,0:T(8,128)(2,1)S(1)} %get-tuple-element.85), channel_id=1, source_target_pairs={{0,128},{2,130},{4,132},{6,134},{8,136},{10,138},{12,140},{14,142}... | collective-permute-start | bytes 442376 | tf_op jit(solution)/shard_map/ppermute | solution.py:37
  113.5 3.6 %collective-permute-done.14 = bf16[512,768]{1,0:T(8,128)(2,1)S(1)} collective-permute-done((bf16[512,768]{1,0:T(8,128)(2,1)}, bf16[512,768]{1,0:T(8,128)(2,1)S(1)}, u32[]{:S(2)}, u32[]{:S(2)}) %collective-permute-start.14) | collective-permute-done | bytes 786464 | tf_op jit(solution)/shard_map/ppermute | solution.py:37
  121.0 2.2 %collective-permute-start.27 = (bf16[256,768]{1,0:T(8,128)(2,1)S(1)}, bf16[256,768]{1,0:T(8,128)(2,1)S(1)}, u32[]{:S(2)}, u32[]{:S(2)}) collective-permute-start(bf16[256,768]{1,0:T(8,128)(2,1)S(1)} %copy-done.11), channel_id=1, source_target_pairs={{0,4},{2,6},{4,8},{6,10},{8,12},{10,14},{16,20},{18,22},{20,24},{2... | collective-permute-start | bytes 1179656 | tf_op jit(solution)/shard_map/ppermute | solution.py:37
  123.2 3.7 %collective-permute-start.28 = (bf16[256,768]{1,0:T(8,128)(2,1)S(1)}, bf16[256,768]{1,0:T(8,128)(2,1)S(1)}, u32[]{:S(2)}, u32[]{:S(2)}) collective-permute-start(bf16[256,768]{1,0:T(8,128)(2,1)S(1)} %copy-done.10), channel_id=1, source_target_pairs={{4,0},{6,2},{8,4},{10,6},{12,8},{14,10},{20,16},{22,18},{24,20},{2... | collective-permute-start | bytes 1179656 | tf_op jit(solution)/shard_map/ppermute | solution.py:37
  128.8 3.7 %collective-permute-start.22 = (bf16[24,768]{1,0:T(8,128)(2,1)S(1)}, bf16[24,768]{1,0:T(8,128)(2,1)S(1)}, u32[]{:S(2)}, u32[]{:S(2)}) collective-permute-start(bf16[24,768]{1,0:T(8,128)(2,1)S(1)} %add_convert_fusion.7), channel_id=1, source_target_pairs={{0,32},{2,34},{4,36},{6,38},{8,40},{10,42},{12,44},{14,46},{16,48}... | collective-permute-start | bytes 110600 | tf_op jit(solution)/shard_map/ppermute | solution.py:37
  132.8 2.3 %collective-permute-done.22 = bf16[24,768]{1,0:T(8,128)(2,1)S(1)} collective-permute-done((bf16[24,768]{1,0:T(8,128)(2,1)S(1)}, bf16[24,768]{1,0:T(8,128)(2,1)S(1)}, u32[]{:S(2)}, u32[]{:S(2)}) %collective-permute-start.22) | collective-permute-done | bytes 36896 | tf_op jit(solution)/shard_map/ppermute | solution.py:37
  135.1 3.2 %collective-permute-done.23 = bf16[24,768]{1,0:T(8,128)(2,1)S(1)} collective-permute-done((bf16[24,768]{1,0:T(8,128)(2,1)S(1)}, bf16[24,768]{1,0:T(8,128)(2,1)S(1)}, u32[]{:S(2)}, u32[]{:S(2)}) %collective-permute-start.23) | collective-permute-done | bytes 36896 | tf_op jit(solution)/shard_map/ppermute | solution.py:37
  139.6 6.2 %collective-permute-start.26 = (bf16[24,768]{1,0:T(8,128)(2,1)S(1)}, bf16[24,768]{1,0:T(8,128)(2,1)S(1)}, u32[]{:S(2)}, u32[]{:S(2)}) collective-permute-start(bf16[24,768]{1,0:T(8,128)(2,1)S(1)} %add_convert_fusion.6), channel_id=1, source_target_pairs={{0,2},{2,0},{4,6},{6,4},{8,10},{10,8},{12,14},{14,12},{16,18},{18,... | collective-permute-start | bytes 110600 | tf_op jit(solution)/shard_map/ppermute | solution.py:37
  149.1 3.9 %collective-permute-start.17 = (bf16[512,768]{1,0:T(8,128)(2,1)S(1)}, bf16[512,768]{1,0:T(8,128)(2,1)S(1)}, u32[]{:S(2)}, u32[]{:S(2)}) collective-permute-start(bf16[512,768]{1,0:T(8,128)(2,1)S(1)} %add_convert_fusion.1), channel_id=1, source_target_pairs={{0,16},{2,18},{4,20},{6,22},{8,24},{10,26},{12,28},{14,30},{16,32}... | collective-permute-start | bytes 2359304 | tf_op jit(solution)/shard_map/ppermute | solution.py:37
  160.0 3.9 %collective-permute-done.16 = bf16[512,768]{1,0:T(8,128)(2,1)S(1)} collective-permute-done((bf16[512,768]{1,0:T(8,128)(2,1)S(1)}, bf16[512,768]{1,0:T(8,128)(2,1)S(1)}, u32[]{:S(2)}, u32[]{:S(2)}) %collective-permute-start.16) | collective-permute-done | bytes 786464 | tf_op jit(solution)/shard_map/ppermute | solution.py:37
  163.9 18.9 %collective-permute-done.17 = bf16[512,768]{1,0:T(8,128)(2,1)S(1)} collective-permute-done((bf16[512,768]{1,0:T(8,128)(2,1)S(1)}, bf16[512,768]{1,0:T(8,128)(2,1)S(1)}, u32[]{:S(2)}, u32[]{:S(2)}) %collective-permute-start.17) | collective-permute-done | bytes 786464 | tf_op jit(solution)/shard_map/ppermute | solution.py:37
  184.1 3.1 %collective-permute-start.29 = (bf16[256,768]{1,0:T(8,128)(2,1)S(1)}, bf16[256,768]{1,0:T(8,128)(2,1)S(1)}, u32[]{:S(2)}, u32[]{:S(2)}) collective-permute-start(bf16[256,768]{1,0:T(8,128)(2,1)S(1)} %get-tuple-element.73), channel_id=1, source_target_pairs={{0,2},{2,0},{4,6},{6,4},{8,10},{10,8},{12,14},{14,12},{16,18},{18,... | collective-permute-start | bytes 1179656 | tf_op jit(solution)/shard_map/ppermute | solution.py:37
  190.0 5.8 %collective-permute-done.29.got_ref = bf16[256,768]{1,0:T(8,128)(2,1)S(1)} collective-permute-done((bf16[256,768]{1,0:T(8,128)(2,1)S(1)}, bf16[256,768]{1,0:T(8,128)(2,1)S(1)}, u32[]{:S(2)}, u32[]{:S(2)}) %collective-permute-start.29) | collective-permute-done | bytes 393248 | tf_op jit(solution)/shard_map/ppermute | solution.py:37
  196.5 2.1 %join_heads.3 = (bf16[2,2,64,768]{3,2,1,0:T(8,128)(2,1)}, bf16[2,2,64,768]{3,2,1,0:T(8,128)(2,1)}) custom-call(s32[1]{0:T(128)} %bitcast.group_ref, bf16[256,768]{1,0:T(8,128)(2,1)} %get-tuple-element.74.keep_ref, bf16[256,768]{1,0:T(8,128)(2,1)} %copy-done.7), custom_call_target="tpu_custom_call" | custom-call | bytes 1600000 | tf_op jit(solution)/shard_map/join_heads/pallas_call | solution.py:112
  (144 shorter events, 40.5 us)
Async XLA Ops:
  2.8 17.6 %collective-permute-start = (bf16[256,768]{1,0:T(8,128)(2,1)}, bf16[256,768]{1,0:T(8,128)(2,1)S(1)}, u32[]{:S(2)}, u32[]{:S(2)}) collective-permute-start(bf16[256,768]{1,0:T(8,128)(2,1)} %get-tuple-element.39), channel_id=1, source_target_pairs={{0,2},{2,0},{4,6},{6,4},{8,10},{10,8},{12,14},{14,12},{16,18},{18,... | collective-permute-start | bytes 1179656 | tf_op jit(solution)/shard_map/ppermute | solution.py:37
  20.6 24.2 %collective-permute-start.1 = (bf16[256,768]{1,0:T(8,128)(2,1)S(1)}, bf16[256,768]{1,0:T(8,128)(2,1)S(1)}, u32[]{:S(2)}, u32[]{:S(2)}) collective-permute-start(bf16[256,768]{1,0:T(8,128)(2,1)S(1)} %get-tuple-element.80.refs_5_), channel_id=1, source_target_pairs={{0,16},{2,18},{4,20},{6,22},{8,24},{10,26},{12,28},{14,30},{16,32}... | collective-permute-start | bytes 1179656 | tf_op jit(solution)/shard_map/ppermute | solution.py:37
  31.5 21.3 %collective-permute-start.2 = (bf16[256,768]{1,0:T(8,128)(2,1)S(1)}, bf16[256,768]{1,0:T(8,128)(2,1)S(1)}, u32[]{:S(2)}, u32[]{:S(2)}) collective-permute-start(bf16[256,768]{1,0:T(8,128)(2,1)S(1)} %get-tuple-element.80.refs_5_), channel_id=1, source_target_pairs={{16,0},{18,2},{20,4},{22,6},{24,8},{26,10},{28,12},{30,14},{32,16}... | collective-permute-start | bytes 1179656 | tf_op jit(solution)/shard_map/ppermute | solution.py:37
  33.5 26.1 %collective-permute-start.9 = (bf16[256,768]{1,0:T(8,128)(2,1)S(1)}, bf16[256,768]{1,0:T(8,128)(2,1)S(1)}, u32[]{:S(2)}, u32[]{:S(2)}) collective-permute-start(bf16[256,768]{1,0:T(8,128)(2,1)S(1)} %get-tuple-element.79.refs_6_), channel_id=1, source_target_pairs={{16,0},{18,2},{20,4},{22,6},{24,8},{26,10},{28,12},{30,14},{32,16}... | collective-permute-start | bytes 1179656 | tf_op jit(solution)/shard_map/ppermute | solution.py:37
  39.4 22.1 %collective-permute-start.4 = (bf16[256,768]{1,0:T(8,128)(2,1)S(1)}, bf16[256,768]{1,0:T(8,128)(2,1)S(1)}, u32[]{:S(2)}, u32[]{:S(2)}) collective-permute-start(bf16[256,768]{1,0:T(8,128)(2,1)S(1)} %get-tuple-element.79.refs_6_), channel_id=1, source_target_pairs={{0,16},{2,18},{4,20},{6,22},{8,24},{10,26},{12,28},{14,30},{16,32}... | collective-permute-start | bytes 1179656 | tf_op jit(solution)/shard_map/ppermute | solution.py:37
  41.4 24.1 %collective-permute-start.7 = (bf16[256,768]{1,0:T(8,128)(2,1)S(1)}, bf16[256,768]{1,0:T(8,128)(2,1)S(1)}, u32[]{:S(2)}, u32[]{:S(2)}) collective-permute-start(bf16[256,768]{1,0:T(8,128)(2,1)S(1)} %get-tuple-element.79.refs_6_), channel_id=1, source_target_pairs={{0,4},{2,6},{4,8},{6,10},{8,12},{10,14},{16,20},{18,22},{20,24},{2... | collective-permute-start | bytes 1179656 | tf_op jit(solution)/shard_map/ppermute | solution.py:37
  44.8 24.1 %collective-permute-start.8 = (bf16[256,768]{1,0:T(8,128)(2,1)S(1)}, bf16[256,768]{1,0:T(8,128)(2,1)}, u32[]{:S(2)}, u32[]{:S(2)}) collective-permute-start(bf16[256,768]{1,0:T(8,128)(2,1)S(1)} %get-tuple-element.80.refs_5_), channel_id=1, source_target_pairs={{4,0},{6,2},{8,4},{10,6},{12,8},{14,10},{20,16},{22,18},{24,20},{2... | collective-permute-start | bytes 1179656 | tf_op jit(solution)/shard_map/ppermute | solution.py:37
  53.6 20.0 %collective-permute-start.3 = (bf16[256,768]{1,0:T(8,128)(2,1)}, bf16[256,768]{1,0:T(8,128)(2,1)S(1)}, u32[]{:S(2)}, u32[]{:S(2)}) collective-permute-start(bf16[256,768]{1,0:T(8,128)(2,1)} %get-tuple-element.44), channel_id=1, source_target_pairs={{0,2},{2,0},{4,6},{6,4},{8,10},{10,8},{12,14},{14,12},{16,18},{18,... | collective-permute-start | bytes 1179656 | tf_op jit(solution)/shard_map/ppermute | solution.py:37
  59.6 14.0 %collective-permute-start.11 = (bf16[256,768]{1,0:T(8,128)(2,1)S(1)}, bf16[256,768]{1,0:T(8,128)(2,1)S(1)}, u32[]{:S(2)}, u32[]{:S(2)}) collective-permute-start(bf16[256,768]{1,0:T(8,128)(2,1)S(1)} %collective-permute-done.2.refs_9_), channel_id=1, source_target_pairs={{4,0},{6,2},{8,4},{10,6},{12,8},{14,10},{20,16},{22,18},{24,20},{2... | collective-permute-start | bytes 1179656 | tf_op jit(solution)/shard_map/ppermute | solution.py:37
  61.6 12.0 %collective-permute-start.10 = (bf16[256,768]{1,0:T(8,128)(2,1)S(1)}, bf16[256,768]{1,0:T(8,128)(2,1)S(1)}, u32[]{:S(2)}, u32[]{:S(2)}) collective-permute-start(bf16[256,768]{1,0:T(8,128)(2,1)S(1)} %collective-permute-done.9.refs_10_), channel_id=1, source_target_pairs={{0,4},{2,6},{4,8},{6,10},{8,12},{10,14},{16,20},{18,22},{20,24},{2... | collective-permute-start | bytes 1179656 | tf_op jit(solution)/shard_map/ppermute | solution.py:37
  65.5 12.2 %collective-permute-start.5 = (bf16[256,768]{1,0:T(8,128)(2,1)S(1)}, bf16[256,768]{1,0:T(8,128)(2,1)S(1)}, u32[]{:S(2)}, u32[]{:S(2)}) collective-permute-start(bf16[256,768]{1,0:T(8,128)(2,1)S(1)} %collective-permute-done.4.refs_2_), channel_id=1, source_target_pairs={{0,4},{2,6},{4,8},{6,10},{8,12},{10,14},{16,20},{18,22},{20,24},{2... | collective-permute-start | bytes 1179656 | tf_op jit(solution)/shard_map/ppermute | solution.py:37
  68.9 9.7 %collective-permute-start.6 = (bf16[256,768]{1,0:T(8,128)(2,1)S(1)}, bf16[256,768]{1,0:T(8,128)(2,1)S(1)}, u32[]{:S(2)}, u32[]{:S(2)}) collective-permute-start(bf16[256,768]{1,0:T(8,128)(2,1)S(1)} %collective-permute-done.1.refs_1_), channel_id=1, source_target_pairs={{4,0},{6,2},{8,4},{10,6},{12,8},{14,10},{20,16},{22,18},{24,20},{2... | collective-permute-start | bytes 1179656 | tf_op jit(solution)/shard_map/ppermute | solution.py:37
  93.2 20.4 %collective-permute-start.13 = (bf16[512,768]{1,0:T(8,128)(2,1)}, bf16[512,768]{1,0:T(8,128)(2,1)S(1)}, u32[]{:S(2)}, u32[]{:S(2)}) collective-permute-start(bf16[512,768]{1,0:T(8,128)(2,1)} %get-tuple-element.50), channel_id=1, source_target_pairs={{0,4},{2,6},{4,8},{6,10},{8,12},{10,14},{16,20},{18,22},{20,24},{2... | collective-permute-start | bytes 2359304 | tf_op jit(solution)/shard_map/ppermute | solution.py:37
  96.6 20.5 %collective-permute-start.14 = (bf16[512,768]{1,0:T(8,128)(2,1)}, bf16[512,768]{1,0:T(8,128)(2,1)S(1)}, u32[]{:S(2)}, u32[]{:S(2)}) collective-permute-start(bf16[512,768]{1,0:T(8,128)(2,1)} %get-tuple-element.51), channel_id=1, source_target_pairs={{4,0},{6,2},{8,4},{10,6},{12,8},{14,10},{20,16},{22,18},{24,20},{2... | collective-permute-start | bytes 2359304 | tf_op jit(solution)/shard_map/ppermute | solution.py:37
  99.1 11.7 %collective-permute-start.12 = (bf16[256,384]{1,0:T(8,128)(2,1)}, bf16[256,384]{1,0:T(8,128)(2,1)S(1)}, u32[]{:S(2)}, u32[]{:S(2)}) collective-permute-start(bf16[256,384]{1,0:T(8,128)(2,1)} %get-tuple-element.47), channel_id=1, source_target_pairs={{0,2},{2,0},{4,6},{6,4},{8,10},{10,8},{12,14},{14,12},{16,18},{18,... | collective-permute-start | bytes 589832 | tf_op jit(solution)/shard_map/ppermute | solution.py:37
  106.4 6.8 %collective-permute-start.15 = (bf16[96,768]{1,0:T(8,128)(2,1)S(1)}, bf16[96,768]{1,0:T(8,128)(2,1)S(1)}, u32[]{:S(2)}, u32[]{:S(2)}) collective-permute-start(bf16[96,768]{1,0:T(8,128)(2,1)S(1)} %get-tuple-element.85), channel_id=1, source_target_pairs={{0,128},{2,130},{4,132},{6,134},{8,136},{10,138},{12,140},{14,142}... | collective-permute-start | bytes 442376 | tf_op jit(solution)/shard_map/ppermute | solution.py:37
  117.2 9.8 %collective-permute-start.18 = (bf16[24,768]{1,0:T(8,128)(2,1)S(1)}, bf16[24,768]{1,0:T(8,128)(2,1)S(1)}, u32[]{:S(2)}, u32[]{:S(2)}) collective-permute-start(bf16[24,768]{1,0:T(8,128)(2,1)S(1)} %get-tuple-element.89), channel_id=1, source_target_pairs={{0,4},{2,6},{4,0},{6,2},{8,12},{10,14},{12,8},{14,10},{16,20},{18,... | collective-permute-start | bytes 110600 | tf_op jit(solution)/shard_map/ppermute | solution.py:37
  117.8 9.2 %collective-permute-start.19 = (bf16[24,768]{1,0:T(8,128)(2,1)S(1)}, bf16[24,768]{1,0:T(8,128)(2,1)S(1)}, u32[]{:S(2)}, u32[]{:S(2)}) collective-permute-start(bf16[24,768]{1,0:T(8,128)(2,1)S(1)} %get-tuple-element.91), channel_id=1, source_target_pairs={{0,8},{2,10},{4,12},{6,14},{8,0},{10,2},{12,4},{14,6},{16,24},{18,... | collective-permute-start | bytes 110600 | tf_op jit(solution)/shard_map/ppermute | solution.py:37
  119.2 7.8 %collective-permute-start.20 = (bf16[24,768]{1,0:T(8,128)(2,1)S(1)}, bf16[24,768]{1,0:T(8,128)(2,1)S(1)}, u32[]{:S(2)}, u32[]{:S(2)}) collective-permute-start(bf16[24,768]{1,0:T(8,128)(2,1)S(1)} %get-tuple-element.90), channel_id=1, source_target_pairs={{0,12},{2,14},{4,8},{6,10},{8,4},{10,6},{12,0},{14,2},{16,28},{18,... | collective-permute-start | bytes 110600 | tf_op jit(solution)/shard_map/ppermute | solution.py:37
  121.0 32.1 %collective-permute-start.27 = (bf16[256,768]{1,0:T(8,128)(2,1)S(1)}, bf16[256,768]{1,0:T(8,128)(2,1)S(1)}, u32[]{:S(2)}, u32[]{:S(2)}) collective-permute-start(bf16[256,768]{1,0:T(8,128)(2,1)S(1)} %copy-done.11), channel_id=1, source_target_pairs={{0,4},{2,6},{4,8},{6,10},{8,12},{10,14},{16,20},{18,22},{20,24},{2... | collective-permute-start | bytes 1179656 | tf_op jit(solution)/shard_map/ppermute | solution.py:37
  123.2 29.9 %collective-permute-start.28 = (bf16[256,768]{1,0:T(8,128)(2,1)S(1)}, bf16[256,768]{1,0:T(8,128)(2,1)S(1)}, u32[]{:S(2)}, u32[]{:S(2)}) collective-permute-start(bf16[256,768]{1,0:T(8,128)(2,1)S(1)} %copy-done.10), channel_id=1, source_target_pairs={{4,0},{6,2},{8,4},{10,6},{12,8},{14,10},{20,16},{22,18},{24,20},{2... | collective-permute-start | bytes 1179656 | tf_op jit(solution)/shard_map/ppermute | solution.py:37
  127.0 5.7 %collective-permute-start.21 = (bf16[24,768]{1,0:T(8,128)(2,1)S(1)}, bf16[24,768]{1,0:T(8,128)(2,1)S(1)}, u32[]{:S(2)}, u32[]{:S(2)}) collective-permute-start(bf16[24,768]{1,0:T(8,128)(2,1)S(1)} %add_convert_fusion.7), channel_id=1, source_target_pairs={{0,16},{2,18},{4,20},{6,22},{8,24},{10,26},{12,28},{14,30},{16,0},... | collective-permute-start | bytes 110600 | tf_op jit(solution)/shard_map/ppermute | solution.py:37
  128.8 6.3 %collective-permute-start.22 = (bf16[24,768]{1,0:T(8,128)(2,1)S(1)}, bf16[24,768]{1,0:T(8,128)(2,1)S(1)}, u32[]{:S(2)}, u32[]{:S(2)}) collective-permute-start(bf16[24,768]{1,0:T(8,128)(2,1)S(1)} %add_convert_fusion.7), channel_id=1, source_target_pairs={{0,32},{2,34},{4,36},{6,38},{8,40},{10,42},{12,44},{14,46},{16,48}... | collective-permute-start | bytes 110600 | tf_op jit(solution)/shard_map/ppermute | solution.py:37
  132.5 5.8 %collective-permute-start.23 = (bf16[24,768]{1,0:T(8,128)(2,1)S(1)}, bf16[24,768]{1,0:T(8,128)(2,1)S(1)}, u32[]{:S(2)}, u32[]{:S(2)}) collective-permute-start(bf16[24,768]{1,0:T(8,128)(2,1)S(1)} %add_convert_fusion.7), channel_id=1, source_target_pairs={{0,48},{2,50},{4,52},{6,54},{8,56},{10,58},{12,60},{14,62},{16,32}... | collective-permute-start | bytes 110600 | tf_op jit(solution)/shard_map/ppermute | solution.py:37
  138.3 8.9 %collective-permute-start.24 = (bf16[24,768]{1,0:T(8,128)(2,1)S(1)}, bf16[24,768]{1,0:T(8,128)(2,1)S(1)}, u32[]{:S(2)}, u32[]{:S(2)}) collective-permute-start(bf16[24,768]{1,0:T(8,128)(2,1)S(1)} %add_convert_fusion.6), channel_id=1, source_target_pairs={{0,66},{2,64},{4,70},{6,68},{8,74},{10,72},{12,78},{14,76},{16,82}... | collective-permute-start | bytes 110600 | tf_op jit(solution)/shard_map/ppermute | solution.py:37
  139.5 9.6 %collective-permute-start.25 = (bf16[24,768]{1,0:T(8,128)(2,1)S(1)}, bf16[24,768]{1,0:T(8,128)(2,1)S(1)}, u32[]{:S(2)}, u32[]{:S(2)}) collective-permute-start(bf16[24,768]{1,0:T(8,128)(2,1)S(1)} %add_convert_fusion.6), channel_id=1, source_target_pairs={{0,64},{2,66},{4,68},{6,70},{8,72},{10,74},{12,76},{14,78},{16,80}... | collective-permute-start | bytes 110600 | tf_op jit(solution)/shard_map/ppermute | solution.py:37
  139.6 13.4 %collective-permute-start.26 = (bf16[24,768]{1,0:T(8,128)(2,1)S(1)}, bf16[24,768]{1,0:T(8,128)(2,1)S(1)}, u32[]{:S(2)}, u32[]{:S(2)}) collective-permute-start(bf16[24,768]{1,0:T(8,128)(2,1)S(1)} %add_convert_fusion.6), channel_id=1, source_target_pairs={{0,2},{2,0},{4,6},{6,4},{8,10},{10,8},{12,14},{14,12},{16,18},{18,... | collective-permute-start | bytes 110600 | tf_op jit(solution)/shard_map/ppermute | solution.py:37
  147.2 16.8 %collective-permute-start.16 = (bf16[512,768]{1,0:T(8,128)(2,1)S(1)}, bf16[512,768]{1,0:T(8,128)(2,1)S(1)}, u32[]{:S(2)}, u32[]{:S(2)}) collective-permute-start(bf16[512,768]{1,0:T(8,128)(2,1)S(1)} %add_convert_fusion.2), channel_id=1, source_target_pairs={{16,0},{18,2},{20,4},{22,6},{24,8},{26,10},{28,12},{30,14},{32,16}... | collective-permute-start | bytes 2359304 | tf_op jit(solution)/shard_map/ppermute | solution.py:37
  149.1 33.8 %collective-permute-start.17 = (bf16[512,768]{1,0:T(8,128)(2,1)S(1)}, bf16[512,768]{1,0:T(8,128)(2,1)S(1)}, u32[]{:S(2)}, u32[]{:S(2)}) collective-permute-start(bf16[512,768]{1,0:T(8,128)(2,1)S(1)} %add_convert_fusion.1), channel_id=1, source_target_pairs={{0,16},{2,18},{4,20},{6,22},{8,24},{10,26},{12,28},{14,30},{16,32}... | collective-permute-start | bytes 2359304 | tf_op jit(solution)/shard_map/ppermute | solution.py:37
  153.2 6.0 %collective-permute-start.31 = (bf16[2,24,768]{2,1,0:T(8,128)(2,1)S(1)}, bf16[2,24,768]{2,1,0:T(8,128)(2,1)S(1)}, u32[]{:S(2)}, u32[]{:S(2)}) collective-permute-start(bf16[2,24,768]{2,1,0:T(8,128)(2,1)S(1)} %pad_maximum_fusion.1), channel_id=1, source_target_pairs={{0,8},{2,10},{4,12},{6,14},{8,0},{10,2},{12,4},{14,6},{16,24},{18,... | collective-permute-start | bytes 221192 | tf_op jit(solution)/shard_map/ppermute | solution.py:37
  159.9 27.2 %collective-permute-start.33 = (bf16[4,2,24,768]{3,2,1,0:T(8,128)(2,1)S(1)}, bf16[4,2,24,768]{3,2,1,0:T(8,128)(2,1)S(1)}, u32[]{:S(2)}, u32[]{:S(2)}) collective-permute-start(bf16[4,2,24,768]{3,2,1,0:T(8,128)(2,1)S(1)} %bitcast_dynamic-update-slice_fusion), channel_id=1, source_target_pairs={{0,128},{2,130},{4,132},{6,134},{8,136},{10,138},{12,140},{14,142}... | collective-permute-start | bytes 884744 | tf_op jit(solution)/shard_map/ppermute | solution.py:37
  184.1 11.7 %collective-permute-start.29 = (bf16[256,768]{1,0:T(8,128)(2,1)S(1)}, bf16[256,768]{1,0:T(8,128)(2,1)S(1)}, u32[]{:S(2)}, u32[]{:S(2)}) collective-permute-start(bf16[256,768]{1,0:T(8,128)(2,1)S(1)} %get-tuple-element.73), channel_id=1, source_target_pairs={{0,2},{2,0},{4,6},{6,4},{8,10},{10,8},{12,14},{14,12},{16,18},{18,... | collective-permute-start | bytes 1179656 | tf_op jit(solution)/shard_map/ppermute | solution.py:37
  (26 other events, 309.9 us)

commit v4 on v3

--- a/solution.py
+++ b/solution.py
@@ -436,6 +436,7 @@
     beyond = [move(sides[1], cols_by(1)), move(sides[0], cols_by(-1))]
     text_key_grad, text_value_grad = sum_text(added(*dtext), group, ha, wa, beyond)
     totals = added(mids[1], outer[0], outer[1], jnp.concatenate(beyond, axis=0))
+    totals, dq_own, dq_got = lax.optimization_barrier((totals, dq_own, dq_got))
     (query_grad,) = join_heads(group_at, dq_own, dq_got, join_one_kernel, 1)
     keep = jnp.where(side == 0, totals[:BLOCK], totals[BLOCK:])
     send = jnp.where(side == 0, totals[BLOCK:], totals[:BLOCK])

time: 201 us -> 200 us (level)
  starting transfers between devices: 101 us -> 97.8 us
    ppermute x34, starting transfers between devices: 101 us -> 97.8 us  [move(): return lax.ppermute(block, AXES, route)]
where the time goes in v4:
time: 200 us; the launch traced here: 196 us
  starting transfers between devices  97.8 us (49%)
  waiting for transfers between devices  60.5 us (30%)
  Pallas kernels  23.5 us (12%)
  local copies, waits for them, and re-layouts  8.15 us (4%)
  other arithmetic  4.56 us (2%)
    ppermute x34, starting transfers between devices, move(): return lax.ppermute(block, AXES, route)  97.8 us
    ppermute x34, waiting for transfers between devices, move(): return lax.ppermute(block, AXES, route)  60.5 us
    pallas_call x1, Pallas kernels, attend(): pl.pallas_call(attend_kernel, out_shape=(wide_out,) * 2 + (wide_out,) * 3...  15.3 us
    pallas_call x2, Pallas kernels, split_heads(): pl.pallas_call(split_kernel, out_shape=(out, out), grid_spec=pltpu.Prefet...  4.26 us
  transfers between devices with their start and end apart: 34, of which 16 were waited for; matrix products, arithmetic and copies ran while one was open for 6% of the time, Pallas kernels for 2%

profile of v4, /device:TPU:10, one launch (start us, length us, event | category | flops | bytes accessed | tf_op | source)
XLA Modules:
  0.0 196.0 jit_solution(58928518094742142)
XLA Ops:
  2.8 7.2 %collective-permute-start = (bf16[256,768]{1,0:T(8,128)(2,1)}, bf16[256,768]{1,0:T(8,128)(2,1)S(1)}, u32[]{:S(2)}, u32[]{:S(2)}) collective-permute-start(bf16[256,768]{1,0:T(8,128)(2,1)} %get-tuple-element.42), channel_id=1, source_target_pairs={{0,2},{2,0},{4,6},{6,4},{8,10},{10,8},{12,14},{14,12},{16,18},{18,... | collective-permute-start | bytes 1179656 | tf_op jit(solution)/shard_map/ppermute | solution.py:37
  10.7 9.8 %collective-permute-done = bf16[256,768]{1,0:T(8,128)(2,1)S(1)} collective-permute-done((bf16[256,768]{1,0:T(8,128)(2,1)}, bf16[256,768]{1,0:T(8,128)(2,1)S(1)}, u32[]{:S(2)}, u32[]{:S(2)}) %collective-permute-start) | collective-permute-done | bytes 393248 | tf_op jit(solution)/shard_map/ppermute | solution.py:37
  20.6 10.4 %collective-permute-start.1 = (bf16[256,768]{1,0:T(8,128)(2,1)S(1)}, bf16[256,768]{1,0:T(8,128)(2,1)S(1)}, u32[]{:S(2)}, u32[]{:S(2)}) collective-permute-start(bf16[256,768]{1,0:T(8,128)(2,1)S(1)} %get-tuple-element.86.refs_5_), channel_id=1, source_target_pairs={{0,16},{2,18},{4,20},{6,22},{8,24},{10,26},{12,28},{14,30},{16,32}... | collective-permute-start | bytes 1179656 | tf_op jit(solution)/shard_map/ppermute | solution.py:37
  33.5 6.0 %collective-permute-start.9 = (bf16[256,768]{1,0:T(8,128)(2,1)S(1)}, bf16[256,768]{1,0:T(8,128)(2,1)S(1)}, u32[]{:S(2)}, u32[]{:S(2)}) collective-permute-start(bf16[256,768]{1,0:T(8,128)(2,1)S(1)} %get-tuple-element.85.refs_6_), channel_id=1, source_target_pairs={{16,0},{18,2},{20,4},{22,6},{24,8},{26,10},{28,12},{30,14},{32,16}... | collective-permute-start | bytes 1179656 | tf_op jit(solution)/shard_map/ppermute | solution.py:37
  41.4 3.4 %collective-permute-start.7 = (bf16[256,768]{1,0:T(8,128)(2,1)S(1)}, bf16[256,768]{1,0:T(8,128)(2,1)S(1)}, u32[]{:S(2)}, u32[]{:S(2)}) collective-permute-start(bf16[256,768]{1,0:T(8,128)(2,1)S(1)} %get-tuple-element.85.refs_6_), channel_id=1, source_target_pairs={{0,4},{2,6},{4,8},{6,10},{8,12},{10,14},{16,20},{18,22},{20,24},{2... | collective-permute-start | bytes 1179656 | tf_op jit(solution)/shard_map/ppermute | solution.py:37
  44.8 2.5 %collective-permute-start.8 = (bf16[256,768]{1,0:T(8,128)(2,1)S(1)}, bf16[256,768]{1,0:T(8,128)(2,1)}, u32[]{:S(2)}, u32[]{:S(2)}) collective-permute-start(bf16[256,768]{1,0:T(8,128)(2,1)S(1)} %get-tuple-element.86.refs_5_), channel_id=1, source_target_pairs={{4,0},{6,2},{8,4},{10,6},{12,8},{14,10},{20,16},{22,18},{24,20},{2... | collective-permute-start | bytes 1179656 | tf_op jit(solution)/shard_map/ppermute | solution.py:37
  53.7 6.0 %collective-permute-start.3 = (bf16[256,768]{1,0:T(8,128)(2,1)}, bf16[256,768]{1,0:T(8,128)(2,1)S(1)}, u32[]{:S(2)}, u32[]{:S(2)}) collective-permute-start(bf16[256,768]{1,0:T(8,128)(2,1)} %get-tuple-element.47), channel_id=1, source_target_pairs={{0,2},{2,0},{4,6},{6,4},{8,10},{10,8},{12,14},{14,12},{16,18},{18,... | collective-permute-start | bytes 1179656 | tf_op jit(solution)/shard_map/ppermute | solution.py:37
  61.6 3.9 %collective-permute-start.10 = (bf16[256,768]{1,0:T(8,128)(2,1)S(1)}, bf16[256,768]{1,0:T(8,128)(2,1)S(1)}, u32[]{:S(2)}, u32[]{:S(2)}) collective-permute-start(bf16[256,768]{1,0:T(8,128)(2,1)S(1)} %collective-permute-done.9.refs_10_), channel_id=1, source_target_pairs={{0,4},{2,6},{4,8},{6,10},{8,12},{10,14},{16,20},{18,22},{20,24},{2... | collective-permute-start | bytes 1179656 | tf_op jit(solution)/shard_map/ppermute | solution.py:37
  65.5 3.4 %collective-permute-start.5 = (bf16[256,768]{1,0:T(8,128)(2,1)S(1)}, bf16[256,768]{1,0:T(8,128)(2,1)S(1)}, u32[]{:S(2)}, u32[]{:S(2)}) collective-permute-start(bf16[256,768]{1,0:T(8,128)(2,1)S(1)} %collective-permute-done.4.refs_2_), channel_id=1, source_target_pairs={{0,4},{2,6},{4,8},{6,10},{8,12},{10,14},{16,20},{18,22},{20,24},{2... | collective-permute-start | bytes 1179656 | tf_op jit(solution)/shard_map/ppermute | solution.py:37
  69.0 2.5 %collective-permute-start.6 = (bf16[256,768]{1,0:T(8,128)(2,1)S(1)}, bf16[256,768]{1,0:T(8,128)(2,1)S(1)}, u32[]{:S(2)}, u32[]{:S(2)}) collective-permute-start(bf16[256,768]{1,0:T(8,128)(2,1)S(1)} %collective-permute-done.1.refs_1_), channel_id=1, source_target_pairs={{4,0},{6,2},{8,4},{10,6},{12,8},{14,10},{20,16},{22,18},{24,20},{2... | collective-permute-start | bytes 1179656 | tf_op jit(solution)/shard_map/ppermute | solution.py:37
  71.4 2.2 %collective-permute-done.3.got_ref = bf16[256,768]{1,0:T(8,128)(2,1)S(1)} collective-permute-done((bf16[256,768]{1,0:T(8,128)(2,1)}, bf16[256,768]{1,0:T(8,128)(2,1)S(1)}, u32[]{:S(2)}, u32[]{:S(2)}) %collective-permute-start.3) | collective-permute-done | bytes 393248 | tf_op jit(solution)/shard_map/ppermute | solution.py:37
  73.7 4.1 %collective-permute-done.5.refs_0_ = bf16[256,768]{1,0:T(8,128)(2,1)S(1)} collective-permute-done((bf16[256,768]{1,0:T(8,128)(2,1)S(1)}, bf16[256,768]{1,0:T(8,128)(2,1)S(1)}, u32[]{:S(2)}, u32[]{:S(2)}) %collective-permute-start.5) | collective-permute-done | bytes 393248 | tf_op jit(solution)/shard_map/ppermute | solution.py:37
  79.5 15.3 %attend.1 = (bf16[512,768]{1,0:T(8,128)(2,1)}, bf16[512,768]{1,0:T(8,128)(2,1)}, bf16[512,768]{1,0:T(8,128)(2,1)}, bf16[512,768]{1,0:T(8,128)(2,1)}, bf16[512,76...) custom-call(s32[37]{0:T(128)} %pad_add_fusion.flag_ref, ...), custom_call_target="tpu_custom_call" | custom-call | flops 5033164800 | bytes 12000000 | tf_op jit(solution)/shard_map/attend/pallas_call | solution.py:271
  94.8 3.6 %collective-permute-start.12 = (bf16[512,768]{1,0:T(8,128)(2,1)}, bf16[512,768]{1,0:T(8,128)(2,1)S(1)}, u32[]{:S(2)}, u32[]{:S(2)}) collective-permute-start(bf16[512,768]{1,0:T(8,128)(2,1)} %get-tuple-element.51), channel_id=1, source_target_pairs={{0,4},{2,6},{4,8},{6,10},{8,12},{10,14},{16,20},{18,22},{20,24},{2... | collective-permute-start | bytes 2359304 | tf_op jit(solution)/shard_map/ppermute | solution.py:37
  98.4 2.4 %collective-permute-start.13 = (bf16[512,768]{1,0:T(8,128)(2,1)}, bf16[512,768]{1,0:T(8,128)(2,1)S(1)}, u32[]{:S(2)}, u32[]{:S(2)}) collective-permute-start(bf16[512,768]{1,0:T(8,128)(2,1)} %get-tuple-element.52), channel_id=1, source_target_pairs={{4,0},{6,2},{8,4},{10,6},{12,8},{14,10},{20,16},{22,18},{24,20},{2... | collective-permute-start | bytes 2359304 | tf_op jit(solution)/shard_map/ppermute | solution.py:37
  101.9 2.4 %collective-permute-start.14 = (bf16[96,768]{1,0:T(8,128)(2,1)S(1)}, bf16[96,768]{1,0:T(8,128)(2,1)S(1)}, u32[]{:S(2)}, u32[]{:S(2)}) collective-permute-start(bf16[96,768]{1,0:T(8,128)(2,1)S(1)} %get-tuple-element.91), channel_id=1, source_target_pairs={{0,128},{2,130},{4,132},{6,134},{8,136},{10,138},{12,140},{14,142}... | collective-permute-start | bytes 442376 | tf_op jit(solution)/shard_map/ppermute | solution.py:37
  104.3 4.4 %collective-permute-done.14 = bf16[96,768]{1,0:T(8,128)(2,1)S(1)} collective-permute-done((bf16[96,768]{1,0:T(8,128)(2,1)S(1)}, bf16[96,768]{1,0:T(8,128)(2,1)S(1)}, u32[]{:S(2)}, u32[]{:S(2)}) %collective-permute-start.14) | collective-permute-done | bytes 147488 | tf_op jit(solution)/shard_map/ppermute | solution.py:37
  108.6 4.9 %collective-permute-done.12 = bf16[512,768]{1,0:T(8,128)(2,1)S(1)} collective-permute-done((bf16[512,768]{1,0:T(8,128)(2,1)}, bf16[512,768]{1,0:T(8,128)(2,1)S(1)}, u32[]{:S(2)}, u32[]{:S(2)}) %collective-permute-start.12) | collective-permute-done | bytes 786464 | tf_op jit(solution)/shard_map/ppermute | solution.py:37
  113.6 3.6 %collective-permute-done.13 = bf16[512,768]{1,0:T(8,128)(2,1)S(1)} collective-permute-done((bf16[512,768]{1,0:T(8,128)(2,1)}, bf16[512,768]{1,0:T(8,128)(2,1)S(1)}, u32[]{:S(2)}, u32[]{:S(2)}) %collective-permute-start.13) | collective-permute-done | bytes 786464 | tf_op jit(solution)/shard_map/ppermute | solution.py:37
  120.8 2.6 %collective-permute-start.26 = (bf16[256,768]{1,0:T(8,128)(2,1)S(1)}, bf16[256,768]{1,0:T(8,128)(2,1)S(1)}, u32[]{:S(2)}, u32[]{:S(2)}) collective-permute-start(bf16[256,768]{1,0:T(8,128)(2,1)S(1)} %copy-done.11), channel_id=1, source_target_pairs={{0,4},{2,6},{4,8},{6,10},{8,12},{10,14},{16,20},{18,22},{20,24},{2... | collective-permute-start | bytes 1179656 | tf_op jit(solution)/shard_map/ppermute | solution.py:37
  123.4 3.3 %collective-permute-start.27 = (bf16[256,768]{1,0:T(8,128)(2,1)S(1)}, bf16[256,768]{1,0:T(8,128)(2,1)S(1)}, u32[]{:S(2)}, u32[]{:S(2)}) collective-permute-start(bf16[256,768]{1,0:T(8,128)(2,1)S(1)} %copy-done.10), channel_id=1, source_target_pairs={{4,0},{6,2},{8,4},{10,6},{12,8},{14,10},{20,16},{22,18},{24,20},{2... | collective-permute-start | bytes 1179656 | tf_op jit(solution)/shard_map/ppermute | solution.py:37
  128.6 3.7 %collective-permute-start.21 = (bf16[24,768]{1,0:T(8,128)(2,1)S(1)}, bf16[24,768]{1,0:T(8,128)(2,1)S(1)}, u32[]{:S(2)}, u32[]{:S(2)}) collective-permute-start(bf16[24,768]{1,0:T(8,128)(2,1)S(1)} %add_convert_fusion.7), channel_id=1, source_target_pairs={{0,32},{2,34},{4,36},{6,38},{8,40},{10,42},{12,44},{14,46},{16,48}... | collective-permute-start | bytes 110600 | tf_op jit(solution)/shard_map/ppermute | solution.py:37
  134.5 3.6 %collective-permute-done.22 = bf16[24,768]{1,0:T(8,128)(2,1)S(1)} collective-permute-done((bf16[24,768]{1,0:T(8,128)(2,1)S(1)}, bf16[24,768]{1,0:T(8,128)(2,1)S(1)}, u32[]{:S(2)}, u32[]{:S(2)}) %collective-permute-start.22) | collective-permute-done | bytes 36896 | tf_op jit(solution)/shard_map/ppermute | solution.py:37
  139.8 5.8 %collective-permute-start.25 = (bf16[24,768]{1,0:T(8,128)(2,1)S(1)}, bf16[24,768]{1,0:T(8,128)(2,1)S(1)}, u32[]{:S(2)}, u32[]{:S(2)}) collective-permute-start(bf16[24,768]{1,0:T(8,128)(2,1)S(1)} %add_convert_fusion.6), channel_id=1, source_target_pairs={{0,2},{2,0},{4,6},{6,4},{8,10},{10,8},{12,14},{14,12},{16,18},{18,... | collective-permute-start | bytes 110600 | tf_op jit(solution)/shard_map/ppermute | solution.py:37
  147.5 3.5 %collective-permute-start.15 = (bf16[512,768]{1,0:T(8,128)(2,1)S(1)}, bf16[512,768]{1,0:T(8,128)(2,1)S(1)}, u32[]{:S(2)}, u32[]{:S(2)}) collective-permute-start(bf16[512,768]{1,0:T(8,128)(2,1)S(1)} %add_convert_fusion.2), channel_id=1, source_target_pairs={{16,0},{18,2},{20,4},{22,6},{24,8},{26,10},{28,12},{30,14},{32,16}... | collective-permute-start | bytes 2359304 | tf_op jit(solution)/shard_map/ppermute | solution.py:37
  151.0 2.4 %collective-permute-start.16 = (bf16[512,768]{1,0:T(8,128)(2,1)S(1)}, bf16[512,768]{1,0:T(8,128)(2,1)S(1)}, u32[]{:S(2)}, u32[]{:S(2)}) collective-permute-start(bf16[512,768]{1,0:T(8,128)(2,1)S(1)} %add_convert_fusion.1), channel_id=1, source_target_pairs={{0,16},{2,18},{4,20},{6,22},{8,24},{10,26},{12,28},{14,30},{16,32}... | collective-permute-start | bytes 2359304 | tf_op jit(solution)/shard_map/ppermute | solution.py:37
  155.3 2.5 %collective-permute-done.30 = bf16[2,24,768]{2,1,0:T(8,128)(2,1)S(1)} collective-permute-done((bf16[2,24,768]{2,1,0:T(8,128)(2,1)S(1)}, bf16[2,24,768]{2,1,0:T(8,128)(2,1)S(1)}, u32[]{:S(2)}, u32[]{:S(2)}) %collective-permute-start.30) | collective-permute-done | bytes 73760 | tf_op jit(solution)/shard_map/ppermute | solution.py:37
  159.5 2.7 %collective-permute-done.32 = bf16[2,24,768]{2,1,0:T(8,128)(2,1)S(1)} collective-permute-done((bf16[2,24,768]{2,1,0:T(8,128)(2,1)S(1)}, bf16[2,24,768]{2,1,0:T(8,128)(2,1)S(1)}, u32[]{:S(2)}, u32[]{:S(2)}) %collective-permute-start.32) | collective-permute-done | bytes 73760 | tf_op jit(solution)/shard_map/ppermute | solution.py:37
  162.2 4.0 %collective-permute-start.33 = (bf16[4,2,24,768]{3,2,1,0:T(8,128)(2,1)S(1)}, bf16[4,2,24,768]{3,2,1,0:T(8,128)(2,1)S(1)}, u32[]{:S(2)}, u32[]{:S(2)}) collective-permute-start(bf16[4,2,24,768]{3,2,1,0:T(8,128)(2,1)S(1)} %bitcast_dynamic-update-slice_fusion), channel_id=1, source_target_pairs={{0,128},{2,130},{4,132},{6,134},{8,136},{10,138},{12,140},{14,142}... | collective-permute-start | bytes 884744 | tf_op jit(solution)/shard_map/ppermute | solution.py:37
  166.2 4.0 %collective-permute-done.15 = bf16[512,768]{1,0:T(8,128)(2,1)S(1)} collective-permute-done((bf16[512,768]{1,0:T(8,128)(2,1)S(1)}, bf16[512,768]{1,0:T(8,128)(2,1)S(1)}, u32[]{:S(2)}, u32[]{:S(2)}) %collective-permute-start.15) | collective-permute-done | bytes 786464 | tf_op jit(solution)/shard_map/ppermute | solution.py:37
  173.4 4.1 %collective-permute-start.29 = (bf16[256,768]{1,0:T(8,128)(2,1)S(1)}, bf16[256,768]{1,0:T(8,128)(2,1)S(1)}, u32[]{:S(2)}, u32[]{:S(2)}) collective-permute-start(bf16[256,768]{1,0:T(8,128)(2,1)S(1)} %get-tuple-element.79), channel_id=1, source_target_pairs={{0,2},{2,0},{4,6},{6,4},{8,10},{10,8},{12,14},{14,12},{16,18},{18,... | collective-permute-start | bytes 1179656 | tf_op jit(solution)/shard_map/ppermute | solution.py:37
  182.1 11.0 %collective-permute-done.29.got_ref = bf16[256,768]{1,0:T(8,128)(2,1)S(1)} collective-permute-done((bf16[256,768]{1,0:T(8,128)(2,1)S(1)}, bf16[256,768]{1,0:T(8,128)(2,1)S(1)}, u32[]{:S(2)}, u32[]{:S(2)}) %collective-permute-start.29) | collective-permute-done | bytes 393248 | tf_op jit(solution)/shard_map/ppermute | solution.py:37
  (146 shorter events, 43.6 us)
Async XLA Ops:
  2.8 17.6 %collective-permute-start = (bf16[256,768]{1,0:T(8,128)(2,1)}, bf16[256,768]{1,0:T(8,128)(2,1)S(1)}, u32[]{:S(2)}, u32[]{:S(2)}) collective-permute-start(bf16[256,768]{1,0:T(8,128)(2,1)} %get-tuple-element.42), channel_id=1, source_target_pairs={{0,2},{2,0},{4,6},{6,4},{8,10},{10,8},{12,14},{14,12},{16,18},{18,... | collective-permute-start | bytes 1179656 | tf_op jit(solution)/shard_map/ppermute | solution.py:37
  20.6 24.2 %collective-permute-start.1 = (bf16[256,768]{1,0:T(8,128)(2,1)S(1)}, bf16[256,768]{1,0:T(8,128)(2,1)S(1)}, u32[]{:S(2)}, u32[]{:S(2)}) collective-permute-start(bf16[256,768]{1,0:T(8,128)(2,1)S(1)} %get-tuple-element.86.refs_5_), channel_id=1, source_target_pairs={{0,16},{2,18},{4,20},{6,22},{8,24},{10,26},{12,28},{14,30},{16,32}... | collective-permute-start | bytes 1179656 | tf_op jit(solution)/shard_map/ppermute | solution.py:37
  31.5 21.3 %collective-permute-start.2 = (bf16[256,768]{1,0:T(8,128)(2,1)S(1)}, bf16[256,768]{1,0:T(8,128)(2,1)S(1)}, u32[]{:S(2)}, u32[]{:S(2)}) collective-permute-start(bf16[256,768]{1,0:T(8,128)(2,1)S(1)} %get-tuple-element.86.refs_5_), channel_id=1, source_target_pairs={{16,0},{18,2},{20,4},{22,6},{24,8},{26,10},{28,12},{30,14},{32,16}... | collective-permute-start | bytes 1179656 | tf_op jit(solution)/shard_map/ppermute | solution.py:37
  33.5 26.2 %collective-permute-start.9 = (bf16[256,768]{1,0:T(8,128)(2,1)S(1)}, bf16[256,768]{1,0:T(8,128)(2,1)S(1)}, u32[]{:S(2)}, u32[]{:S(2)}) collective-permute-start(bf16[256,768]{1,0:T(8,128)(2,1)S(1)} %get-tuple-element.85.refs_6_), channel_id=1, source_target_pairs={{16,0},{18,2},{20,4},{22,6},{24,8},{26,10},{28,12},{30,14},{32,16}... | collective-permute-start | bytes 1179656 | tf_op jit(solution)/shard_map/ppermute | solution.py:37
  39.4 22.1 %collective-permute-start.4 = (bf16[256,768]{1,0:T(8,128)(2,1)S(1)}, bf16[256,768]{1,0:T(8,128)(2,1)S(1)}, u32[]{:S(2)}, u32[]{:S(2)}) collective-permute-start(bf16[256,768]{1,0:T(8,128)(2,1)S(1)} %get-tuple-element.85.refs_6_), channel_id=1, source_target_pairs={{0,16},{2,18},{4,20},{6,22},{8,24},{10,26},{12,28},{14,30},{16,32}... | collective-permute-start | bytes 1179656 | tf_op jit(solution)/shard_map/ppermute | solution.py:37
  41.4 24.1 %collective-permute-start.7 = (bf16[256,768]{1,0:T(8,128)(2,1)S(1)}, bf16[256,768]{1,0:T(8,128)(2,1)S(1)}, u32[]{:S(2)}, u32[]{:S(2)}) collective-permute-start(bf16[256,768]{1,0:T(8,128)(2,1)S(1)} %get-tuple-element.85.refs_6_), channel_id=1, source_target_pairs={{0,4},{2,6},{4,8},{6,10},{8,12},{10,14},{16,20},{18,22},{20,24},{2... | collective-permute-start | bytes 1179656 | tf_op jit(solution)/shard_map/ppermute | solution.py:37
  44.8 24.1 %collective-permute-start.8 = (bf16[256,768]{1,0:T(8,128)(2,1)S(1)}, bf16[256,768]{1,0:T(8,128)(2,1)}, u32[]{:S(2)}, u32[]{:S(2)}) collective-permute-start(bf16[256,768]{1,0:T(8,128)(2,1)S(1)} %get-tuple-element.86.refs_5_), channel_id=1, source_target_pairs={{4,0},{6,2},{8,4},{10,6},{12,8},{14,10},{20,16},{22,18},{24,20},{2... | collective-permute-start | bytes 1179656 | tf_op jit(solution)/shard_map/ppermute | solution.py:37
  53.7 20.0 %collective-permute-start.3 = (bf16[256,768]{1,0:T(8,128)(2,1)}, bf16[256,768]{1,0:T(8,128)(2,1)S(1)}, u32[]{:S(2)}, u32[]{:S(2)}) collective-permute-start(bf16[256,768]{1,0:T(8,128)(2,1)} %get-tuple-element.47), channel_id=1, source_target_pairs={{0,2},{2,0},{4,6},{6,4},{8,10},{10,8},{12,14},{14,12},{16,18},{18,... | collective-permute-start | bytes 1179656 | tf_op jit(solution)/shard_map/ppermute | solution.py:37
  59.7 14.0 %collective-permute-start.11 = (bf16[256,768]{1,0:T(8,128)(2,1)S(1)}, bf16[256,768]{1,0:T(8,128)(2,1)S(1)}, u32[]{:S(2)}, u32[]{:S(2)}) collective-permute-start(bf16[256,768]{1,0:T(8,128)(2,1)S(1)} %collective-permute-done.2.refs_9_), channel_id=1, source_target_pairs={{4,0},{6,2},{8,4},{10,6},{12,8},{14,10},{20,16},{22,18},{24,20},{2... | collective-permute-start | bytes 1179656 | tf_op jit(solution)/shard_map/ppermute | solution.py:37
  61.6 12.0 %collective-permute-start.10 = (bf16[256,768]{1,0:T(8,128)(2,1)S(1)}, bf16[256,768]{1,0:T(8,128)(2,1)S(1)}, u32[]{:S(2)}, u32[]{:S(2)}) collective-permute-start(bf16[256,768]{1,0:T(8,128)(2,1)S(1)} %collective-permute-done.9.refs_10_), channel_id=1, source_target_pairs={{0,4},{2,6},{4,8},{6,10},{8,12},{10,14},{16,20},{18,22},{20,24},{2... | collective-permute-start | bytes 1179656 | tf_op jit(solution)/shard_map/ppermute | solution.py:37
  65.5 12.2 %collective-permute-start.5 = (bf16[256,768]{1,0:T(8,128)(2,1)S(1)}, bf16[256,768]{1,0:T(8,128)(2,1)S(1)}, u32[]{:S(2)}, u32[]{:S(2)}) collective-permute-start(bf16[256,768]{1,0:T(8,128)(2,1)S(1)} %collective-permute-done.4.refs_2_), channel_id=1, source_target_pairs={{0,4},{2,6},{4,8},{6,10},{8,12},{10,14},{16,20},{18,22},{20,24},{2... | collective-permute-start | bytes 1179656 | tf_op jit(solution)/shard_map/ppermute | solution.py:37
  69.0 9.7 %collective-permute-start.6 = (bf16[256,768]{1,0:T(8,128)(2,1)S(1)}, bf16[256,768]{1,0:T(8,128)(2,1)S(1)}, u32[]{:S(2)}, u32[]{:S(2)}) collective-permute-start(bf16[256,768]{1,0:T(8,128)(2,1)S(1)} %collective-permute-done.1.refs_1_), channel_id=1, source_target_pairs={{4,0},{6,2},{8,4},{10,6},{12,8},{14,10},{20,16},{22,18},{24,20},{2... | collective-permute-start | bytes 1179656 | tf_op jit(solution)/shard_map/ppermute | solution.py:37
  94.8 18.7 %collective-permute-start.12 = (bf16[512,768]{1,0:T(8,128)(2,1)}, bf16[512,768]{1,0:T(8,128)(2,1)S(1)}, u32[]{:S(2)}, u32[]{:S(2)}) collective-permute-start(bf16[512,768]{1,0:T(8,128)(2,1)} %get-tuple-element.51), channel_id=1, source_target_pairs={{0,4},{2,6},{4,8},{6,10},{8,12},{10,14},{16,20},{18,22},{20,24},{2... | collective-permute-start | bytes 2359304 | tf_op jit(solution)/shard_map/ppermute | solution.py:37
  98.4 18.7 %collective-permute-start.13 = (bf16[512,768]{1,0:T(8,128)(2,1)}, bf16[512,768]{1,0:T(8,128)(2,1)S(1)}, u32[]{:S(2)}, u32[]{:S(2)}) collective-permute-start(bf16[512,768]{1,0:T(8,128)(2,1)} %get-tuple-element.52), channel_id=1, source_target_pairs={{4,0},{6,2},{8,4},{10,6},{12,8},{14,10},{20,16},{22,18},{24,20},{2... | collective-permute-start | bytes 2359304 | tf_op jit(solution)/shard_map/ppermute | solution.py:37
  101.9 6.7 %collective-permute-start.14 = (bf16[96,768]{1,0:T(8,128)(2,1)S(1)}, bf16[96,768]{1,0:T(8,128)(2,1)S(1)}, u32[]{:S(2)}, u32[]{:S(2)}) collective-permute-start(bf16[96,768]{1,0:T(8,128)(2,1)S(1)} %get-tuple-element.91), channel_id=1, source_target_pairs={{0,128},{2,130},{4,132},{6,134},{8,136},{10,138},{12,140},{14,142}... | collective-permute-start | bytes 442376 | tf_op jit(solution)/shard_map/ppermute | solution.py:37
  117.2 9.6 %collective-permute-start.17 = (bf16[24,768]{1,0:T(8,128)(2,1)S(1)}, bf16[24,768]{1,0:T(8,128)(2,1)S(1)}, u32[]{:S(2)}, u32[]{:S(2)}) collective-permute-start(bf16[24,768]{1,0:T(8,128)(2,1)S(1)} %get-tuple-element.95), channel_id=1, source_target_pairs={{0,4},{2,6},{4,0},{6,2},{8,12},{10,14},{12,8},{14,10},{16,20},{18,... | collective-permute-start | bytes 110600 | tf_op jit(solution)/shard_map/ppermute | solution.py:37
  118.0 8.8 %collective-permute-start.18 = (bf16[24,768]{1,0:T(8,128)(2,1)S(1)}, bf16[24,768]{1,0:T(8,128)(2,1)S(1)}, u32[]{:S(2)}, u32[]{:S(2)}) collective-permute-start(bf16[24,768]{1,0:T(8,128)(2,1)S(1)} %get-tuple-element.97), channel_id=1, source_target_pairs={{0,8},{2,10},{4,12},{6,14},{8,0},{10,2},{12,4},{14,6},{16,24},{18,... | collective-permute-start | bytes 110600 | tf_op jit(solution)/shard_map/ppermute | solution.py:37
  119.5 7.4 %collective-permute-start.19 = (bf16[24,768]{1,0:T(8,128)(2,1)S(1)}, bf16[24,768]{1,0:T(8,128)(2,1)S(1)}, u32[]{:S(2)}, u32[]{:S(2)}) collective-permute-start(bf16[24,768]{1,0:T(8,128)(2,1)S(1)} %get-tuple-element.96), channel_id=1, source_target_pairs={{0,12},{2,14},{4,8},{6,10},{8,4},{10,6},{12,0},{14,2},{16,28},{18,... | collective-permute-start | bytes 110600 | tf_op jit(solution)/shard_map/ppermute | solution.py:37
  120.8 32.6 %collective-permute-start.26 = (bf16[256,768]{1,0:T(8,128)(2,1)S(1)}, bf16[256,768]{1,0:T(8,128)(2,1)S(1)}, u32[]{:S(2)}, u32[]{:S(2)}) collective-permute-start(bf16[256,768]{1,0:T(8,128)(2,1)S(1)} %copy-done.11), channel_id=1, source_target_pairs={{0,4},{2,6},{4,8},{6,10},{8,12},{10,14},{16,20},{18,22},{20,24},{2... | collective-permute-start | bytes 1179656 | tf_op jit(solution)/shard_map/ppermute | solution.py:37
  123.4 30.0 %collective-permute-start.27 = (bf16[256,768]{1,0:T(8,128)(2,1)S(1)}, bf16[256,768]{1,0:T(8,128)(2,1)S(1)}, u32[]{:S(2)}, u32[]{:S(2)}) collective-permute-start(bf16[256,768]{1,0:T(8,128)(2,1)S(1)} %copy-done.10), channel_id=1, source_target_pairs={{4,0},{6,2},{8,4},{10,6},{12,8},{14,10},{20,16},{22,18},{24,20},{2... | collective-permute-start | bytes 1179656 | tf_op jit(solution)/shard_map/ppermute | solution.py:37
  126.9 5.7 %collective-permute-start.20 = (bf16[24,768]{1,0:T(8,128)(2,1)S(1)}, bf16[24,768]{1,0:T(8,128)(2,1)S(1)}, u32[]{:S(2)}, u32[]{:S(2)}) collective-permute-start(bf16[24,768]{1,0:T(8,128)(2,1)S(1)} %add_convert_fusion.7), channel_id=1, source_target_pairs={{0,16},{2,18},{4,20},{6,22},{8,24},{10,26},{12,28},{14,30},{16,0},... | collective-permute-start | bytes 110600 | tf_op jit(solution)/shard_map/ppermute | solution.py:37
  128.6 5.9 %collective-permute-start.21 = (bf16[24,768]{1,0:T(8,128)(2,1)S(1)}, bf16[24,768]{1,0:T(8,128)(2,1)S(1)}, u32[]{:S(2)}, u32[]{:S(2)}) collective-permute-start(bf16[24,768]{1,0:T(8,128)(2,1)S(1)} %add_convert_fusion.7), channel_id=1, source_target_pairs={{0,32},{2,34},{4,36},{6,38},{8,40},{10,42},{12,44},{14,46},{16,48}... | collective-permute-start | bytes 110600 | tf_op jit(solution)/shard_map/ppermute | solution.py:37
  132.4 5.8 %collective-permute-start.22 = (bf16[24,768]{1,0:T(8,128)(2,1)S(1)}, bf16[24,768]{1,0:T(8,128)(2,1)S(1)}, u32[]{:S(2)}, u32[]{:S(2)}) collective-permute-start(bf16[24,768]{1,0:T(8,128)(2,1)S(1)} %add_convert_fusion.7), channel_id=1, source_target_pairs={{0,48},{2,50},{4,52},{6,54},{8,56},{10,58},{12,60},{14,62},{16,32}... | collective-permute-start | bytes 110600 | tf_op jit(solution)/shard_map/ppermute | solution.py:37
  138.1 9.3 %collective-permute-start.23 = (bf16[24,768]{1,0:T(8,128)(2,1)S(1)}, bf16[24,768]{1,0:T(8,128)(2,1)S(1)}, u32[]{:S(2)}, u32[]{:S(2)}) collective-permute-start(bf16[24,768]{1,0:T(8,128)(2,1)S(1)} %add_convert_fusion.6), channel_id=1, source_target_pairs={{0,66},{2,64},{4,70},{6,68},{8,74},{10,72},{12,78},{14,76},{16,82}... | collective-permute-start | bytes 110600 | tf_op jit(solution)/shard_map/ppermute | solution.py:37
  139.3 8.2 %collective-permute-start.24 = (bf16[24,768]{1,0:T(8,128)(2,1)S(1)}, bf16[24,768]{1,0:T(8,128)(2,1)S(1)}, u32[]{:S(2)}, u32[]{:S(2)}) collective-permute-start(bf16[24,768]{1,0:T(8,128)(2,1)S(1)} %add_convert_fusion.6), channel_id=1, source_target_pairs={{0,64},{2,66},{4,68},{6,70},{8,72},{10,74},{12,76},{14,78},{16,80}... | collective-permute-start | bytes 110600 | tf_op jit(solution)/shard_map/ppermute | solution.py:37
  139.8 11.2 %collective-permute-start.25 = (bf16[24,768]{1,0:T(8,128)(2,1)S(1)}, bf16[24,768]{1,0:T(8,128)(2,1)S(1)}, u32[]{:S(2)}, u32[]{:S(2)}) collective-permute-start(bf16[24,768]{1,0:T(8,128)(2,1)S(1)} %add_convert_fusion.6), channel_id=1, source_target_pairs={{0,2},{2,0},{4,6},{6,4},{8,10},{10,8},{12,14},{14,12},{16,18},{18,... | collective-permute-start | bytes 110600 | tf_op jit(solution)/shard_map/ppermute | solution.py:37
  147.5 25.1 %collective-permute-start.28 = (bf16[256,384]{1,0:T(8,128)(2,1)S(1)}, bf16[256,384]{1,0:T(8,128)(2,1)S(1)}, u32[]{:S(2)}, u32[]{:S(2)}) collective-permute-start(bf16[256,384]{1,0:T(8,128)(2,1)S(1)} %copy-done.22), channel_id=1, source_target_pairs={{0,2},{2,0},{4,6},{6,4},{8,10},{10,8},{12,14},{14,12},{16,18},{18,... | collective-permute-start | bytes 589832 | tf_op jit(solution)/shard_map/ppermute | solution.py:37
  147.5 22.7 %collective-permute-start.15 = (bf16[512,768]{1,0:T(8,128)(2,1)S(1)}, bf16[512,768]{1,0:T(8,128)(2,1)S(1)}, u32[]{:S(2)}, u32[]{:S(2)}) collective-permute-start(bf16[512,768]{1,0:T(8,128)(2,1)S(1)} %add_convert_fusion.2), channel_id=1, source_target_pairs={{16,0},{18,2},{20,4},{22,6},{24,8},{26,10},{28,12},{30,14},{32,16}... | collective-permute-start | bytes 2359304 | tf_op jit(solution)/shard_map/ppermute | solution.py:37
  151.0 21.2 %collective-permute-start.16 = (bf16[512,768]{1,0:T(8,128)(2,1)S(1)}, bf16[512,768]{1,0:T(8,128)(2,1)S(1)}, u32[]{:S(2)}, u32[]{:S(2)}) collective-permute-start(bf16[512,768]{1,0:T(8,128)(2,1)S(1)} %add_convert_fusion.1), channel_id=1, source_target_pairs={{0,16},{2,18},{4,20},{6,22},{8,24},{10,26},{12,28},{14,30},{16,32}... | collective-permute-start | bytes 2359304 | tf_op jit(solution)/shard_map/ppermute | solution.py:37
  153.5 5.9 %collective-permute-start.31 = (bf16[2,24,768]{2,1,0:T(8,128)(2,1)S(1)}, bf16[2,24,768]{2,1,0:T(8,128)(2,1)S(1)}, u32[]{:S(2)}, u32[]{:S(2)}) collective-permute-start(bf16[2,24,768]{2,1,0:T(8,128)(2,1)S(1)} %pad_maximum_fusion.1), channel_id=1, source_target_pairs={{0,8},{2,10},{4,12},{6,14},{8,0},{10,2},{12,4},{14,6},{16,24},{18,... | collective-permute-start | bytes 221192 | tf_op jit(solution)/shard_map/ppermute | solution.py:37
  162.2 15.3 %collective-permute-start.33 = (bf16[4,2,24,768]{3,2,1,0:T(8,128)(2,1)S(1)}, bf16[4,2,24,768]{3,2,1,0:T(8,128)(2,1)S(1)}, u32[]{:S(2)}, u32[]{:S(2)}) collective-permute-start(bf16[4,2,24,768]{3,2,1,0:T(8,128)(2,1)S(1)} %bitcast_dynamic-update-slice_fusion), channel_id=1, source_target_pairs={{0,128},{2,130},{4,132},{6,134},{8,136},{10,138},{12,140},{14,142}... | collective-permute-start | bytes 884744 | tf_op jit(solution)/shard_map/ppermute | solution.py:37
  173.4 19.7 %collective-permute-start.29 = (bf16[256,768]{1,0:T(8,128)(2,1)S(1)}, bf16[256,768]{1,0:T(8,128)(2,1)S(1)}, u32[]{:S(2)}, u32[]{:S(2)}) collective-permute-start(bf16[256,768]{1,0:T(8,128)(2,1)S(1)} %get-tuple-element.79), channel_id=1, source_target_pairs={{0,2},{2,0},{4,6},{6,4},{8,10},{10,8},{12,14},{14,12},{16,18},{18,... | collective-permute-start | bytes 1179656 | tf_op jit(solution)/shard_map/ppermute | solution.py:37
  (27 other events, 324.1 us)
